TPU v7x, 32 devices: a whole 2x2x4 slice. The times are simulated.
32 devices in a mesh: fsdp: 2 (over x), ctx: 4 (over y, core), tp: 4 (over z).
Axes of the slice: x: 2, y: 2, z: 4, core: 2. Of those that a mesh axis runs over, the one named last changes fastest.
Arguments:
- tokens: bfloat16 [2, 1024, 768], P('fsdp', 'ctx'), may hold values from -6 to 6
- mixing_weight: bfloat16 [768, 3, 768], P(('fsdp', 'ctx'), None, 'tp'), may hold values from -0.21875 to 0.21875
- output_weight: bfloat16 [768, 768], P('tp', ('fsdp', 'ctx')), may hold values from -3.5 to 3.5
- first_gain: bfloat16 [768], P(('fsdp', 'ctx')), may hold values from 0.5 to 1.5
- second_gain: bfloat16 [768], P(('fsdp', 'ctx')), may hold values from 0.5 to 1.5
- centroids: bfloat16 [32, 768], P(None, ('fsdp', 'ctx')), may hold values from -0.109375 to 0.109375
- expert_up: bfloat16 [32, 768, 3072], P('fsdp', 'ctx', 'tp'), may hold values from -0.21875 to 0.21875
- expert_down: bfloat16 [32, 3072, 768], P('fsdp', 'tp', 'ctx'), may hold values from -0.3125 to 0.3125
- prefix_length: int32 [2], P('fsdp'), may hold values from 0 to 1024
- assignment: int32 [2, 1024, 1], P('fsdp', 'ctx'), may hold values from 0 to 31, as said below
- validity: int32 [2, 1024], P('fsdp', 'ctx'), may hold values 0 or 1
- teacher: bfloat16 [2, 1024, 768], P('fsdp', 'ctx'), may hold values from -6 to 6
- cotangent: bfloat16 [2, 1024, 768], P('fsdp', 'ctx'), may hold values from -6 to 6
Outputs:
- activations: bfloat16 [2, 1024, 768], P('fsdp', 'ctx')
- tokens_gradient: bfloat16 [2, 1024, 768], P('fsdp', 'ctx')
- mixing_gradient: float32 [768, 3, 768], P(('fsdp', 'ctx'), None, 'tp')
- output_gradient: float32 [768, 768], P('tp', ('fsdp', 'ctx'))
- first_gradient: float32 [768], P(('fsdp', 'ctx'))
- second_gradient: float32 [768], P(('fsdp', 'ctx'))
- centroid_gradient: float32 [32, 768], P(None, ('fsdp', 'ctx'))
- upward_gradient: float32 [32, 768, 3072], P('fsdp', 'ctx', 'tp')
- downward_gradient: float32 [32, 3072, 768], P('fsdp', 'tp', 'ctx')
- balance_loss: float32 [], replicated
- distill_loss: float32 [], replicated
Inputs may be any that keep to these rules, and one draw needn't show every extreme that they name: `assignment`: in each aligned block of 256 tokens (the tokens of one sequence piece, in order of sequence and position) a quarter of the experts are named by exactly 16 tokens, half by exactly 8, and the rest by none; which experts these are differs from block to block.
All inputs are finite; a program needn't handle non-finite values. No bound on the sum of `validity` on one device may be relied on, other than what follows from the above.
Results may differ from a plain program's by a relative error of at most 0.015.
Values may be sent and summed in bfloat16 or wider, within the bound.
A program may use at most 256 MiB of HBM per device.

v0:
```python
from functools import partial
import math

import jax
import jax.numpy as jnp
from jax import lax
from jax.sharding import PartitionSpec as P

HD = 64


EPSILON = 1e-05
TOP_PRECISION = lax.Precision.HIGHEST


def layer_norm(values, gain):
    centred = values - jnp.mean(values, axis=-1, keepdims=True)
    variance = jnp.mean(centred * centred, axis=-1, keepdims=True)
    return centred * lax.rsqrt(variance + EPSILON) * gain


def masked_scores(query_block, key_head, offset, prefix, key_valid):
    raw_scores = jnp.einsum(
        "qd,kd->qk", query_block, key_head, preferred_element_type=jnp.float32
    ) * (1.0 / math.sqrt(HD))
    query_pos = offset + jnp.arange(query_block.shape[0], dtype=jnp.int32)
    key_pos = jnp.arange(key_head.shape[0], dtype=jnp.int32)
    visible = (key_pos[None, :] <= query_pos[:, None]) | (key_pos[None, :] < prefix)
    allowed = visible & ((key_valid[None, :] > 0.5) | (key_pos[None, :] == query_pos[:, None]))
    return jnp.where(allowed, raw_scores, -1e30)


def unit_total(values):
    return lax.psum(values, "tp")


def per_device(
    tokens,
    mixing_weight,
    output_weight,
    first_gain,
    second_gain,
    centroids,
    expert_up,
    expert_down,
    prefix_length,
    assignment,
    validity,
    teacher,
    cotangent,
):
    local_tokens = tokens.shape[1]
    width = tokens.shape[2]
    fsdp_size = lax.axis_size("fsdp")
    ctx_size = lax.axis_size("ctx")
    inputs = tokens[0].astype(jnp.float32)
    mixing_layer, layer_output, gain_one, gain_two, centres = (
        lax.all_gather(mixing_weight, ("fsdp", "ctx"), axis=0, tiled=True),
        lax.all_gather(output_weight, ("fsdp", "ctx"), axis=1, tiled=True),
        lax.all_gather(first_gain, ("fsdp", "ctx"), axis=0, tiled=True),
        lax.all_gather(second_gain, ("fsdp", "ctx"), axis=0, tiled=True),
        lax.all_gather(centroids, ("fsdp", "ctx"), axis=1, tiled=True),
    )
    gain_one_f = gain_one.astype(jnp.float32)
    gain_two_f = gain_two.astype(jnp.float32)
    normalized_input = layer_norm(inputs, gain_one_f).astype(jnp.bfloat16)
    projected_heads = jnp.einsum(
        "td,djk->tjk", normalized_input, mixing_layer, preferred_element_type=jnp.float32
    )
    queries = projected_heads[:, 0].astype(jnp.bfloat16)
    keys_local = projected_heads[:, 1].astype(jnp.bfloat16)
    values_local = projected_heads[:, 2].astype(jnp.bfloat16)
    valid_local = validity[0].astype(jnp.bfloat16)
    keys_all, values_all, key_valid, up_full, down_full = (
        lax.all_gather(keys_local, "ctx", axis=0, tiled=True),
        lax.all_gather(values_local, "ctx", axis=0, tiled=True),
        lax.all_gather(valid_local, "ctx", axis=0, tiled=True),
        lax.all_gather(expert_up, "ctx", axis=1, tiled=True),
        lax.all_gather(expert_down, "ctx", axis=2, tiled=True),
    )
    seq_length = keys_all.shape[0]
    local_heads = queries.shape[1] // HD
    block_rows = min(512, local_tokens)
    block_count = local_tokens // block_rows
    query_heads = queries.reshape(local_tokens, local_heads, HD).transpose(1, 0, 2)
    key_heads = keys_all.reshape(seq_length, local_heads, HD).transpose(1, 0, 2)
    value_heads = values_all.reshape(seq_length, local_heads, HD).transpose(1, 0, 2)
    head_ids = jnp.repeat(jnp.arange(local_heads, dtype=jnp.int32), block_count)
    offsets = lax.axis_index("ctx") * local_tokens + jnp.tile(
        jnp.arange(block_count, dtype=jnp.int32) * block_rows, local_heads
    )
    prefix = prefix_length[0]

    def attend(packet):
        query_block, head_index, offset = packet
        masked = masked_scores(query_block, key_heads[head_index], offset, prefix, key_valid)
        row_max = jnp.max(masked, axis=-1, keepdims=True)
        unscaled = jnp.exp(masked - row_max)
        row_sum = jnp.sum(unscaled, axis=-1, keepdims=True)
        weights = unscaled / row_sum
        blended = jnp.dot(
            weights.astype(jnp.bfloat16),
            value_heads[head_index],
            preferred_element_type=jnp.float32,
        )
        return (blended.astype(jnp.bfloat16), row_max, row_sum)

    context_heads, row_maxes, row_sums = lax.map(attend, (query_heads, head_ids, offsets))
    attended_context = context_heads.transpose(1, 0, 2).reshape(local_tokens, local_heads * HD)
    partial_branch = jnp.dot(attended_context, layer_output, preferred_element_type=jnp.float32)
    branch_output = lax.psum(partial_branch, "tp")
    residual = inputs + branch_output
    mixed_in = layer_norm(residual, gain_two_f).astype(jnp.bfloat16)
    mixed_float = mixed_in.astype(jnp.float32)
    chosen = assignment[0, :, 0]
    expert_count = centres.shape[0]
    local_experts = expert_up.shape[0]
    capacity = 2 * local_tokens // expert_count
    onehot = chosen[:, None] == jnp.arange(expert_count, dtype=jnp.int32)[None, :]
    hot_float = onehot.astype(jnp.float32)
    hot_int = onehot.astype(jnp.int32)
    earlier = jnp.cumsum(hot_int, axis=0) - hot_int
    rank = jnp.sum(earlier * hot_int, axis=1)
    slots = chosen * capacity + rank
    centre_rows = jnp.dot(onehot.astype(jnp.bfloat16), centres, preferred_element_type=jnp.float32)
    logits = jnp.sum(mixed_float * centre_rows, axis=-1)
    gates = jax.nn.sigmoid(logits)
    send = (
        jnp.zeros((expert_count * capacity, width), jnp.bfloat16)
        .at[slots]
        .set(mixed_in)
        .reshape(fsdp_size, local_experts * capacity, width)
    )
    received = lax.all_to_all(send, "fsdp", split_axis=0, concat_axis=0, tiled=True).reshape(
        fsdp_size, local_experts, capacity, width
    )
    hidden_pre = jnp.einsum("sgcd,gdf->sgcf", received, up_full, preferred_element_type=jnp.float32)
    activated = jax.nn.gelu(hidden_pre, approximate=False).astype(jnp.bfloat16)
    partial_rows = jnp.einsum(
        "sgcf,gfd->sgcd", activated, down_full, preferred_element_type=jnp.float32
    )
    came_back = lax.all_to_all(
        partial_rows.reshape(fsdp_size, local_experts * capacity, width),
        "fsdp",
        split_axis=0,
        concat_axis=0,
        tiled=True,
    ).reshape(expert_count * capacity, width)
    returned = unit_total(came_back[slots]).astype(jnp.bfloat16)
    returned_f = returned.astype(jnp.float32)
    mixed = residual + gates[:, None] * returned_f
    valid_float = validity[0].astype(jnp.float32)
    difference = mixed - teacher[0].astype(jnp.float32)
    counts, gate_total, valid_count, square_sum = lax.psum(
        (
            jnp.sum(hot_float, axis=0),
            jnp.sum(jnp.where(onehot, gates[:, None], 0.0), axis=0),
            jnp.sum(valid_float),
            jnp.sum(valid_float[:, None] * difference * difference),
        ),
        ("fsdp", "ctx"),
    )
    all_tokens = float(local_tokens * ctx_size * fsdp_size)
    share = counts / all_tokens - 1.0 / expert_count
    balance = expert_count * expert_count * jnp.sum(share * gate_total / all_tokens)
    distill = square_sum / (valid_count * width)
    grad_mixed = cotangent[0].astype(jnp.float32) + 2.0 * valid_float[:, None] * difference / (
        valid_count * width
    )
    grad_gate = jnp.sum(grad_mixed * returned_f, axis=-1)
    grad_logit = grad_gate * gates * (1.0 - gates)
    grad_send = (
        jnp.zeros((expert_count * capacity, width), jnp.bfloat16)
        .at[slots]
        .set((gates[:, None] * grad_mixed).astype(jnp.bfloat16))
        .reshape(fsdp_size, local_experts * capacity, width)
    )
    grad_received = lax.all_to_all(
        grad_send, "fsdp", split_axis=0, concat_axis=0, tiled=True
    ).reshape(fsdp_size, local_experts, capacity, width)
    grad_act = jnp.einsum(
        "sgcd,gfd->sgcf", grad_received, down_full, preferred_element_type=jnp.float32
    )
    gelu_pull = jax.vjp(partial(jax.nn.gelu, approximate=False), hidden_pre)[1]
    grad_pre = gelu_pull(grad_act)[0].astype(jnp.bfloat16)
    down_partial = jnp.einsum(
        "sgcf,sgcd->gfd", activated, grad_received, preferred_element_type=jnp.float32
    )
    up_partial = jnp.einsum(
        "sgcd,sgcf->gdf", received, grad_pre, preferred_element_type=jnp.float32
    )
    slot_partial = jnp.einsum(
        "sgcf,gdf->sgcd", grad_pre, up_full, preferred_element_type=jnp.float32
    )
    slot_gradient = (
        lax.psum(slot_partial, "tp")
        .astype(jnp.bfloat16)
        .reshape(fsdp_size, local_experts * capacity, width)
    )
    grad_back = (
        lax.all_to_all(slot_gradient, "fsdp", split_axis=0, concat_axis=0, tiled=True)
        .reshape(expert_count * capacity, width)[slots]
        .astype(jnp.float32)
    )
    grad_mixed_in = grad_back + grad_logit[:, None] * centre_rows
    centre_gradient = jnp.dot(
        hot_float.T,
        grad_logit[:, None] * mixed_float,
        precision=TOP_PRECISION,
        preferred_element_type=jnp.float32,
    )
    second_pull = jax.vjp(layer_norm, residual, gain_two_f)[1]
    grad_norm_in, gain_two_grad = second_pull(grad_mixed_in)
    grad_residual = grad_mixed + grad_norm_in
    grad_branch = grad_residual.astype(jnp.bfloat16)
    output_gradient = jnp.einsum(
        "tk,td->kd", attended_context, grad_branch, preferred_element_type=jnp.float32
    )
    grad_context = jnp.einsum(
        "td,kd->tk", grad_branch, layer_output, preferred_element_type=jnp.float32
    ).astype(jnp.bfloat16)
    grad_heads = grad_context.reshape(local_tokens, local_heads, HD).transpose(1, 0, 2)
    scale = 1.0 / math.sqrt(HD)

    def attend_back(carry, packet):
        key_acc, value_acc = carry
        query_block, head_index, offset, row_max, row_sum, grad_block = packet
        masked = masked_scores(query_block, key_heads[head_index], offset, prefix, key_valid)
        weights = jnp.exp(masked - row_max) / row_sum
        grad_weights = jnp.einsum(
            "qd,kd->qk", grad_block, value_heads[head_index], preferred_element_type=jnp.float32
        )
        grad_scores = (
            weights * (grad_weights - jnp.sum(weights * grad_weights, axis=-1, keepdims=True))
        ).astype(jnp.bfloat16)
        grad_query = (
            jnp.einsum(
                "qk,kd->qd", grad_scores, key_heads[head_index], preferred_element_type=jnp.float32
            )
            * scale
        ).astype(jnp.bfloat16)
        key_acc = key_acc.at[head_index].add(
            jnp.einsum("qk,qd->kd", grad_scores, query_block, preferred_element_type=jnp.float32)
            * scale
        )
        value_acc = value_acc.at[head_index].add(
            jnp.einsum(
                "qk,qd->kd",
                weights.astype(jnp.bfloat16),
                grad_block,
                preferred_element_type=jnp.float32,
            )
        )
        return ((key_acc, value_acc), grad_query)

    zero_heads = jnp.zeros((local_heads, seq_length, HD), jnp.float32)
    sums_back, query_grads = lax.scan(
        attend_back,
        (zero_heads, zero_heads),
        (query_heads, head_ids, offsets, row_maxes, row_sums, grad_heads),
    )
    query_gradient = query_grads.transpose(1, 0, 2).reshape(local_tokens, local_heads * HD)
    key_full = sums_back[0].transpose(1, 0, 2).reshape(seq_length, local_heads * HD)
    value_full = sums_back[1].transpose(1, 0, 2).reshape(seq_length, local_heads * HD)
    key_part, value_part, up_gradient, down_gradient = (
        lax.psum_scatter(key_full, "ctx", scatter_dimension=0, tiled=True),
        lax.psum_scatter(value_full, "ctx", scatter_dimension=0, tiled=True),
        lax.psum_scatter(up_partial, "ctx", scatter_dimension=1, tiled=True),
        lax.psum_scatter(down_partial, "ctx", scatter_dimension=2, tiled=True),
    )
    grad_mixing = jnp.stack(
        [query_gradient, key_part.astype(jnp.bfloat16), value_part.astype(jnp.bfloat16)], axis=1
    )
    mixing_gradient = jnp.einsum(
        "td,tjk->djk", normalized_input, grad_mixing, preferred_element_type=jnp.float32
    )
    normed_partial = jnp.einsum(
        "tjk,djk->td", grad_mixing, mixing_layer, preferred_element_type=jnp.float32
    )
    grad_normed = lax.psum(normed_partial, "tp")
    first_pull = jax.vjp(layer_norm, inputs, gain_one_f)[1]
    grad_inputs, gain_one_grad = first_pull(grad_normed)
    input_gradient = (grad_residual + grad_inputs).astype(jnp.bfloat16)
    mixing_part, output_part, first_part, second_part, centre_part = (
        lax.psum_scatter(mixing_gradient, ("fsdp", "ctx"), scatter_dimension=0, tiled=True),
        lax.psum_scatter(output_gradient, ("fsdp", "ctx"), scatter_dimension=1, tiled=True),
        lax.psum_scatter(gain_one_grad, ("fsdp", "ctx"), scatter_dimension=0, tiled=True),
        lax.psum_scatter(gain_two_grad, ("fsdp", "ctx"), scatter_dimension=0, tiled=True),
        lax.psum_scatter(centre_gradient, ("fsdp", "ctx"), scatter_dimension=1, tiled=True),
    )
    return (
        mixed.astype(jnp.bfloat16)[None],
        input_gradient[None],
        mixing_part,
        output_part,
        first_part,
        second_part,
        centre_part,
        up_gradient,
        down_gradient,
        balance,
        distill,
    )


def solution(mesh):
    in_specs = (
        P("fsdp", "ctx", None),
        P(("fsdp", "ctx"), None, "tp"),
        P("tp", ("fsdp", "ctx")),
        P(("fsdp", "ctx")),
        P(("fsdp", "ctx")),
        P(None, ("fsdp", "ctx")),
        P("fsdp", "ctx", "tp"),
        P("fsdp", "tp", "ctx"),
        P("fsdp"),
        P("fsdp", "ctx", None),
        P("fsdp", "ctx"),
        P("fsdp", "ctx", None),
        P("fsdp", "ctx", None),
    )
    out_specs = (
        P("fsdp", "ctx", None),
        P("fsdp", "ctx", None),
        P(("fsdp", "ctx"), None, "tp"),
        P("tp", ("fsdp", "ctx")),
        P(("fsdp", "ctx")),
        P(("fsdp", "ctx")),
        P(None, ("fsdp", "ctx")),
        P("fsdp", "ctx", "tp"),
        P("fsdp", "tp", "ctx"),
        P(),
        P(),
    )
    return jax.shard_map(
        per_device, mesh=mesh, in_specs=in_specs, out_specs=out_specs, check_vma=False
    )
```

profile of v0, /device:TPU:0, one launch (start us, length us, event | category | flops | bytes accessed | tf_op | source)
XLA Modules:
  0.0 1303.2 jit_solution(1168936021362597713)
XLA Ops:
  10.5 1.3 fusion.148
  14.2 15.1 %all-reduce.5 = (bf16[768]{0:T(1024)(128)(2,1)S(1)}, bf16[768]{0:T(1024)(128)(2,1)S(1)}) all-reduce(bf16[768]{0:T(1024)(128)(2,1)S(1)} %dynamic-update-slice.6, bf16[768]{0:T(1024)(128)(2,1)S(1)} %dynamic-update-slice.7), channel_id=1, replica_groups=mesh['fsdp'=2,'ctx'=4,'tp'=4] {'fsdp','ctx'}, use_global_device_ids=true, to_apply=%add | all-reduce | flops 1536 | bytes 6144
  29.3 1.3 fusion.147
  30.6 5.1 all-gather
  37.6 8.6 all_gather.35
  46.3 13.4 %all_gather.32 = bf16[768,3,192]{2,1,0:T(4,128)(2,1)S(1)} all-gather(bf16[96,3,192]{2,1,0:T(4,128)(2,1)S(1)} %copy.46), channel_id=1, replica_groups=mesh['fsdp'=2,'ctx'=4,'tp'=4] {'fsdp','ctx'}, dimensions={0}, use_global_device_ids=true | all-gather | bytes 995328 | tf_op jit(solution)/shard_map/all_gather | solution.py:58
  61.6 6.6 all-gather.2
  68.6 6.6 all-gather.1
  75.6 20.7 %while.30 = (s32[]{:T(128)}, bf16[3,256,64]{1,2,0:T(8,128)(2,1)S(1)}, f32[3,256,1]{1,2,0:T(1,128)}, f32[3,256,1]{1,2,0:T(1,128)}, s32[3]{0:T(128)S(1)}, /*index=...) while((s32[]{:T(128)}, ...), condition=%wide.region_5.6_spmd, body=%wide.region_2.5_spmd.sunk | while | flops 70536960 | bytes 3785959 | solution.py:108
  96.3 1.5 fusion.149
  100.0 8.3 all-gather.3
  108.5 33.4 %all-reduce.11.cloned.1.call-done = f32[256,768]{1,0:T(8,128)} async-done(((f32[256,768]{1,0:T(8,128)}), f32[256,768]{1,0:T(8,128)}) %all-reduce.11.cloned.1.call-update) | async-done | bytes 786448 | tf_op jit(solution)/shard_map/psum | solution.py:111
  143.5 1.8 fusion.101
  145.3 1.9 scatter_custom_fusion
  147.2 13.4 %all_to_all.20 = bf16[2,256,768]{2,1,0:T(8,128)(2,1)S(1)} all-to-all(bf16[2,256,768]{2,1,0:T(8,128)(2,1)S(1)} %bitcast.389), channel_id=1, replica_groups=mesh['fsdp'=2,'ctx'=4,'tp'=4] {'fsdp'}, dimensions={0} | all-to-all | bytes 1572864 | tf_op jit(solution)/shard_map/all_to_all | solution.py:134
  160.6 59.3 %all-gather.7.cloned.1.call-done = bf16[16,768,768]{2,1,0:T(8,128)(2,1)} async-done(((bf16[16,192,768]{2,1,0:T(8,128)(2,1)}), bf16[16,768,768]{2,1,0:T(8,128)(2,1)}) %all-gather.7.cloned.1.call-update) | async-done | bytes 18874384 | tf_op jit(solution)/shard_map/all_gather | solution.py:78
  220.0 8.1 fusion.55
  228.1 113.2 %all-gather.9.cloned.1.call-done = bf16[16,768,768]{1,2,0:T(8,128)(2,1)} async-done(((bf16[16,768,192]{1,2,0:T(8,128)(2,1)}), bf16[16,768,768]{1,2,0:T(8,128)(2,1)}) %all-gather.9.cloned.1.call-update) | async-done | bytes 18874384 | tf_op jit(solution)/shard_map/all_gather | solution.py:79
  341.2 9.3 fusion.83
  351.8 3.7 all-to-all-start.1
  356.7 26.3 %psum.58 = f32[]{:T(128)} all-reduce(f32[]{:T(128)} %convert_reduce_fusion.2), channel_id=1, replica_groups=mesh['fsdp'=2,'ctx'=4,'tp'=4] {'fsdp','ctx'}, use_global_device_ids=true, to_apply=%region_16.17 | all-reduce | flops 1 | bytes 8 | tf_op jit(solution)/shard_map/psum | solution.py:154
  387.4 2.1 gather_fusion
  389.5 35.4 %all-reduce.14 = bf16[256,768]{1,0:T(8,128)(2,1)S(1)} all-reduce(f32[256,768]{1,0:T(8,128)} %gather_fusion), channel_id=1, replica_groups=mesh['fsdp'=2,'ctx'=4,'tp'=4] {'tp'}, use_global_device_ids=true, to_apply=%region_14.15 | all-reduce | flops 196608 | bytes 1179648 | tf_op jit(solution)/shard_map/psum | solution.py:34
  425.0 2.1 fusion.104
  427.1 1.7 fusion.103
  428.8 2.1 scatter_custom_fusion.1
  430.9 10.6 all_to_all.21
  442.3 9.6 fusion.67
  451.9 12.2 fusion.86
  464.1 51.8 %all-reduce.15 = bf16[2,16,16,768]{3,2,0,1:T(8,128)(2,1)} all-reduce(f32[2,16,16,768]{3,2,0,1:T(8,128)S(1)} %fusion.86), channel_id=1, replica_groups=mesh['fsdp'=2,'ctx'=4,'tp'=4] {'tp'}, use_global_device_ids=true, to_apply=%region_18.19 | all-reduce | flops 393216 | bytes 2359296 | tf_op jit(solution)/shard_map/psum | solution.py:196
  515.9 2.1 copy.57
  518.0 3.5 all-to-all-start.3
  522.2 7.3 all-to-all-done.3
  529.5 2.2 gather_fusion.1
  531.8 2.0 multiply_reduce_fusion.1
  537.8 47.8 %while.31 = (s32[]{:T(128)}, f32[3,1024,64]{1,2,0:T(8,128)S(1)}, f32[3,1024,64]{1,2,0:T(8,128)S(1)}, bf16[3,256,64]{1,2,0:T(8,128)(2,1)}, s32[3]{0:T(128)}, /*in...) while((s32[]{:T(128)}, f32[3,1024,64]{1,2,0:T(8,128)S(1)}, ...), condition=%wide.region_25.26_spmd, body=%wide.region_22.25_spmd.sunk | while | flops 172068880 | bytes 10014584 | solution.py:257
  546.3 1.8 multiply_reduce_fusion.6
  548.3 1.8 fusion.191
  550.1 1.9 fusion.192
  552.0 1.8 fusion.190
  560.9 1.3 fusion.189
  562.2 1.8 multiply_reduce_fusion.6
  564.2 1.8 fusion.191
  566.0 1.9 fusion.192
  567.9 1.8 fusion.190
  578.1 1.8 multiply_reduce_fusion.6
  580.2 1.8 fusion.191
  582.0 1.9 fusion.192
  583.8 1.8 fusion.190
  587.4 2.6 convolution_bitcast_fusion.5
  591.4 24.4 %reduce-scatter.12.cloned.1.call-done = f32[256,192]{0,1:T(8,128)} async-done(((f32[1024,192]{0,1:T(8,128)}), f32[256,192]{0,1:T(8,128)}) %reduce-scatter.12.cloned.1.call-update) | async-done | bytes 196624 | tf_op jit(solution)/shard_map/reduce_scatter | solution.py:266
  616.7 25.6 %reduce-scatter.14.cloned.1.call-done = f32[256,192]{0,1:T(8,128)} async-done(((f32[1024,192]{0,1:T(8,128)}), f32[256,192]{0,1:T(8,128)}) %reduce-scatter.14.cloned.1.call-update) | async-done | bytes 196624 | tf_op jit(solution)/shard_map/reduce_scatter | solution.py:267
  643.3 2.6 convolution_bitcast_fusion.3
  645.9 2.1 fusion.115
  649.4 15.5 %convolution_bitcast_fusion.1 = f32[16,768,768]{1,2,0:T(8,128)} fusion(bf16[2,16,16,768]{3,2,1,0:T(8,128)(2,1)} %bitcast.397, f32[16,2,16,768]{3,2,1,0:T(8,128)S(1)} %copy-done.15), kind=kOutput, calls=%fused_computation.90 | convolution fusion | flops 629538816 | bytes 40108032 | tf_op jit(solution)/shard_map/sgcf,sgcd->gfd/dot_general | solution.py:186
  666.2 15.0 %convolution_bitcast_fusion.2 = f32[16,768,768]{2,1,0:T(8,128)} fusion(bf16[2,16,16,768]{3,2,1,0:T(8,128)(2,1)S(1)} %bitcast.383, bf16[2,16,16,768]{3,2,0,1:T(8,128)(2,1)S(1)} %copy-done.3), kind=kOutput, calls=%fused_computation.91 | convolution fusion | flops 603979776 | bytes 39321600 | tf_op jit(solution)/shard_map/sgcd,sgcf->gdf/dot_general | solution.py:189
  682.0 1.5 copy.71
  683.4 34.5 %reduce-scatter.22.cloned.1.call-done = f32[96,192]{1,0:T(8,128)} async-done(((f32[768,192]{1,0:T(8,128)}), f32[96,192]{1,0:T(8,128)}) %reduce-scatter.22.cloned.1.call-update) | async-done | bytes 73744
  718.0 1.6 copy.69
  719.6 1.5 fusion.100
  721.6 13.3 %all-reduce.4 = (f32[768]{0:T(1024)S(1)}, f32[768]{0:T(1024)S(1)}, f32[32]{0:T(128)S(1)}, f32[32]{0:T(128)S(1)}, f32[]{:T(128)}) all-reduce(f32[768]{0:T(1024)S(1)} %get-tuple-element.176, f32[768]{0:T(1024)S(1)} %copy-done.36, f32[32]{0:T(128)S(1)} %get-tuple-element.179, ...), channel_id=9, replica_groups=mesh['fsdp'=2,'ctx'=4,'tp'=4] {'fsdp','ctx'}, use_global_device_ids=true, to_apply=%region_34.35.clone | all-reduce | flops 1601 | bytes 12808
  739.1 25.0 %reduce-scatter.16.cloned.1.call-done = f32[96,3,192]{2,0,1:T(8,128)} async-done(((f32[768,3,192]{2,0,1:T(8,128)}), f32[96,3,192]{2,0,1:T(8,128)}) %reduce-scatter.16.cloned.1.call-update) | async-done | bytes 221200 | tf_op jit(solution)/shard_map/reduce_scatter | solution.py:285
  764.1 264.7 %reduce-scatter.20.cloned.1.call-done = f32[16,768,192]{1,2,0:T(8,128)} async-done(((f32[16,768,768]{1,2,0:T(8,128)}), f32[16,768,192]{1,2,0:T(8,128)}) %reduce-scatter.20.cloned.1.call-update) | async-done | bytes 9437200 | tf_op jit(solution)/shard_map/reduce_scatter | solution.py:269
  1028.8 264.5 %reduce-scatter.18.cloned.1.call-done = f32[16,192,768]{2,1,0:T(8,128)} async-done(((f32[16,768,768]{2,1,0:T(8,128)}), f32[16,192,768]{2,1,0:T(8,128)}) %reduce-scatter.18.cloned.1.call-update) | async-done | bytes 9437200 | tf_op jit(solution)/shard_map/reduce_scatter | solution.py:268
  (242 shorter events, 68.6 us)
Async XLA Ops:
  8.0 133.9 %all-reduce.11.cloned.1.call-start = ((), (), s32[]{:S(2)}) async-start(), calls=%async_computation.11 | async-start | bytes 1572864 | tf_op jit(solution)/shard_map/psum | solution.py:111
  10.5 25.2 %copy-start.39 = (f32[256]{0:T(256)}, f32[256]{0:T(256)S(1)}, u32[]{:S(2)}) copy-start(f32[256]{0:T(256)S(1)} %fusion.99) | copy-start | bytes 3076
  10.5 50.0 %copy-start.33 = (f32[256]{0:T(256)}, f32[256]{0:T(256)S(1)}, u32[]{:S(2)}) copy-start(f32[256]{0:T(256)S(1)} %fusion.131) | copy-start | bytes 3076
  46.3 50.1 %copy-start.10 = (bf16[192,768]{0,1:T(8,128)(2,1)}, bf16[192,768]{0,1:T(8,128)(2,1)S(1)}, u32[]{:S(2)}) copy-start(bf16[192,768]{0,1:T(8,128)(2,1)S(1)} %all_gather.35) | copy-start | bytes 884740
  59.7 1.0 copy-start
  60.5 0.9 copy-start.21
  96.3 2.1 copy-start.8
  96.3 2.1 copy-start.9
  96.3 2.1 copy-start.18
  96.3 2.1 copy-start.19
  96.3 2.1 copy-start.48
  97.8 122.2 %all-gather.7.cloned.1.call-start = ((), (), s32[]{:S(2)}) async-start(), calls=%async_computation.12 | async-start | bytes 23592960 | tf_op jit(solution)/shard_map/all_gather | solution.py:78
  98.5 0.7 copy-start.25
  98.5 1.5 copy-start.44
  98.5 242.8 %all-gather.9.cloned.1.call-start = ((), (), s32[]{:S(2)}) async-start(), calls=%async_computation.13 | async-start | bytes 23592960 | tf_op jit(solution)/shard_map/all_gather | solution.py:79
  108.5 36.8 %copy-start.47 = (s32[256,1]{0,1:T(1,128)}, s32[256,1]{0,1:T(1,128)S(1)}, u32[]{:S(2)}) copy-start(s32[256,1]{0,1:T(1,128)S(1)} %compare_select_fusion) | copy-start | bytes 3076
  143.2 4.0 copy-start.27
  143.4 3.8 copy-start.41
  143.5 3.7 copy-start.31
  145.3 1.9 copy-start.17
  228.0 122.5 %copy-start.13 = (f32[16,2,16,768]{3,2,1,0:T(8,128)}, f32[16,2,16,768]{3,2,1,0:T(8,128)S(1)}, u32[]{:S(2)}) copy-start(f32[16,2,16,768]{3,2,1,0:T(8,128)S(1)} %fusion.55) | copy-start | bytes 4718596
  351.8 35.6 %all-to-all-start.1 = ((f32[2,256,768]{2,1,0:T(8,128)}), f32[2,256,768]{2,1,0:T(8,128)S(1)}, u32[]{:S(2)}, u32[]{:S(2)}) async-start(f32[2,256,768]{2,1,0:T(8,128)} %bitcast.384), calls=%async_computation.1 | async-start | bytes 3145728 | tf_op jit(solution)/shard_map/all_to_all | solution.py:142
  389.5 37.6 %copy-start.16 = (bf16[1,256,768]{2,1,0:T(8,128)(2,1)S(1)}, bf16[1,256,768]{2,1,0:T(8,128)(2,1)}, u32[]{:S(2)}) copy-start(bf16[1,256,768]{2,1,0:T(8,128)(2,1)} %param.32) | copy-start | bytes 1179652
  424.9 2.2 copy-start.23
  425.0 2.1 copy-start.46
  428.8 12.7 copy-start.6
  430.9 11.4 copy-start.14
  441.5 0.9 copy-start.22
  515.9 5.7 copy-start.43
  515.9 5.7 copy-start.45
  518.0 11.5 all-to-all-start.3
  521.6 94.2 %reduce-scatter.12.cloned.1.call-start = ((), (), s32[]{:S(2)}) async-start(), calls=%async_computation.14 | async-start | bytes 983040 | tf_op jit(solution)/shard_map/reduce_scatter | solution.py:266
  529.5 2.2 copy-start.5
  531.7 2.1 copy-start.42
  531.7 2.1 copy-start.12
  531.7 2.1 copy-start.28
  531.7 2.1 copy-start.29
  531.7 2.1 copy-start.32
  533.8 1.1 copy-start.7
  534.3 1.1 copy-start.11
  535.4 2.5 copy-start.37
  548.3 5.5 copy-start.38
  564.2 5.5 copy-start.38
  580.2 5.5 copy-start.38
  585.6 0.9 copy-start.1
  585.6 1.1 copy-start.2
  585.7 1.7 copy-start.26
  585.7 1.7 copy-start.30
  586.5 3.5 copy-start.20
  586.6 55.7 %reduce-scatter.14.cloned.1.call-start = ((), (), s32[]{:S(2)}) async-start(), calls=%async_computation.15 | async-start | bytes 983040 | tf_op jit(solution)/shard_map/reduce_scatter | solution.py:267
  587.3 94.7 %reduce-scatter.24.cloned.1.call-start = ((), (), s32[]{:S(2)}) async-start(), calls=%async_computation.21 | async-start | bytes 442368
  590.0 53.2 %copy-start.24 = (bf16[3,256,64]{1,2,0:T(8,128)(2,1)S(1)}, bf16[3,256,64]{1,2,0:T(8,128)(2,1)}, u32[]{:S(2)}) copy-start(bf16[3,256,64]{1,2,0:T(8,128)(2,1)} %get-tuple-element.588) | copy-start | bytes 294916
  590.0 128.0 %reduce-scatter.22.cloned.1.call-start = ((), (), s32[]{:S(2)}) async-start(), calls=%async_computation.20 | async-start | bytes 884736
  591.3 128.3 %all-reduce.13.cloned.1.call-start = ((), (), s32[]{:S(2)}) async-start(), calls=%async_computation.16 | async-start | bytes 1572864 | tf_op jit(solution)/shard_map/psum | solution.py:280
  643.2 2.7 copy-start.34
  645.9 118.2 %reduce-scatter.16.cloned.1.call-start = ((), (), s32[]{:S(2)}) async-start(), calls=%async_computation.17 | async-start | bytes 2654208 | tf_op jit(solution)/shard_map/reduce_scatter | solution.py:285
  648.0 1.4 copy-start.15
  648.1 380.8 %reduce-scatter.20.cloned.1.call-start = ((), (), s32[]{:S(2)}) async-start(), calls=%async_computation.19 | async-start | bytes 47185920 | tf_op jit(solution)/shard_map/reduce_scatter | solution.py:269
  665.0 1.2 copy-start.3
  665.0 628.3 %reduce-scatter.18.cloned.1.call-start = ((), (), s32[]{:S(2)}) async-start(), calls=%async_computation.18 | async-start | bytes 47185920 | tf_op jit(solution)/shard_map/reduce_scatter | solution.py:268
  681.1 0.7 copy-start.35
  681.1 40.0 %copy-start.40 = (f32[256]{0:T(256)S(1)}, f32[256]{0:T(256)}, u32[]{:S(2)}) copy-start(f32[256]{0:T(256)} %copy-done.39) | copy-start | bytes 3076
  681.2 40.4 %copy-start.36 = (f32[768]{0:T(1024)S(1)}, f32[768]{0:T(1024)}, u32[]{:S(2)}) copy-start(f32[768]{0:T(1024)} %get-tuple-element.174) | copy-start | bytes 9220
  719.6 1.5 copy-start.4
Sparse Core Ops, SparseCore 0:
  97.9 43.9 all-reduce.10
  646.0 43.6 all-reduce.12
Sparse Core Ops, SparseCore 1:
  99.9 120.1 all-gather.6
  221.4 119.8 all-gather.8
  586.6 29.1 reduce-scatter.11
  619.1 23.2 reduce-scatter.13
  646.0 33.8 reduce-scatter.23
  683.0 34.9 reduce-scatter.21
  721.8 42.3 reduce-scatter.15
  767.3 261.4 reduce-scatter.19
  1031.9 261.4 reduce-scatter.17
where the time goes:
time: 1310 us; the launch traced here: 1300 us
  waiting for transfers between devices  854 us (65%)
  blocking collectives  215 us (16%)
  matrix products  111 us (8%)
  local copies, waits for them, and re-layouts  44.6 us (3%)
  other arithmetic  37.2 us (3%)
  between operations  22.1 us (2%)
    reduce_scatter x1, waiting for transfers between devices, per_device(): lax.psum_scatter(down_partial, 'ctx', scatter_dimension=2, tiled=True)  265 us
    reduce_scatter x1, waiting for transfers between devices, per_device(): lax.psum_scatter(up_partial, 'ctx', scatter_dimension=1, tiled=True)  264 us
    all_gather x1, waiting for transfers between devices, per_device(): lax.all_gather(expert_down, 'ctx', axis=2, tiled=True)  113 us
    all_gather x1, waiting for transfers between devices, per_device(): lax.all_gather(expert_up, 'ctx', axis=1, tiled=True)  59.3 us
    psum x1, blocking collectives, per_device(): lax.psum(slot_partial, 'tp').astype(jnp.bfloat16)  51.8 us
    unnamed x13, waiting for transfers between devices  36.3 us
    psum x1, blocking collectives, unit_total(): return lax.psum(values, 'tp')  35.4 us
    psum x1, waiting for transfers between devices, per_device(): branch_output = lax.psum(partial_branch, 'tp')  33.4 us
  transfers between devices with their start and end apart: 13, of which 10 were waited for; matrix products, arithmetic and copies ran while one was open for 5% of the time, Pallas kernels for 0%

commit v1 on v0

v1 whole, which is shorter than its diff:
```python
from functools import partial
import math

import jax
import jax.numpy as jnp
from jax import lax
from jax.experimental import pallas as pl
from jax.experimental.pallas import tpu as pltpu
from jax.sharding import PartitionSpec as P

HD = 64
EPSILON = 1e-05
BF = jnp.bfloat16
F32 = jnp.float32
MESH = pl.DeviceIdType.MESH
TOP = lax.Precision.HIGHEST
VMEM = pltpu.VMEM
ANY = pl.ANY
COLS = 896
OUT_AT = 640
CEN_AT = 832


def _dot(a, b, ca, cb, precision=None):
    return lax.dot_general(
        a, b, (((ca,), (cb,)), ((), ())), preferred_element_type=F32, precision=precision
    )


def nn(a, b):
    return _dot(a, b, 1, 0)


def nt(a, b):
    return _dot(a, b, 1, 1)


def tn(a, b):
    return _dot(a, b, 0, 0)


def vspec():
    return pl.BlockSpec(memory_space=VMEM)


def sds(shape, dtype):
    return jax.ShapeDtypeStruct(shape, dtype)


def params(cid=None, mib=56):
    if cid is None:
        return pltpu.CompilerParams(vmem_limit_bytes=mib * 2**20)
    return pltpu.CompilerParams(
        vmem_limit_bytes=mib * 2**20, collective_id=cid, has_side_effects=True
    )


def iota(shape, dim):
    return lax.broadcasted_iota(jnp.int32, shape, dim)


def to_col(row):
    n = row.shape[1]
    return jnp.sum(jnp.where(iota((n, n), 0) == iota((n, n), 1), row, 0.0), axis=1, keepdims=True)


def to_row(col):
    n = col.shape[0]
    return jnp.sum(jnp.where(iota((n, n), 0) == iota((n, n), 1), col, 0.0), axis=0, keepdims=True)


def norm_parts(x):
    c = x - jnp.mean(x, axis=-1, keepdims=True)
    inv = lax.rsqrt(jnp.mean(c * c, axis=-1, keepdims=True) + EPSILON)
    return c * inv, inv


def norm_back(grad, xhat, inv, gain):
    gx = grad * gain
    return inv * (
        gx
        - jnp.mean(gx, axis=-1, keepdims=True)
        - xhat * jnp.mean(gx * xhat, axis=-1, keepdims=True)
    )


def route(chosen, experts, cap):
    n = chosen.shape[0]
    hot = (chosen == iota((n, experts), 1)).astype(F32)
    lower = (iota((n, n), 1) < iota((n, n), 0)).astype(BF)
    earlier = nn(lower, hot.astype(BF))
    rank = jnp.sum(earlier * hot, axis=1, keepdims=True)
    return hot, chosen.astype(F32) * cap + rank


def slot_rows(slot, rows, slots, s_ref):
    n, d = rows.shape
    place = (iota((slots, n), 0).astype(F32) == to_row(slot)).astype(BF)
    filled = nn(place, rows).astype(BF)
    fs, _, _, r, h = s_ref.shape
    for f in range(fs):
        for c in range(2):
            at = (f * 2 + c) * r
            for y in range(2):
                s_ref[f, y, c] = filled[at : at + r, y * h : (y + 1) * h]


def token_rows(slot, rb_ref, slots):
    n = slot.shape[0]
    sources = rb_ref.shape[0]
    parts = []
    for f in range(sources // 4):
        for c in range(2):
            parts.append(
                jnp.concatenate([rb_ref[f * 4 + c], rb_ref[f * 4 + 2 + c]], axis=1)
            )
    rows = jnp.concatenate(parts, axis=0)
    place = (iota((n, slots), 1).astype(F32) == slot).astype(BF)
    return nn(place, rows)


def z_peers(zs):
    f, i, z = lax.axis_index("fsdp"), lax.axis_index("ctx"), lax.axis_index("tp")
    return [(f, i, lax.rem(z + s, zs)) for s in range(1, zs)]


def greet(peers):
    barrier = pltpu.get_barrier_semaphore()
    for peer in peers:
        pl.semaphore_signal(barrier, inc=1, device_id=peer, device_id_type=MESH)
    pl.semaphore_wait(barrier, len(peers))


def remote(src, dst, send, recv, peer):
    return pltpu.make_async_remote_copy(
        src_ref=src, dst_ref=dst, send_sem=send, recv_sem=recv, device_id=peer, device_id_type=MESH
    )


def sum_over_z(zs, x_ref, o_ref, parts, send, recv):
    z = lax.axis_index("tp")
    n = x_ref.shape[0] // zs
    peers = z_peers(zs)

    def chunk(at):
        return pl.ds(pl.multiple_of(at * n, n), n)

    first = []
    for s in range(1, zs):
        to = lax.rem(z + s, zs)
        cp = remote(x_ref.at[chunk(to)], parts.at[s - 1], send.at[0, s - 1], recv.at[0, s - 1], peers[s - 1])
        cp.start()
        first.append(cp)
    total = x_ref[chunk(z), :].astype(F32)
    for s in range(1, zs):
        first[s - 1].wait_recv()
        total = total + parts[s - 1].astype(F32)
    o_ref[chunk(z), :] = total.astype(BF)
    second = []
    for s in range(1, zs):
        cp = remote(o_ref.at[chunk(z)], o_ref.at[chunk(z)], send.at[1, s - 1], recv.at[1, s - 1], peers[s - 1])
        cp.start()
        second.append(cp)
    for cp in second:
        cp.wait_recv()
    for cp in first + second:
        cp.wait_send()


def sum_scratch(zs, n, d):
    return [
        VMEM((zs - 1, n // zs, d), BF),
        pltpu.SemaphoreType.DMA((2, zs - 1)),
        pltpu.SemaphoreType.DMA((2, zs - 1)),
    ]


def group_peers(fs):
    f, i, z = lax.axis_index("fsdp"), lax.axis_index("ctx"), lax.axis_index("tp")
    y, c = lax.div(i, 2), lax.rem(i, 2)
    out = []
    for df in range(fs):
        for dy in range(2):
            for dc in range(2):
                if df or dy or dc:
                    fp = lax.rem(f + df, fs)
                    yp = y if dy == 0 else 1 - y
                    cp = c if dc == 0 else 1 - c
                    out.append((fp, yp, cp, (fp, yp * 2 + cp, z)))
    return out


def project_body(tok_ref, w_ref, t_ref, normed_ref, qt_ref, kv_ref):
    d, k = tok_ref.shape[1], qt_ref.shape[0]
    xhat, _ = norm_parts(tok_ref[...].astype(F32))
    normed = (xhat * t_ref[32:33, :].astype(F32)).astype(BF)
    normed_ref[...] = normed
    qkv = nn(normed, w_ref[:, : 3 * k])
    qt_ref[...] = jnp.transpose(qkv[:, :k]).astype(BF)
    kv_ref[...] = qkv[:, k:].astype(BF)


def attend_body(at_ref, qt_ref, own_ref, far_ref, sib_ref, valid_ref, w_ref, pt_ref, ctx_ref, out_ref):
    k, n = qt_ref.shape
    mine, prefix = at_ref[0], at_ref[1]
    pieces = [own_ref[...], far_ref[...], sib_ref[0], sib_ref[1]]
    offsets = [at_ref[2 + j] for j in range(4)]
    query = iota((n, n), 1) + mine * n
    allowed = []
    for j in range(4):
        key = iota((n, n), 0) + offsets[j] * n
        col = to_col(valid_ref[pl.ds(offsets[j], 1), :])
        allowed.append(((key <= query) | (key < prefix)) & ((col > 0.5) | (key == query)))
    outs = []
    for h in range(k // HD):
        lo = h * HD
        qt = qt_ref[lo : lo + HD, :]
        scores = [
            jnp.where(allowed[j], nn(pieces[j][:, lo : lo + HD], qt) * (1.0 / math.sqrt(HD)), -1e30)
            for j in range(4)
        ]
        top = jnp.max(scores[0], axis=0, keepdims=True)
        for j in range(1, 4):
            top = jnp.maximum(top, jnp.max(scores[j], axis=0, keepdims=True))
        exps = [jnp.exp(s - top) for s in scores]
        total = sum(jnp.sum(e, axis=0, keepdims=True) for e in exps)
        acc = jnp.zeros((HD, n), F32)
        for j in range(4):
            w = (exps[j] / total).astype(BF)
            pt_ref[h, j] = w
            acc = acc + tn(pieces[j][:, k + lo : k + lo + HD], w)
        outs.append(acc)
    ctx = jnp.transpose(jnp.concatenate(outs, axis=0)).astype(BF)
    ctx_ref[...] = ctx
    out_ref[...] = nt(ctx, w_ref[:, OUT_AT : OUT_AT + k]).astype(BF)


def attend_back_body(gb_ref, qt_ref, own_ref, far_ref, sib_ref, pt_ref, ctx_ref, w_ref, dq_ref, near_ref, away_ref, og_ref):
    k, n = qt_ref.shape
    scale = 1.0 / math.sqrt(HD)
    gb = gb_ref[...]
    og_ref[...] = tn(gb, ctx_ref[...])
    gct = jnp.transpose(nn(gb, w_ref[:, OUT_AT : OUT_AT + k]).astype(BF).astype(F32)).astype(BF)
    pieces = [own_ref[...], far_ref[...], sib_ref[0], sib_ref[1]]
    dqs = []
    for h in range(k // HD):
        lo = h * HD
        dot_ = gct[lo : lo + HD, :]
        qt = qt_ref[lo : lo + HD, :]
        ws = [pt_ref[h, j] for j in range(4)]
        dps = [nn(pieces[j][:, k + lo : k + lo + HD], dot_) for j in range(4)]
        mean = sum(jnp.sum(ws[j].astype(F32) * dps[j], axis=0, keepdims=True) for j in range(4))
        dq = jnp.zeros((HD, n), F32)
        for j in range(4):
            ds = (ws[j].astype(F32) * (dps[j] - mean)).astype(BF)
            dq = dq + tn(pieces[j][:, lo : lo + HD], ds)
            target = near_ref if j < 2 else away_ref
            target[j % 2, :, lo : lo + HD] = nt(ds, qt) * scale
            target[j % 2, :, k + lo : k + lo + HD] = nt(ws[j], dot_)
        dqs.append(dq * scale)
    dq_ref[...] = jnp.transpose(jnp.concatenate(dqs, axis=0)).astype(BF)


def mixing_back_body(normed_ref, dq_ref, near_ref, sib_ref, far_ref, w_ref, mg_ref, gn_ref):
    kv = (near_ref[0] + sib_ref[0] + far_ref[...].astype(F32)).astype(BF)
    g = jnp.concatenate([dq_ref[...], kv], axis=1)
    mg_ref[...] = tn(normed_ref[...], g)
    gn_ref[...] = nt(g, w_ref[:, : g.shape[1]]).astype(BF)


def expert_grad_body(c_ref, half, act_ref, actx_ref, gh_ref, ghx_ref, r_ref, rx_ref, g_ref, gx_ref, up_ref, down_ref):
    e = pl.program_id(0)
    c = c_ref[0]
    q = up_ref.shape[1]

    def emit(a, g, rows, grads):
        n = a.shape[0]
        rows = rows.reshape(n, 2 * q)
        grads = grads.reshape(n, 2 * q)
        rows = jnp.where(c == 0, rows[:, :q], rows[:, q:])
        grads = jnp.where(c == 0, grads[:, :q], grads[:, q:])
        up_ref[0] = tn(rows, g)
        down_ref[0] = tn(a, grads)

    own = lax.div(e, half) == c

    @pl.when(own)
    def _():
        emit(act_ref[0], gh_ref[0], r_ref[...], g_ref[...])

    @pl.when(jnp.logical_not(own))
    def _():
        emit(actx_ref[0], ghx_ref[0], rx_ref[...], gx_ref[...])


def mix_body(zs, cap, br_ref, tok_ref, t_ref, as_ref, res_ref, mi_ref, gate_ref, s_ref, summed, parts, send, recv):
    greet(z_peers(zs))
    sum_over_z(zs, br_ref, summed, parts, send, recv)
    residual = tok_ref[...].astype(F32) + summed[...].astype(F32)
    res_ref[...] = residual
    xhat, _ = norm_parts(residual)
    mixed_in = (xhat * t_ref[33:34, :].astype(F32)).astype(BF)
    mi_ref[...] = mixed_in
    hot, slot = route(as_ref[...], 32, cap)
    rows = nn(hot.astype(BF), t_ref[0:32, :])
    logit = jnp.sum(mixed_in.astype(F32) * rows, axis=-1, keepdims=True)
    gate_ref[...] = jax.nn.sigmoid(logit)
    slot_rows(slot, mixed_in, 32 * cap, s_ref)


def loss_body(zs, cap, rb_ref, res_ref, gate_ref, as_ref, valid_ref, at_ref, tea_ref, cot_ref,
              act_ref, gm_ref, gl_ref, stat_ref, s_ref, partial_rows, summed, parts, send, recv):
    greet(z_peers(zs))
    hot, slot = route(as_ref[...], 32, cap)
    partial_rows[...] = token_rows(slot, rb_ref, 32 * cap).astype(BF)
    sum_over_z(zs, partial_rows, summed, parts, send, recv)
    returned = summed[...].astype(F32)
    gate = gate_ref[...]
    d = returned.shape[1]
    mixed = res_ref[...] + gate * returned
    act_ref[...] = mixed.astype(BF)
    diff = mixed - tea_ref[...].astype(F32)
    valid = to_col(valid_ref[pl.ds(at_ref[6], 1), :])
    scale = 1.0 / (jnp.sum(valid_ref[...]) * d)
    weighted = valid * diff
    grad = cot_ref[...].astype(F32) + 2.0 * weighted * scale
    gm_ref[...] = grad
    grad_gate = jnp.sum(grad * returned, axis=-1, keepdims=True)
    gl_ref[...] = grad_gate * gate * (1.0 - gate)
    stat_ref[...] = jnp.zeros_like(stat_ref)
    stat_ref[0:1, 0:32] = jnp.sum(hot, axis=0, keepdims=True)
    stat_ref[1:2, 0:32] = jnp.sum(hot * gate, axis=0, keepdims=True)
    stat_ref[2:3, :] = jnp.broadcast_to(jnp.sum(weighted * diff * scale), (1, 128))
    slot_rows(slot, (gate * grad).astype(BF), 32 * cap, s_ref)


def norm2_body(zs, cap, rb_ref, res_ref, mi_ref, gm_ref, gl_ref, as_ref, t_ref,
               gr_ref, gb_ref, cg_ref, g2_ref, partial_rows, summed, parts, send, recv):
    greet(z_peers(zs))
    hot, slot = route(as_ref[...], 32, cap)
    partial_rows[...] = token_rows(slot, rb_ref, 32 * cap).astype(BF)
    sum_over_z(zs, partial_rows, summed, parts, send, recv)
    gl = gl_ref[...]
    rows = nn(hot.astype(BF), t_ref[0:32, :])
    grad_in = summed[...].astype(F32) + gl * rows
    cg_ref[...] = _dot(mi_ref[...].astype(F32), hot * gl, 0, 0, TOP)
    xhat, inv = norm_parts(res_ref[...])
    g2_ref[...] = jnp.broadcast_to(jnp.sum(grad_in * xhat, axis=0, keepdims=True), g2_ref.shape)
    grad = gm_ref[...] + norm_back(grad_in, xhat, inv, t_ref[33:34, :].astype(F32))
    gr_ref[...] = grad
    gb_ref[...] = grad.astype(BF)


def norm1_body(zs, gn_ref, tok_ref, t_ref, gr_ref, tg_ref, g1_ref, summed, parts, send, recv):
    greet(z_peers(zs))
    sum_over_z(zs, gn_ref, summed, parts, send, recv)
    grad = summed[...].astype(F32)
    xhat, inv = norm_parts(tok_ref[...].astype(F32))
    g1_ref[...] = jnp.broadcast_to(jnp.sum(grad * xhat, axis=0, keepdims=True), g1_ref.shape)
    tg_ref[...] = (gr_ref[...] + norm_back(grad, xhat, inv, t_ref[32:33, :].astype(F32))).astype(BF)


def expert_body(back, fs, *refs):
    if back:
        (s_ref, up_ref, upx_ref, dn_ref, dnx_ref, gp_ref, st_ref,
         rb_ref, h_ref, r_ref, sto_ref,
         wu, wd, ps, pr, ret, stin, wsem, d_s, d_r, x_s, x_r, b_s, b_r, t_s, t_r) = refs
    else:
        (s_ref, up_ref, upx_ref, dn_ref, dnx_ref,
         rb_ref, h_ref, r_ref, gp_ref,
         wu, wd, ps, pr, ret, wsem, d_s, d_r, x_s, x_r, b_s, b_r) = refs
    f, i, z = lax.axis_index("fsdp"), lax.axis_index("ctx"), lax.axis_index("tp")
    y, c = lax.div(i, 2), lax.rem(i, 2)
    me = f * 4 + i
    half, width = wu.shape[0], up_ref.shape[1]
    sources, _, dh = r_ref.shape
    cap = 16
    n = sources * cap
    peers = group_peers(fs)
    across = (f, (1 - y) * 2 + c, z)

    own = pl.ds(pl.multiple_of(c * width, 64), width)
    other = pl.ds(pl.multiple_of((1 - c) * width, 64), width)
    mine = pl.ds(c * half, half)
    loads = [
        pltpu.make_async_copy(up_ref.at[mine], wu.at[:, own, :], wsem.at[0]),
        pltpu.make_async_copy(upx_ref, wu.at[:, other, :], wsem.at[1]),
        pltpu.make_async_copy(dn_ref.at[mine], wd.at[c], wsem.at[2]),
        pltpu.make_async_copy(dnx_ref, wd.at[1 - c], wsem.at[3]),
        pltpu.make_async_copy(s_ref.at[f, y, c], r_ref.at[me], wsem.at[4]),
    ]
    for cp in loads:
        cp.start()
    greet([p[3] for p in peers])
    out = []
    for k, (fp, yp, cp_, peer) in enumerate(peers):
        cp = remote(s_ref.at[fp, yp, cp_], r_ref.at[me], d_s.at[k], d_r.at[k], peer)
        cp.start()
        out.append(cp)
    stats = []
    if back:
        for k, (fp, yp, cp_, peer) in enumerate(peers):
            cp = remote(st_ref, stin.at[me], t_s.at[k], t_r.at[k], peer)
            cp.start()
            stats.append(cp)
    for cp in loads:
        cp.wait()
    for cp in out:
        cp.wait_recv()

    def cross(e):
        return remote(ps.at[e], pr.at[e], x_s.at[e], x_r.at[e], across)

    def rows_of(e):
        return r_ref[:, pl.ds(pl.multiple_of(e * cap, cap), cap), :].reshape(n, dh)

    @pl.loop(0, half)
    def _(e):
        rows = rows_of(e)
        if back:
            part = nt(rows[:, :width], wd[0, e]) + nt(rows[:, width:], wd[1, e])
        else:
            part = nn(rows, wu[e])
        ps[e] = part.astype(BF)
        cross(e).start()

    @pl.loop(0, half)
    def _(e):
        cross(e).wait_recv()
        total = ps[e].astype(F32) + pr[e].astype(F32)
        if back:
            grad = (total * gp_ref[e].astype(F32)).astype(BF)
            h_ref[e] = grad
            rows = nt(grad, wu[e])
        else:
            phi = 0.5 * (1.0 + lax.erf(total * math.sqrt(0.5)))
            act = (total * phi).astype(BF)
            h_ref[e] = act
            bell = jnp.exp(-0.5 * total * total) * (1.0 / math.sqrt(2.0 * math.pi))
            gp_ref[e] = (phi + total * bell).astype(BF)
            rows = jnp.concatenate([nn(act, wd[0, e]), nn(act, wd[1, e])], axis=1)
        ret[:, pl.ds(pl.multiple_of(e * cap, cap), cap), :] = rows.astype(BF).reshape(sources, cap, dh)

    keep = pltpu.make_async_copy(ret.at[me], rb_ref.at[me], wsem.at[5])
    keep.start()
    returns = []
    for k, (fp, yp, cp_, peer) in enumerate(peers):
        cp = remote(ret.at[fp * 4 + yp * 2 + cp_], rb_ref.at[me], b_s.at[k], b_r.at[k], peer)
        cp.start()
        returns.append(cp)
    if back:
        stin[me] = st_ref[...]
        for cp in stats:
            cp.wait_recv()
        total = stin[0]
        for k in range(1, sources):
            total = total + stin[k]
        sto_ref[...] = total
    keep.wait()
    for cp in returns:
        cp.wait_recv()
    for cp in out + returns + stats:
        cp.wait_send()

    @pl.loop(0, half)
    def _(e):
        cross(e).wait_send()


def expert_call(back, fs, s, up, upx, dn, dnx, extra, cid):
    experts, width, units = up.shape
    half = experts // 2
    sources = fs * 4
    cap = 16
    n = sources * cap
    dh = 2 * width
    row = (sources, half * cap, dh)
    hid = (half, n, units)
    outs = [sds(row, BF), sds(hid, BF), sds(row, BF)]
    outs.append(sds((8, 128), F32) if back else sds(hid, BF))
    peers = sources - 1
    dma = pltpu.SemaphoreType.DMA
    scratch = [
        VMEM((half, dh, units), BF),
        VMEM((2, half, units, width), BF),
        VMEM(hid, BF),
        VMEM(hid, BF),
        VMEM(row, BF),
    ]
    if back:
        scratch.append(VMEM((sources, 8, 128), F32))
    scratch += [dma((6,))] + [dma((peers,))] * 2 + [dma((half,))] * 2 + [dma((peers,))] * 2
    if back:
        scratch += [dma((peers,))] * 2
    anyspec = pl.BlockSpec(memory_space=ANY)
    return pl.pallas_call(
        partial(expert_body, back, fs),
        out_shape=outs,
        in_specs=[vspec()] + [anyspec] * 4 + [vspec()] * len(extra),
        out_specs=[vspec()] * len(outs),
        scratch_shapes=scratch,
        compiler_params=params(cid),
        name="experts_back" if back else "experts",
    )(s, up, upx, dn, dnx, *extra)


def per_device(tokens, mixing_weight, output_weight, first_gain, second_gain, centroids, expert_up,
               expert_down, prefix_length, assignment, validity, teacher, cotangent):
    fs, zs = lax.axis_size("fsdp"), lax.axis_size("tp")
    f, i = lax.axis_index("fsdp"), lax.axis_index("ctx")
    c = lax.rem(i, 2)
    y = lax.div(i, 2)
    n, d = tokens.shape[1], tokens.shape[2]
    rows = mixing_weight.shape[0]
    k = mixing_weight.shape[2]
    local_experts, width, units = expert_up.shape
    half = local_experts // 2
    experts = centroids.shape[0]
    cap = 2 * n // experts
    sources = fs * 4
    core_pairs = [(0, 1), (1, 0), (2, 3), (3, 2)]
    y_pairs = [(0, 2), (2, 0), (1, 3), (3, 1)]

    def core_swap(v):
        return lax.ppermute(v, "ctx", core_pairs)

    def y_swap(v):
        return lax.ppermute(v, "ctx", y_pairs)

    packed = jnp.zeros((rows, COLS), BF)
    packed = jnp.concatenate(
        [
            mixing_weight.reshape(rows, 3 * k),
            jnp.zeros((rows, OUT_AT - 3 * k), BF),
            output_weight.T,
            centroids.T,
            first_gain[:, None],
            second_gain[:, None],
            jnp.zeros((rows, COLS - CEN_AT - experts - 2), BF),
        ],
        axis=1,
    )
    pad_rows = -rows % 16 + 16
    last = jnp.pad(validity.astype(BF), ((0, pad_rows - 1), (0, COLS - n)))
    gathered = lax.all_gather(jnp.concatenate([packed, last], axis=0), ("fsdp", "ctx"), axis=0)
    weights = gathered[:, :rows].reshape(d, COLS)
    valid_all = gathered[:, rows, :n].astype(F32)
    table = weights[:, CEN_AT:].T
    table = jnp.pad(table, ((0, 0), (0, 0)))

    up_x = core_swap(lax.dynamic_slice_in_dim(expert_up, (1 - c) * half, half, 0))
    dn_x = core_swap(lax.dynamic_slice_in_dim(expert_down, (1 - c) * half, half, 0))

    tok = tokens[0]
    normed, qt, kv = pl.pallas_call(
        project_body,
        out_shape=[sds((n, d), BF), sds((k, n), BF), sds((n, 2 * k), BF)],
        in_specs=[vspec()] * 3,
        out_specs=[vspec()] * 3,
        compiler_params=params(),
        name="project",
    )(tok, weights, table)
    kv_far = y_swap(kv)
    kv_sib = core_swap(jnp.stack([kv, kv_far]))
    own_valid = lax.dynamic_slice_in_dim(valid_all, f * 4, 4, 0)
    far, sib = i + 2 - 4 * y, i + 1 - 2 * c
    sib_far = sib + 2 - 4 * y
    at = jnp.stack([i, prefix_length[0], i, far, sib, sib_far, f * 4 + i]).astype(jnp.int32)
    smem = pl.BlockSpec(memory_space=pltpu.SMEM)
    heads = k // HD
    pt, ctx, branch = pl.pallas_call(
        attend_body,
        out_shape=[sds((heads, 4, n, n), BF), sds((n, k), BF), sds((n, d), BF)],
        in_specs=[smem] + [vspec()] * 6,
        out_specs=[vspec()] * 3,
        compiler_params=params(),
        name="attend",
    )(at, qt, kv, kv_far, kv_sib, own_valid, weights)

    chosen = assignment[0]
    row_shape = (fs, 2, 2, half * cap, d // 2)
    summed = [VMEM((n, d), BF)] + sum_scratch(zs, n, d)
    residual, mixed_in, gate, slots = pl.pallas_call(
        partial(mix_body, zs, cap),
        out_shape=[sds((n, d), F32), sds((n, d), BF), sds((n, 1), F32), sds(row_shape, BF)],
        in_specs=[vspec()] * 4,
        out_specs=[vspec()] * 4,
        scratch_shapes=summed,
        compiler_params=params(1),
        name="mix",
    )(branch, tok, table, chosen)
    back_rows, act, received, gelu_slope = expert_call(
        False, fs, slots, expert_up, up_x, expert_down, dn_x, (), 2
    )
    activations, grad_mixed, grad_logit, stat, grad_slots = pl.pallas_call(
        partial(loss_body, zs, cap),
        out_shape=[sds((n, d), BF), sds((n, d), F32), sds((n, 1), F32), sds((8, 128), F32), sds(row_shape, BF)],
        in_specs=[vspec()] * 5 + [smem] + [vspec()] * 2,
        out_specs=[vspec()] * 5,
        scratch_shapes=[VMEM((n, d), BF)] + summed,
        compiler_params=params(3),
        name="losses",
    )(back_rows, residual, gate, chosen, valid_all, at, teacher[0], cotangent[0])
    back_grads, grad_hidden, grad_received, stats = expert_call(
        True, fs, grad_slots, expert_up, up_x, expert_down, dn_x, (gelu_slope, stat), 4
    )
    all_tokens = float(n * sources)
    share = stats[0, :experts] / all_tokens - 1.0 / experts
    balance = experts * experts * jnp.sum(share * stats[1, :experts] / all_tokens)
    distill = stats[2, 0]

    act_x, gh_x, rec_x, grec_x = (
        core_swap(act), core_swap(grad_hidden), core_swap(received), core_swap(grad_received)
    )
    grad_residual, grad_branch, centre_grad, g2 = pl.pallas_call(
        partial(norm2_body, zs, cap),
        out_shape=[sds((n, d), F32), sds((n, d), BF), sds((d, experts), F32), sds((8, d), F32)],
        in_specs=[vspec()] * 7,
        out_specs=[vspec()] * 4,
        scratch_shapes=[VMEM((n, d), BF)] + summed,
        compiler_params=params(5),
        name="norm_two",
    )(back_grads, residual, mixed_in, grad_mixed, grad_logit, chosen, table)
    dq, near, away, out_grad = pl.pallas_call(
        attend_back_body,
        out_shape=[sds((n, k), BF), sds((2, n, 2 * k), F32), sds((2, n, 2 * k), F32), sds((d, k), F32)],
        in_specs=[vspec()] * 8,
        out_specs=[vspec()] * 4,
        compiler_params=params(),
        name="attend_back",
    )(grad_branch, qt, kv, kv_far, kv_sib, pt, ctx, weights)
    near_sib = core_swap(away)
    near_far = y_swap((near[1] + near_sib[1]).astype(BF))
    mix_grad, gn = pl.pallas_call(
        mixing_back_body,
        out_shape=[sds((d, 3 * k), F32), sds((n, d), BF)],
        in_specs=[vspec()] * 6,
        out_specs=[vspec()] * 2,
        compiler_params=params(),
        name="mixing_back",
    )(normed, dq, near, near_sib, near_far, weights)

    sums = jnp.concatenate([mix_grad, out_grad, centre_grad], axis=1).reshape(fs, 2, 2, rows, 3 * k + k + experts)
    keep = lax.dynamic_index_in_dim(sums, c, 2, keepdims=False)
    give = lax.dynamic_index_in_dim(sums, 1 - c, 2, keepdims=False)
    sums = keep + core_swap(give)
    sums = lax.dynamic_index_in_dim(sums, y, 1, keepdims=False) + y_swap(
        lax.dynamic_index_in_dim(sums, 1 - y, 1, keepdims=False).astype(BF)
    ).astype(F32)
    total = lax.dynamic_index_in_dim(sums, f, 0, keepdims=False)
    for s in range(1, fs):
        piece = lax.dynamic_index_in_dim(sums, lax.rem(f + s, fs), 0, keepdims=False).astype(BF)
        total = total + lax.ppermute(piece, "fsdp", [(a, (a + s) % fs) for a in range(fs)]).astype(F32)

    tokens_gradient, g1 = pl.pallas_call(
        partial(norm1_body, zs),
        out_shape=[sds((n, d), BF), sds((8, d), F32)],
        in_specs=[vspec()] * 4,
        out_specs=[vspec()] * 2,
        scratch_shapes=summed,
        compiler_params=params(6),
        name="norm_one",
    )(gn, tok, table, grad_residual)
    gains = lax.psum_scatter(jnp.stack([g1[0], g2[0]]), ("fsdp", "ctx"), scatter_dimension=1, tiled=True)

    block = lambda e, *_: (e % half, 0, 0)
    slab = lambda e, *_: (0, e % half, 0)
    slots_in = sources * cap
    up_gradient, down_gradient = pl.pallas_call(
        lambda c_ref, *refs: expert_grad_body(c_ref, half, *refs),
        grid_spec=pltpu.PrefetchScalarGridSpec(
            num_scalar_prefetch=1,
            grid=(local_experts,),
            in_specs=[pl.BlockSpec((1, slots_in, units), block)] * 4
            + [pl.BlockSpec((sources, cap, 2 * width), slab)] * 4,
            out_specs=[
                pl.BlockSpec((1, width, units), lambda e, *_: (e, 0, 0)),
                pl.BlockSpec((1, units, width), lambda e, *_: (e, 0, 0)),
            ],
        ),
        out_shape=[sds(expert_up.shape, F32), sds(expert_down.shape, F32)],
        compiler_params=params(),
        name="expert_grads",
    )(c.reshape(1), act, act_x, grad_hidden, gh_x, received, rec_x, grad_received, grec_x)

    return (
        activations[None],
        tokens_gradient[None],
        total[:, : 3 * k].reshape(rows, 3, k),
        total[:, 3 * k : 4 * k].T,
        gains[0],
        gains[1],
        total[:, 4 * k :].T,
        up_gradient,
        down_gradient,
        balance,
        distill,
    )


def solution(mesh):
    in_specs = (
        P("fsdp", "ctx", None),
        P(("fsdp", "ctx"), None, "tp"),
        P("tp", ("fsdp", "ctx")),
        P(("fsdp", "ctx")),
        P(("fsdp", "ctx")),
        P(None, ("fsdp", "ctx")),
        P("fsdp", "ctx", "tp"),
        P("fsdp", "tp", "ctx"),
        P("fsdp"),
        P("fsdp", "ctx", None),
        P("fsdp", "ctx"),
        P("fsdp", "ctx", None),
        P("fsdp", "ctx", None),
    )
    out_specs = (
        P("fsdp", "ctx", None),
        P("fsdp", "ctx", None),
        P(("fsdp", "ctx"), None, "tp"),
        P("tp", ("fsdp", "ctx")),
        P(("fsdp", "ctx")),
        P(("fsdp", "ctx")),
        P(None, ("fsdp", "ctx")),
        P("fsdp", "ctx", "tp"),
        P("fsdp", "tp", "ctx"),
        P(),
        P(),
    )
    return jax.shard_map(
        per_device, mesh=mesh, in_specs=in_specs, out_specs=out_specs, check_vma=False
    )
```

time: 1310 us -> 432 us (0.33)
  waiting for transfers between devices: 854 us -> 74.2 us
  Pallas kernels: 0 us -> 269 us
  blocking collectives: 215 us -> 0 us
  matrix products: 111 us -> 0 us
  other arithmetic: 37.2 us -> 8.32 us
    reduce_scatter x5 -> x0, waiting for transfers between devices: 604 us -> none  [the longest x1 265 us: per_device(): lax.psum_scatter(down_partial, 'ctx', scatter_dimension=2, tiled=True)]
    pallas_call x0 -> x11, Pallas kernels: none -> 269 us  [the longest x2 125 us: expert_call(): pl.pallas_call(partial(expert_body, back, fs), out_shape=outs, in_specs=[...]
    all_gather x2 -> x1, waiting for transfers between devices: 173 us -> 23.1 us  [per_device(): lax.all_gather(jnp.concatenate([packed, last], axis=0), ('fsdp', 'ctx'),...]
    psum x3 -> x0, blocking collectives: 114 us -> none  [the longest x1 51.8 us: per_device(): lax.psum(slot_partial, 'tp').astype(jnp.bfloat16)]
    dot_general x32 -> x0, matrix products: 107 us -> none  [the longest x1 15.5 us: per_device(): jnp.einsum('sgcf,sgcd->gfd', activated, grad_received, preferred_element_...]
    all_gather x6 -> x0, blocking collectives: 48.5 us -> none  [the longest x1 13.4 us: per_device(): lax.all_gather(mixing_weight, ('fsdp', 'ctx'), axis=0, tiled=True)]
    psum x2 -> x0, waiting for transfers between devices: 33.4 us -> none  [the longest x1 33.4 us: per_device(): branch_output = lax.psum(partial_branch, 'tp')]
    unnamed x2 -> x0, blocking collectives: 28.5 us -> none
  transfers between devices with their start and end apart: 13 -> 15, of which waited for: 10 -> 6; matrix products, arithmetic and copies ran while one was open for 5% -> 11% of each run, Pallas kernels for 0% -> 18%
where the time goes in v1:
time: 432 us; the launch traced here: 430 us
  Pallas kernels  269 us (62%)
  waiting for transfers between devices  74.2 us (17%)
  local copies, waits for them, and re-layouts  55.2 us (13%)
  between operations  16.8 us (4%)
  other arithmetic  8.32 us (2%)
  starting transfers between devices  6.49 us (2%)
    pallas_call x2, Pallas kernels, expert_call(): pl.pallas_call(partial(expert_body, back, fs), out_shape=outs, in_specs=[...  125 us
    unnamed x3, waiting for transfers between devices  34.6 us
    unnamed x39, local copies, waits for them, and re-layouts  29.6 us
    pallas_call x1, Pallas kernels, per_device(): pl.pallas_call(partial(norm2_body, zs, cap), out_shape=[sds((n, d), F32),...  27.2 us
    pallas_call x1, Pallas kernels, per_device(): pl.pallas_call(partial(loss_body, zs, cap), out_shape=[sds((n, d), BF), s...  27.1 us
    pallas_call x1, Pallas kernels, per_device(): pl.pallas_call(partial(norm1_body, zs), out_shape=[sds((n, d), BF), sds((...  24.6 us
    all_gather x1, waiting for transfers between devices, per_device(): lax.all_gather(jnp.concatenate([packed, last], axis=0), ('fsdp', 'ctx'),...  23.1 us
    pallas_call x1, Pallas kernels, per_device(): pl.pallas_call(lambda c_ref, *refs: expert_grad_body(c_ref, half, *refs),...  23 us
  transfers between devices with their start and end apart: 15, of which 6 were waited for; matrix products, arithmetic and copies ran while one was open for 11% of the time, Pallas kernels for 18%

profile of v1, /device:TPU:0, one launch (start us, length us, event | category | flops | bytes accessed | tf_op | source)
XLA Modules:
  0.0 429.8 jit_solution(14444583871387242749)
XLA Ops:
  7.2 0.7 convert_element_type.34
  8.1 1.1 copy.70
  9.1 2.4 concatenate.9
  11.7 0.8 copy.72
  12.6 3.4 constant_dynamic-slice_fusion.1
  16.0 0.5 collective-permute-start.3
  16.4 1.6 constant_dynamic-slice_fusion.2
  18.1 23.1 %all-gather.3.cloned.1.call-done = bf16[896,896]{1,0:T(8,128)(2,1)} async-done(((bf16[112,896]{1,0:T(8,128)(2,1)}), bf16[896,896]{1,0:T(8,128)(2,1)}) %all-gather.3.cloned.1.call-update) | async-done | bytes 1605648 | tf_op jit(solution)/shard_map/all_gather | solution.py:545
  41.2 1.4 slice.60
  42.8 1.0 copy.88
  43.8 2.9 project.1
  46.6 1.4 collective-permute-start
  48.1 5.9 %collective-permute-done.far_ref = bf16[256,384]{1,0:T(8,128)(2,1)S(1)} collective-permute-done((bf16[256,384]{1,0:T(8,128)(2,1)}, bf16[256,384]{1,0:T(8,128)(2,1)S(1)}, u32[]{:S(2)}, u32[]{:S(2)}) %collective-permute-start) | collective-permute-done | bytes 196640 | tf_op jit(solution)/shard_map/ppermute | solution.py:528
  53.9 1.0 pad_maximum_fusion.1
  55.1 7.9 %copy.76.refs_3_ = bf16[16,768,192]{2,1,0:T(8,128)(2,1)} copy(bf16[16,768,192]{1,2,0:T(8,128)(2,1)} %param.20) | data formatting | bytes 9437184 | tf_op args[7]
  63.6 0.8 copy.75.as_ref
  64.4 0.6 stack.36.at_ref
  65.0 4.5 %copy.77.refs_4_ = bf16[8,768,192]{2,1,0:T(8,128)(2,1)} copy(bf16[8,768,192]{1,2,0:T(8,128)(2,1)} %collective-permute-done.3) | data formatting | bytes 4718592 | tf_op jit(solution)/shard_map/ppermute | solution.py:525
  69.5 0.8 slice.62
  70.3 0.6 fusion.6
  70.9 0.6 dynamic-slice_bitcast_fusion.1.valid_ref
  71.5 0.7 copy-done.6
  72.2 5.1 %attend.1 = (bf16[3,4,256,256]{3,2,1,0:T(8,128)(2,1)}, bf16[256,192]{1,0:T(8,128)(2,1)}, bf16[256,768]{1,0:T(8,128)(2,1)}) custom-call(s32[7]{0:T(128)} %stack.36.at_ref, bf16[192,256]{1,0:T(8,128)(2,1)} %get-tuple-element.48.qt_ref, bf16[256,384]{1,0:T(8,128)(2,1)} %get-tuple-element.49.own_ref, bf16[256,384]{1,0:T(8,128)(2,1)} %copy-done.4, ...), custom_call_target="tpu_custom_call" | custom-call | tf_op jit(solution)/shard_map/attend/pallas_call | solution.py:571
  77.3 22.9 %mix.1 = (f32[256,768]{1,0:T(8,128)}, bf16[256,768]{1,0:T(8,128)(2,1)}, f32[256,1]{1,0:T(8,128)}, bf16[2,2,2,128,384]{4,3,2,1,0:T(8,128)(2,1)}) custom-call(bf16[256,768]{1,0:T(8,128)(2,1)} %get-tuple-element.50.br_ref, bf16[256,768]{1,0:T(8,128)(2,1)} %bitcast.58, bf16[64,768]{1,0:T(8,128)(2,1)} %bitcast.61, s32[256,1]{1,0:T(8,128)} %copy.75.as_ref), custom_call_target="tpu_custom_call" | custom-call | tf_op jit(solution)/shard_map/mix/pallas_call | solution.py:583
  100.2 62.7 %experts.1 = (bf16[8,128,384]{2,1,0:T(8,128)(2,1)}, bf16[8,128,768]{2,1,0:T(8,128)(2,1)}, bf16[8,128,384]{2,1,0:T(8,128)(2,1)}, bf16[8,128,768]{2,1,0:T(8,128)(2,1)}) custom-call(bf16[2,2,2,128,384]{4,3,2,1,0:T(8,128)(2,1)} %get-tuple-element.51.refs_0_, bf16[16,192,768]{2,1,0:T(8,128)(2,1)} %refs_1_.3, bf16[8,192,768]{2,1,0:T(8,128)(2,1)} %collective-permute-done.2.refs_2_, ...), custom_call_target="tpu_custom_call" | custom-call | tf_op jit(solution)/shard_map/experts/pallas_call | solution.py:496
  162.9 27.1 %losses.1 = (bf16[256,768]{1,0:T(8,128)(2,1)}, f32[256,768]{1,0:T(8,128)}, f32[256,1]{1,0:T(8,128)}, f32[8,128]{1,0:T(8,128)}, bf16[2,2,2,128,384]{4,3,2,1,0:T(8,128)(2,1)}) custom-call(bf16[8,128,384]{2,1,0:T(8,128)(2,1)} %get-tuple-element.52.rb_ref, f32[256,768]{1,0:T(8,128)} %get-tuple-element.53.res_ref, f32[256,1]{1,0:T(8,128)} %get-tuple-element.54.gate_ref, ...), custom_call_target="tpu_custom_call" | custom-call | tf_op jit(solution)/shard_map/losses/pallas_call | solution.py:595
  190.0 62.7 %experts_back.1 = (bf16[8,128,384]{2,1,0:T(8,128)(2,1)}, bf16[8,128,768]{2,1,0:T(8,128)(2,1)}, bf16[8,128,384]{2,1,0:T(8,128)(2,1)}, f32[8,128]{1,0:T(8,128)}) custom-call(bf16[2,2,2,128,384]{4,3,2,1,0:T(8,128)(2,1)} %get-tuple-element.57.refs_0_, bf16[16,192,768]{2,1,0:T(8,128)(2,1)} %refs_1_.3, bf16[8,192,768]{2,1,0:T(8,128)(2,1)} %collective-permute-done.2.refs_2_, ...), custom_call_target="tpu_custom_call" | custom-call | tf_op jit(solution)/shard_map/experts_back/pallas_call | solution.py:496
  252.7 27.2 %norm_two.1 = (f32[256,768]{1,0:T(8,128)}, bf16[256,768]{1,0:T(8,128)(2,1)}, f32[768,32]{1,0:T(8,128)}, f32[8,768]{1,0:T(8,128)}) custom-call(bf16[8,128,384]{2,1,0:T(8,128)(2,1)} %get-tuple-element.60.rb_ref, f32[256,768]{1,0:T(8,128)} %get-tuple-element.53.res_ref, bf16[256,768]{1,0:T(8,128)(2,1)} %get-tuple-element.61.mi_ref, ...), custom_call_target="tpu_custom_call" | custom-call | tf_op jit(solution)/shard_map/norm_two/pallas_call | solution.py:615
  279.9 6.4 %attend_back.1 = (bf16[256,192]{1,0:T(8,128)(2,1)}, f32[2,256,384]{2,1,0:T(8,128)}, f32[2,256,384]{2,1,0:T(8,128)}, f32[768,192]{1,0:T(8,128)}) custom-call(bf16[256,768]{1,0:T(8,128)(2,1)} %get-tuple-element.64.gb_ref, bf16[192,256]{1,0:T(8,128)(2,1)} %get-tuple-element.48.qt_ref, bf16[256,384]{1,0:T(8,128)(2,1)} %get-tuple-element.49.own_ref, ...), custom_call_target="tpu_custom_call" | custom-call | tf_op jit(solution)/shard_map/attend_back/pallas_call | solution.py:624
  286.3 2.5 collective-permute-done.4.sib_ref
  288.8 1.3 fusion.5
  290.1 1.3 collective-permute-start.5
  291.5 5.7 %collective-permute-done.5.far_ref = bf16[256,384]{1,0:T(8,128)(2,1)S(1)} collective-permute-done((bf16[256,384]{1,0:T(8,128)(2,1)S(1)}, bf16[256,384]{1,0:T(8,128)(2,1)S(1)}, u32[]{:S(2)}, u32[]{:S(2)}) %collective-permute-start.5) | collective-permute-done | bytes 196640 | tf_op jit(solution)/shard_map/ppermute | solution.py:528
  297.2 0.7 copy-done.12
  297.8 4.1 mixing_back.1
  302.0 2.0 pad_maximum_fusion
  303.9 1.3 constant_dynamic-slice_fusion
  305.2 0.5 collective-permute-start.10
  305.7 0.5 copy.82
  306.2 2.4 collective-permute-done.6
  308.7 1.9 copy.83
  310.7 1.2 copy-done.2
  311.9 1.3 collective-permute-start.7
  313.3 1.2 slice.59
  314.5 0.7 slice.53
  315.2 0.5 collective-permute-start.12
  315.7 1.4 multiply_reduce_fusion
  317.7 24.6 %norm_one.1 = (bf16[256,768]{1,0:T(8,128)(2,1)}, f32[8,768]{1,0:T(8,128)}) custom-call(bf16[256,768]{1,0:T(8,128)(2,1)} %get-tuple-element.70.gn_ref, bf16[256,768]{1,0:T(8,128)(2,1)} %bitcast.59, bf16[64,768]{1,0:T(8,128)(2,1)} %bitcast.63, f32[256,768]{1,0:T(8,128)} %get-tuple-element.71.gr_ref), custom_call_target="tpu_custom_call" | custom-call | tf_op jit(solution)/shard_map/norm_one/pallas_call | solution.py:655
  342.3 0.7 slice.52
  343.1 0.9 copy.86
  344.1 1.1 bitcast_add_fusion.1
  345.2 0.7 collective-permute-start.8
  345.9 34.6 %reduce-scatter.4.cloned.1.call-done = f32[96,2]{1,0:T(8,128)} async-done(((f32[768,2]{1,0:T(8,128)}), f32[96,2]{1,0:T(8,128)}) %reduce-scatter.4.cloned.1.call-update) | async-done | bytes 784
  380.5 0.9 fusion.7
  381.4 0.6 copy.91
  382.0 0.6 copy.90
  382.6 0.9 copy-done.7
  383.5 23.0 %expert_grads.1 = (f32[16,192,768]{2,1,0:T(8,128)}, f32[16,768,192]{2,1,0:T(8,128)}) custom-call(s32[1]{0:T(128)} %bitcast.38.c_ref, bf16[8,128,768]{2,1,0:T(8,128)(2,1)} %get-tuple-element.78.refs_0_, bf16[8,128,768]{2,1,0:T(8,128)(2,1)} %collective-permute-done.9.refs_1_, bf16[8,128,768]{2,1,0:T(8,128)(2,1)} %get-tuple-element.79.refs_2_, ...), custom_call_target="tpu_custom_call" | custom-call | tf_op jit(solution)/shard_map/expert_grads/pallas_call | solution.py:669
  406.5 11.6 %copy.85 = f32[16,768,192]{1,2,0:T(8,128)} copy(f32[16,768,192]{2,1,0:T(8,128)} %get-tuple-element.126) | data formatting | bytes 18874368
  418.1 0.6 slice_bitcast_fusion.1
  418.7 0.6 slice_bitcast_fusion
  419.4 0.9 copy.84
  420.3 0.7 copy.99
  421.0 0.7 copy.100
  (54 shorter events, 1.0 us)
Async XLA Ops:
  7.2 34.0 %all-gather.3.cloned.1.call-start = ((), (), s32[]{:S(2)}) async-start(), calls=%async_computation.1 | async-start | bytes 1806336 | tf_op jit(solution)/shard_map/all_gather | solution.py:545
  12.5 367.9 %reduce-scatter.4.cloned.1.call-start = ((), (), s32[]{:S(2)}) async-start(), calls=%async_computation.2 | async-start | bytes 442368
  12.6 3.8 copy-start.1
  16.0 49.0 %collective-permute-start.3 = (bf16[8,768,192]{1,2,0:T(8,128)(2,1)}, bf16[8,768,192]{1,2,0:T(8,128)(2,1)}, u32[]{:S(2)}, u32[]{:S(2)}) collective-permute-start(bf16[8,768,192]{1,2,0:T(8,128)(2,1)} %constant_dynamic-slice_fusion.1), channel_id=1, source_target_pairs={{0,4},{4,0},{8,12},{12,8},{1,5},{5,1},{9,13},{13,9},{2,6},{6,2},{1... | collective-permute-start | bytes 7077896 | tf_op jit(solution)/shard_map/ppermute | solution.py:525
  18.0 82.2 %collective-permute-start.2 = (bf16[8,192,768]{2,1,0:T(8,128)(2,1)}, bf16[8,192,768]{2,1,0:T(8,128)(2,1)}, u32[]{:S(2)}, u32[]{:S(2)}) collective-permute-start(bf16[8,192,768]{2,1,0:T(8,128)(2,1)} %constant_dynamic-slice_fusion.2), channel_id=1, source_target_pairs={{0,4},{4,0},{8,12},{12,8},{1,5},{5,1},{9,13},{13,9},{2,6},{6,2},{1... | collective-permute-start | bytes 7077896 | tf_op jit(solution)/shard_map/ppermute | solution.py:525
  42.7 1.1 copy-start
  46.6 7.3 %collective-permute-start = (bf16[256,384]{1,0:T(8,128)(2,1)}, bf16[256,384]{1,0:T(8,128)(2,1)S(1)}, u32[]{:S(2)}, u32[]{:S(2)}) collective-permute-start(bf16[256,384]{1,0:T(8,128)(2,1)} %get-tuple-element.49.own_ref), channel_id=1, source_target_pairs={{0,8},{8,0},{4,12},{12,4},{1,9},{9,1},{5,13},{13,5},{2,10},{10,2},... | collective-permute-start | bytes 589832 | tf_op jit(solution)/shard_map/ppermute | solution.py:528
  53.9 9.0 %copy-start.4 = (bf16[256,384]{1,0:T(8,128)(2,1)}, bf16[256,384]{1,0:T(8,128)(2,1)S(1)}, u32[]{:S(2)}) copy-start(bf16[256,384]{1,0:T(8,128)(2,1)S(1)} %collective-permute-done.far_ref) | copy-start | bytes 589828
  55.0 16.5 %collective-permute-start.1 = (bf16[2,256,384]{2,1,0:T(8,128)(2,1)S(1)}, bf16[2,256,384]{2,1,0:T(8,128)(2,1)S(1)}, u32[]{:S(2)}, u32[]{:S(2)}) collective-permute-start(bf16[2,256,384]{2,1,0:T(8,128)(2,1)S(1)} %pad_maximum_fusion.1), channel_id=1, source_target_pairs={{0,4},{4,0},{8,12},{12,8},{1,5},{5,1},{9,13},{13,9},{2,6},{6,2},{1... | collective-permute-start | bytes 1179656 | tf_op jit(solution)/shard_map/ppermute | solution.py:525
  55.1 8.6 %copy-start.13 = (s32[1,256,1]{1,2,0:T(1,128)S(1)}, s32[1,256,1]{1,2,0:T(1,128)}, u32[]{:S(2)}) copy-start(s32[1,256,1]{1,2,0:T(1,128)} %param.22) | copy-start | bytes 3076
  71.5 0.7 copy-start.6
  286.3 2.5 collective-permute-start.4
  288.8 8.3 %copy-start.5 = (f32[2,256,384]{2,1,0:T(8,128)}, f32[2,256,384]{2,1,0:T(8,128)S(1)}, u32[]{:S(2)}) copy-start(f32[2,256,384]{2,1,0:T(8,128)S(1)} %collective-permute-done.4.sib_ref) | copy-start | bytes 2359300
  290.1 11.8 %copy-start.8 = (f32[768,192]{1,0:T(8,128)S(1)}, f32[768,192]{1,0:T(8,128)}, u32[]{:S(2)}) copy-start(f32[768,192]{1,0:T(8,128)} %get-tuple-element.74) | copy-start | bytes 1769476
  290.1 11.8 %copy-start.9 = (f32[768,32]{1,0:T(8,128)S(1)}, f32[768,32]{1,0:T(8,128)}, u32[]{:S(2)}) copy-start(f32[768,32]{1,0:T(8,128)} %get-tuple-element.75) | copy-start | bytes 294916
  290.1 7.0 %collective-permute-start.5 = (bf16[256,384]{1,0:T(8,128)(2,1)S(1)}, bf16[256,384]{1,0:T(8,128)(2,1)S(1)}, u32[]{:S(2)}, u32[]{:S(2)}) collective-permute-start(bf16[256,384]{1,0:T(8,128)(2,1)S(1)} %fusion.5), channel_id=1, source_target_pairs={{0,8},{8,0},{4,12},{12,4},{1,9},{9,1},{5,13},{13,5},{2,10},{10,2},... | collective-permute-start | bytes 589832 | tf_op jit(solution)/shard_map/ppermute | solution.py:528
  297.2 0.7 copy-start.12
  305.2 3.5 collective-permute-start.6
  305.2 77.4 %collective-permute-start.10 = (bf16[8,128,768]{2,1,0:T(8,128)(2,1)}, bf16[8,128,768]{2,1,0:T(8,128)(2,1)}, u32[]{:S(2)}, u32[]{:S(2)}) collective-permute-start(bf16[8,128,768]{2,1,0:T(8,128)(2,1)} %get-tuple-element.79.refs_2_), channel_id=1, source_target_pairs={{0,4},{4,0},{8,12},{12,8},{1,5},{5,1},{9,13},{13,9},{2,6},{6,2},{1... | collective-permute-start | bytes 4718600 | tf_op jit(solution)/shard_map/ppermute | solution.py:525
  305.7 76.9 %collective-permute-start.9 = (bf16[8,128,768]{2,1,0:T(8,128)(2,1)}, bf16[8,128,768]{2,1,0:T(8,128)(2,1)}, u32[]{:S(2)}, u32[]{:S(2)}) collective-permute-start(bf16[8,128,768]{2,1,0:T(8,128)(2,1)} %get-tuple-element.78.refs_0_), channel_id=1, source_target_pairs={{0,4},{4,0},{8,12},{12,8},{1,5},{5,1},{9,13},{13,9},{2,6},{6,2},{1... | collective-permute-start | bytes 4718600 | tf_op jit(solution)/shard_map/ppermute | solution.py:525
  310.7 1.2 copy-start.2
  311.9 32.1 %copy-start.3 = (f32[2,2,96,800]{2,3,0,1:T(8,128)S(1)}, f32[2,2,96,800]{2,3,0,1:T(8,128)}, u32[]{:S(2)}) copy-start(f32[2,2,96,800]{2,3,0,1:T(8,128)} %copy-done.2) | copy-start | bytes 3686404
  311.9 32.1 %collective-permute-start.7 = (bf16[2,96,800]{1,2,0:T(8,128)(2,1)S(1)}, bf16[2,96,800]{1,2,0:T(8,128)(2,1)}, u32[]{:S(2)}, u32[]{:S(2)}) collective-permute-start(bf16[2,96,800]{1,2,0:T(8,128)(2,1)S(1)} %fusion.1), channel_id=1, source_target_pairs={{0,8},{8,0},{4,12},{12,4},{1,9},{9,1},{5,13},{13,5},{2,10},{10,2},... | collective-permute-start | bytes 921608 | tf_op jit(solution)/shard_map/ppermute | solution.py:528
  313.3 69.3 %collective-permute-start.11 = (bf16[8,128,384]{2,1,0:T(8,128)(2,1)}, bf16[8,128,384]{2,1,0:T(8,128)(2,1)S(1)}, u32[]{:S(2)}, u32[]{:S(2)}) collective-permute-start(bf16[8,128,384]{2,1,0:T(8,128)(2,1)} %get-tuple-element.80.refs_4_), channel_id=1, source_target_pairs={{0,4},{4,0},{8,12},{12,8},{1,5},{5,1},{9,13},{13,9},{2,6},{6,2},{1... | collective-permute-start | bytes 2359304 | tf_op jit(solution)/shard_map/ppermute | solution.py:525
  315.2 67.4 %collective-permute-start.12 = (bf16[8,128,384]{2,1,0:T(8,128)(2,1)}, bf16[8,128,384]{2,1,0:T(8,128)(2,1)}, u32[]{:S(2)}, u32[]{:S(2)}) collective-permute-start(bf16[8,128,384]{2,1,0:T(8,128)(2,1)} %get-tuple-element.81.refs_6_), channel_id=1, source_target_pairs={{0,4},{4,0},{8,12},{12,8},{1,5},{5,1},{9,13},{13,9},{2,6},{6,2},{1... | collective-permute-start | bytes 2359304 | tf_op jit(solution)/shard_map/ppermute | solution.py:525
  345.2 72.9 %collective-permute-start.8 = (bf16[96,800]{0,1:T(8,128)(2,1)S(1)}, bf16[96,800]{0,1:T(8,128)(2,1)S(1)}, u32[]{:S(2)}, u32[]{:S(2)}) collective-permute-start(bf16[96,800]{0,1:T(8,128)(2,1)S(1)} %fusion.4), channel_id=1, source_target_pairs={{0,16},{16,0},{1,17},{17,1},{2,18},{18,2},{3,19},{19,3},{4,20},{20... | collective-permute-start | bytes 460808 | tf_op jit(solution)/shard_map/ppermute | solution.py:653
  382.6 0.9 copy-start.7
  418.1 2.2 copy-start.10
  418.1 3.0 copy-start.11
Sparse Core Ops, SparseCore 0:
  12.7 28.5 all-gather.2
  344.2 36.2 reduce-scatter.3

commit v2 on v1

v2 whole, which is shorter than its diff:
```python
from functools import partial
import math

import jax
import jax.numpy as jnp
from jax import lax
from jax.experimental import pallas as pl
from jax.experimental.pallas import tpu as pltpu
from jax.sharding import PartitionSpec as P

HD = 64
EPSILON = 1e-05
BF = jnp.bfloat16
F32 = jnp.float32
MESH = pl.DeviceIdType.MESH
TOP = lax.Precision.HIGHEST
VMEM = pltpu.VMEM
ANY = pl.ANY
CAP = 16
EXP = 32
TAB = 48


def _dot(a, b, ca, cb, precision=None):
    return lax.dot_general(
        a, b, (((ca,), (cb,)), ((), ())), preferred_element_type=F32, precision=precision
    )


def nn(a, b):
    return _dot(a, b, 1, 0)


def nt(a, b):
    return _dot(a, b, 1, 1)


def tn(a, b):
    return _dot(a, b, 0, 0)


def vspec():
    return pl.BlockSpec(memory_space=VMEM)


def sds(shape, dtype):
    return jax.ShapeDtypeStruct(shape, dtype)


def params(cid=None, mib=56):
    if cid is None:
        return pltpu.CompilerParams(vmem_limit_bytes=mib * 2**20)
    return pltpu.CompilerParams(
        vmem_limit_bytes=mib * 2**20, collective_id=cid, has_side_effects=True
    )


def iota(shape, dim):
    return lax.broadcasted_iota(jnp.int32, shape, dim)


def to_col(row):
    n = row.shape[1]
    return jnp.sum(jnp.where(iota((n, n), 0) == iota((n, n), 1), row, 0.0), axis=1, keepdims=True)


def to_row(col):
    n = col.shape[0]
    return jnp.sum(jnp.where(iota((n, n), 0) == iota((n, n), 1), col, 0.0), axis=0, keepdims=True)


def norm_parts(x):
    c = x - jnp.mean(x, axis=-1, keepdims=True)
    inv = lax.rsqrt(jnp.mean(c * c, axis=-1, keepdims=True) + EPSILON)
    return c * inv, inv


def norm_back(grad, xhat, inv, gain):
    gx = grad * gain
    return inv * (
        gx
        - jnp.mean(gx, axis=-1, keepdims=True)
        - xhat * jnp.mean(gx * xhat, axis=-1, keepdims=True)
    )


def route(chosen):
    n = chosen.shape[1]
    chosen = to_col(chosen.astype(F32))
    hot = (chosen == iota((n, EXP), 1).astype(F32)).astype(F32)
    lower = (iota((n, n), 1) < iota((n, n), 0)).astype(BF)
    earlier = nn(lower, hot.astype(BF))
    rank = jnp.sum(earlier * hot, axis=1, keepdims=True)
    return hot, chosen * CAP + rank


def slot_rows(slot, rows, s_ref):
    n, d = rows.shape
    place = (iota((EXP * CAP, n), 0).astype(F32) == to_row(slot)).astype(BF)
    filled = nn(place, rows).astype(BF)
    fs, _, _, r, h = s_ref.shape
    for f in range(fs):
        for c in range(2):
            at = (f * 2 + c) * r
            for y in range(2):
                s_ref[f, y, c] = filled[at : at + r, y * h : (y + 1) * h]


def token_rows(slot, rb_ref):
    n = slot.shape[0]
    sources = rb_ref.shape[0]
    parts = []
    for f in range(sources // 4):
        for c in range(2):
            parts.append(
                jnp.concatenate([rb_ref[f * 4 + c], rb_ref[f * 4 + 2 + c]], axis=1)
            )
    rows = jnp.concatenate(parts, axis=0)
    place = (iota((n, EXP * CAP), 1).astype(F32) == slot).astype(BF)
    return nn(place, rows)


def z_peers(zs):
    f, i, z = lax.axis_index("fsdp"), lax.axis_index("ctx"), lax.axis_index("tp")
    return [(f, i, lax.rem(z + s, zs)) for s in range(1, zs)]


def greet(peers):
    barrier = pltpu.get_barrier_semaphore()
    for peer in peers:
        pl.semaphore_signal(barrier, inc=1, device_id=peer, device_id_type=MESH)
    pl.semaphore_wait(barrier, len(peers))


def remote(src, dst, send, recv, peer):
    return pltpu.make_async_remote_copy(
        src_ref=src, dst_ref=dst, send_sem=send, recv_sem=recv, device_id=peer, device_id_type=MESH
    )


def sum_over_z(zs, x_ref, o_ref, parts, send, recv):
    z = lax.axis_index("tp")
    n = x_ref.shape[0] // zs
    peers = z_peers(zs)

    def chunk(at):
        return pl.ds(pl.multiple_of(at * n, n), n)

    first = []
    for s in range(1, zs):
        to = lax.rem(z + s, zs)
        cp = remote(x_ref.at[chunk(to)], parts.at[s - 1], send.at[0, s - 1], recv.at[0, s - 1], peers[s - 1])
        cp.start()
        first.append(cp)
    total = x_ref[chunk(z), :].astype(F32)
    for s in range(1, zs):
        first[s - 1].wait_recv()
        total = total + parts[s - 1].astype(F32)
    o_ref[chunk(z), :] = total.astype(BF)
    second = []
    for s in range(1, zs):
        cp = remote(o_ref.at[chunk(z)], o_ref.at[chunk(z)], send.at[1, s - 1], recv.at[1, s - 1], peers[s - 1])
        cp.start()
        second.append(cp)
    for cp in second:
        cp.wait_recv()
    for cp in first + second:
        cp.wait_send()


def sum_scratch(zs, n, d):
    return [
        VMEM((zs - 1, n // zs, d), BF),
        pltpu.SemaphoreType.DMA((2, zs - 1)),
        pltpu.SemaphoreType.DMA((2, zs - 1)),
    ]


def group_peers(fs):
    f, i, z = lax.axis_index("fsdp"), lax.axis_index("ctx"), lax.axis_index("tp")
    y, c = lax.div(i, 2), lax.rem(i, 2)
    out = []
    for df in range(fs):
        for dy in range(2):
            for dc in range(2):
                if df or dy or dc:
                    fp = lax.rem(f + df, fs)
                    yp = y if dy == 0 else 1 - y
                    cp = c if dc == 0 else 1 - c
                    out.append((fp, yp, cp, (fp, yp * 2 + cp, z)))
    return out


def attend(mine, prefix, offsets, qt_ref, kv_ref, valid_ref, row0, pt_ref):
    k, n = qt_ref.shape
    query = iota((n, n), 1) + mine * n
    allowed = []
    for j in range(4):
        key = iota((n, n), 0) + offsets[j] * n
        col = to_col(valid_ref[pl.ds(row0 + offsets[j], 1), :])
        allowed.append(((key <= query) | (key < prefix)) & ((col > 0.5) | (key == query)))
    outs = []
    for h in range(k // HD):
        lo = h * HD
        qt = qt_ref[lo : lo + HD, :]
        scores = [
            jnp.where(allowed[j], nn(kv_ref[j, :, lo : lo + HD], qt) * (1.0 / math.sqrt(HD)), -1e30)
            for j in range(4)
        ]
        top = jnp.max(scores[0], axis=0, keepdims=True)
        for j in range(1, 4):
            top = jnp.maximum(top, jnp.max(scores[j], axis=0, keepdims=True))
        exps = [jnp.exp(s - top) for s in scores]
        share = 1.0 / sum(jnp.sum(e, axis=0, keepdims=True) for e in exps)
        acc = jnp.zeros((HD, n), F32)
        for j in range(4):
            w = (exps[j] * share).astype(BF)
            pt_ref[h, j] = w
            acc = acc + tn(kv_ref[j, :, k + lo : k + lo + HD], w)
        outs.append(acc)
    return jnp.transpose(jnp.concatenate(outs, axis=0)).astype(BF)


def attend_back(gct, qt_ref, kv_ref, pt_ref, near_ref, away_ref):
    k, n = qt_ref.shape
    scale = 1.0 / math.sqrt(HD)
    dqs = []
    for h in range(k // HD):
        lo = h * HD
        dot_ = gct[lo : lo + HD, :]
        qt = qt_ref[lo : lo + HD, :]
        ws = [pt_ref[h, j] for j in range(4)]
        dps = [nn(kv_ref[j, :, k + lo : k + lo + HD], dot_) for j in range(4)]
        mean = sum(jnp.sum(ws[j].astype(F32) * dps[j], axis=0, keepdims=True) for j in range(4))
        dq = jnp.zeros((HD, n), F32)
        for j in range(4):
            ds = (ws[j].astype(F32) * (dps[j] - mean)).astype(BF)
            dq = dq + tn(kv_ref[j, :, lo : lo + HD], ds)
            target = near_ref if j < 2 else away_ref
            target[j % 2, :, lo : lo + HD] = nt(ds, qt) * scale
            target[j % 2, :, k + lo : k + lo + HD] = nt(ws[j], dot_)
        dqs.append(dq * scale)
    return jnp.transpose(jnp.concatenate(dqs, axis=0)).astype(BF)


def expert_grad_body(c_ref, half, l_ref, lx_ref, r_ref, rx_ref, out_ref):
    e = pl.program_id(0)
    c = c_ref[0]
    q = out_ref.shape[1]

    def emit(left, right):
        left = left.reshape(right.shape[0], 2 * q)
        left = jnp.where(c == 0, left[:, :q], left[:, q:])
        out_ref[0] = tn(left, right)

    own = lax.div(e, half) == c

    @pl.when(own)
    def _():
        emit(l_ref[...], r_ref[0])

    @pl.when(jnp.logical_not(own))
    def _():
        emit(lx_ref[...], rx_ref[0])


def expert_grads(c, left, left_x, right, right_x, name):
    half, n, units = right.shape
    sources, _, dh = left.shape
    own = lambda e, c_ref: jnp.clip(e - c_ref[0] * half, 0, half - 1)
    sib = lambda e, c_ref: jnp.clip(e - (1 - c_ref[0]) * half, 0, half - 1)
    return pl.pallas_call(
        lambda c_ref, *refs: expert_grad_body(c_ref, half, *refs),
        grid_spec=pltpu.PrefetchScalarGridSpec(
            num_scalar_prefetch=1,
            grid=(2 * half,),
            in_specs=[
                pl.BlockSpec((sources, CAP, dh), lambda e, c_ref: (0, own(e, c_ref), 0)),
                pl.BlockSpec((sources, CAP, dh), lambda e, c_ref: (0, sib(e, c_ref), 0)),
                pl.BlockSpec((1, n, units), lambda e, c_ref: (own(e, c_ref), 0, 0)),
                pl.BlockSpec((1, n, units), lambda e, c_ref: (sib(e, c_ref), 0, 0)),
            ],
            out_specs=pl.BlockSpec((1, dh // 2, units), lambda e, c_ref: (e, 0, 0)),
        ),
        out_shape=sds((2 * half, dh // 2, units), F32),
        compiler_params=params(),
        cost_estimate=pl.CostEstimate(
            flops=4 * half * n * units * dh, bytes_accessed=2 * half * dh * units * 3, transcendentals=0
        ),
        name=name,
    )(c.reshape(1), left, left_x, right, right_x)


def reduce_body(zs, fs, rows, k, experts, *refs):
    own_ref, z_refs = refs[0], refs[1:zs]
    kept_ref, g_refs = refs[zs], refs[zs + 1 : zs + 2 * fs]
    chunk_ref, mix_ref, out_ref, cen_ref, g2_ref = refs[zs + 2 * fs :]
    total = own_ref[...].astype(F32)
    for r in z_refs:
        total = total + r[...].astype(F32)
    n, d = total.shape
    dense = kept_ref[...]
    for r in g_refs:
        dense = dense + r[...].astype(F32)
    for j in range(3):
        mix_ref[j] = dense[:rows, j * k : (j + 1) * k]
    out_ref[...] = jnp.transpose(dense[:rows, 3 * k : 4 * k])
    cen_ref[...] = jnp.transpose(dense[:rows, 4 * k :])[:experts, :]
    last = kept_ref.shape[0] - 16
    g2_ref[...] = dense[last + 1 : last + 2, :rows]
    chunk_ref[0:n, :] = total.astype(BF)
    chunk_ref[n : n + 16, :] = jnp.concatenate(
        [dense[last : last + 16, :rows], jnp.zeros((16, d - rows), F32)], axis=1
    ).astype(BF)


def finish_body(zs, at_ref, tok_ref, t_ref, gr_ref, *refs):
    chunks, (tg_ref, g1_ref, full) = refs[:zs], refs[zs:]
    n = chunks[0].shape[0] - 16
    z = at_ref[0]
    g1 = jnp.zeros((1, full.shape[1]), F32)
    for s in range(zs):
        at = lax.rem(z - s + zs, zs)
        full[pl.ds(pl.multiple_of(at * n, n), n), :] = chunks[s][0:n, :].astype(F32)
        g1 = g1 + chunks[s][n : n + 1, :].astype(F32)
    g1_ref[...] = g1[:, : g1_ref.shape[1]]
    grad = full[...]
    xhat, inv = norm_parts(tok_ref[...].astype(F32))
    tg_ref[...] = (gr_ref[...] + norm_back(grad, xhat, inv, t_ref[32:33, :].astype(F32))).astype(BF)


def whereabouts():
    f, i, z = lax.axis_index("fsdp"), lax.axis_index("ctx"), lax.axis_index("tp")
    return f, i, z, lax.div(i, 2), lax.rem(i, 2)


def head_body(fs, zs, gather, *refs):
    if gather:
        (prefix_ref, tok_ref, mix_ref, ow_ref, small_ref, as_ref, up_ref, dn_ref,
         w3_ref, wo_ref, t_ref, valid_ref, upx_ref, dnx_ref,
         normed_ref, qt_ref, kv_ref, pt_ref, ctx_ref, res_ref, mi_ref, gate_ref, s_ref,
         small_all, branch, summed, parts, send, recv, wx_s, wx_r, kv_s, kv_r, p_s, p_r, q_s, q_r) = refs
    else:
        (prefix_ref, tok_ref, w3_ref, wo_ref, t_ref, valid_ref, as_ref, up_ref, dn_ref,
         upx_ref, dnx_ref,
         normed_ref, qt_ref, kv_ref, pt_ref, ctx_ref, res_ref, mi_ref, gate_ref, s_ref,
         branch, summed, parts, send, recv, wx_s, wx_r, kv_s, kv_r) = refs
    f, i, z, y, c = whereabouts()
    me = f * 4 + i
    half = upx_ref.shape[0]
    k = qt_ref.shape[0]
    sibling = (f, y * 2 + 1 - c, z)
    across = (f, (1 - y) * 2 + c, z)
    same = []
    for df in range(fs):
        for dy in range(2):
            if df or dy:
                fp = lax.rem(f + df, fs)
                yp = y if dy == 0 else 1 - y
                same.append(((fp, yp * 2 + c, z), df, dy))
    greeted = same if gather else [s for s in same if s[1] == 0]
    greet([s[0] for s in greeted] + [sibling] + z_peers(zs))

    give = pl.ds((1 - c) * half, half)
    swaps = [
        remote(up_ref.at[give], upx_ref, wx_s.at[0], wx_r.at[0], sibling),
        remote(dn_ref.at[give], dnx_ref, wx_s.at[1], wx_r.at[1], sibling),
    ]
    waits = []
    xhat, _ = norm_parts(tok_ref[...].astype(F32))
    if gather:
        rows = mix_ref.shape[1]

        def places(at):
            span = pl.ds(pl.multiple_of(at * rows, rows), rows)
            return [w3_ref.at[:, span, :], wo_ref.at[span, :], small_all.at[at]]

        span = pl.ds(pl.multiple_of(me * rows, rows), rows)
        w3_ref[:, span, :] = mix_ref[...]
        wo_ref[span, :] = jnp.transpose(ow_ref[...].astype(F32)).astype(BF)
        small_all[me] = small_ref[...]
        sends, relays = [], []
        for n_, (peer, df, dy) in enumerate(same):
            for m, ref in enumerate(places(me)):
                cp = remote(ref, ref, p_s.at[n_, m], p_r.at[n_, m], peer)
                cp.start()
                sends.append(cp)
        for m, ref in enumerate(places(me)):
            cp = remote(ref, ref, q_s.at[0, m], q_r.at[0, m], sibling)
            cp.start()
            relays.append(cp)
        for n_, (peer, df, dy) in enumerate(same):
            fp = lax.rem(f - df + fs, fs)
            yp = y if dy == 0 else 1 - y
            for m, ref in enumerate(places(fp * 4 + yp * 2 + c)):
                sends[n_ * 3 + m].wait_recv()
                cp = remote(ref, ref, q_s.at[n_ + 1, m], q_r.at[n_ + 1, m], sibling)
                cp.start()
                relays.append(cp)
        for cp in relays:
            cp.wait_recv()
        sources = fs * 4
        t_ref[...] = jnp.concatenate([small_all[s, :, :rows] for s in range(sources)], axis=1)
        for s in range(sources):
            valid_ref[s : s + 1, :] = small_all[s, 34:35, :].astype(F32)
        waits += sends + relays
    for cp in swaps:
        cp.start()
    normed = (xhat * t_ref[32:33, :].astype(F32)).astype(BF)
    normed_ref[...] = normed
    kv_ref[0, :, :k] = nn(normed, w3_ref[1]).astype(BF)
    kv_ref[0, :, k:] = nn(normed, w3_ref[2]).astype(BF)
    far = remote(kv_ref.at[0], kv_ref.at[1], kv_s.at[0], kv_r.at[0], across)
    sib = remote(kv_ref.at[0], kv_ref.at[2], kv_s.at[1], kv_r.at[1], sibling)
    far.start()
    sib.start()
    qt_ref[...] = jnp.transpose(nn(normed, w3_ref[0])).astype(BF)
    far.wait_recv()
    relay = remote(kv_ref.at[1], kv_ref.at[3], kv_s.at[2], kv_r.at[2], sibling)
    relay.start()
    sib.wait_recv()
    relay.wait_recv()
    offsets = [i, (1 - y) * 2 + c, y * 2 + 1 - c, (1 - y) * 2 + 1 - c]
    ctx = attend(i, prefix_ref[0], offsets, qt_ref, kv_ref, valid_ref, f * 4, pt_ref)
    ctx_ref[...] = ctx
    branch[...] = nt(ctx, wo_ref[...]).astype(BF)
    sum_over_z(zs, branch, summed, parts, send, recv)
    residual = tok_ref[...].astype(F32) + summed[...].astype(F32)
    res_ref[...] = residual
    xhat, _ = norm_parts(residual)
    mixed_in = (xhat * t_ref[33:34, :].astype(F32)).astype(BF)
    mi_ref[...] = mixed_in
    hot, slot = route(as_ref[...])
    rows_ = nn(hot.astype(BF), t_ref[0:EXP, :])
    logit = jnp.sum(mixed_in.astype(F32) * rows_, axis=-1, keepdims=True)
    gate_ref[...] = jax.nn.sigmoid(logit)
    slot_rows(slot, mixed_in, s_ref)
    for cp in swaps:
        cp.wait_recv()
    for cp in waits + swaps + [far, sib, relay]:
        cp.wait_send()


def loss_body(zs, rb_ref, res_ref, gate_ref, as_ref, valid_ref, tea_ref, cot_ref,
              act_ref, gm_ref, gl_ref, stat_ref, s_ref, partial_rows, summed, parts, send, recv):
    greet(z_peers(zs))
    f, i, _, _, _ = whereabouts()
    hot, slot = route(as_ref[...])
    partial_rows[...] = token_rows(slot, rb_ref).astype(BF)
    sum_over_z(zs, partial_rows, summed, parts, send, recv)
    returned = summed[...].astype(F32)
    gate = gate_ref[...]
    d = returned.shape[1]
    mixed = res_ref[...] + gate * returned
    act_ref[...] = mixed.astype(BF)
    diff = mixed - tea_ref[...].astype(F32)
    valid = to_col(valid_ref[pl.ds(f * 4 + i, 1), :])
    scale = 1.0 / (jnp.sum(valid_ref[...]) * d)
    weighted = valid * diff
    grad = cot_ref[...].astype(F32) + 2.0 * weighted * scale
    gm_ref[...] = grad
    grad_gate = jnp.sum(grad * returned, axis=-1, keepdims=True)
    gl_ref[...] = grad_gate * gate * (1.0 - gate)
    stat_ref[...] = jnp.zeros_like(stat_ref)
    stat_ref[0:1, 0:EXP] = jnp.sum(hot, axis=0, keepdims=True)
    stat_ref[1:2, 0:EXP] = jnp.sum(hot * gate, axis=0, keepdims=True)
    stat_ref[2:3, :] = jnp.broadcast_to(jnp.sum(weighted * diff * scale), (1, 128))
    slot_rows(slot, (gate * grad).astype(BF), s_ref)


def back_body(fs, zs, rows, rb_ref, res_ref, mi_ref, gm_ref, gl_ref, as_ref, tok_ref, t_ref, w3_ref, wo_ref,
              normed_ref, qt_ref, kv_ref, pt_ref, ctx_ref, *refs):
    gr_ref, own_ref = refs[0:2]
    z_refs = refs[2 : 1 + zs]
    kept_ref = refs[1 + zs]
    g_refs = refs[2 + zs : 1 + zs + 2 * fs]
    (partial_rows, summed, parts, near, away, away_in, far_out, far_in, gn, dense, dense_in,
     send, recv, k_s, k_r) = refs[1 + zs + 2 * fs :]
    f, i, z, y, c = whereabouts()
    sibling = (f, y * 2 + 1 - c, z)
    across = (f, (1 - y) * 2 + c, z)
    greet(z_peers(zs) + [sibling, across])
    hot, slot = route(as_ref[...])
    partial_rows[...] = token_rows(slot, rb_ref).astype(BF)
    sum_over_z(zs, partial_rows, summed, parts, send, recv)
    n, d = res_ref.shape
    k = qt_ref.shape[0]
    gl = gl_ref[...]
    grad_in = summed[...].astype(F32) + gl * nn(hot.astype(BF), t_ref[0:EXP, :])
    xhat, inv = norm_parts(res_ref[...])
    g2 = jnp.sum(grad_in * xhat, axis=0, keepdims=True)
    grad = gm_ref[...] + norm_back(grad_in, xhat, inv, t_ref[33:34, :].astype(F32))
    gr_ref[...] = grad
    gb = grad.astype(BF)
    gct = jnp.transpose(nn(gb, wo_ref[...])).astype(BF)
    dq = attend_back(gct, qt_ref, kv_ref, pt_ref, near, away)
    swap = remote(away, away_in, k_s.at[0], k_r.at[0], sibling)
    swap.start()
    og = tn(gb, ctx_ref[...])
    cg = _dot(mi_ref[...].astype(F32), hot * gl, 0, 0, TOP)
    swap.wait_recv()
    far_out[...] = (near[1] + away_in[1]).astype(BF)
    cross = remote(far_out, far_in, k_s.at[1], k_r.at[1], across)
    cross.start()
    normed = normed_ref[...]
    mg = [tn(normed, dq), None, None]
    gq = nt(dq, w3_ref[0])
    cross.wait_recv()
    kvg = (near[0] + away_in[0] + far_in[...].astype(F32)).astype(BF)
    mg[1] = tn(normed, kvg[:, :k])
    mg[2] = tn(normed, kvg[:, k:])
    partial_normed = gq + nt(kvg[:, :k], w3_ref[1]) + nt(kvg[:, k:], w3_ref[2])
    gn[...] = partial_normed.astype(BF)
    xhat, _ = norm_parts(tok_ref[...].astype(F32))
    g1 = jnp.sum(partial_normed * xhat, axis=0, keepdims=True)
    last = dense.shape[3] - 16
    dense[:, :, :, last:, :] = jnp.zeros((fs, 2, 2, 16, dense.shape[4]), F32)
    for s in range(4 * fs):
        at = (s // 4, s % 4 // 2, s % 2)
        lo = s * rows
        for j in range(3):
            dense[at[0], at[1], at[2], 0:rows, j * k : (j + 1) * k] = mg[j][lo : lo + rows, :]
        dense[at[0], at[1], at[2], 0:rows, 3 * k : 4 * k] = og[lo : lo + rows, :]
        dense[at[0], at[1], at[2], 0:rows, 4 * k :] = cg[lo : lo + rows, :]
        dense[at[0], at[1], at[2], last : last + 1, 0:rows] = g1[:, lo : lo + rows]
        dense[at[0], at[1], at[2], last + 1 : last + 2, 0:rows] = g2[:, lo : lo + rows]
    pair = remote(dense.at[:, :, 1 - c], dense_in, k_s.at[2], k_r.at[2], sibling)
    pair.start()
    m = n // zs
    own_ref[...] = gn[pl.ds(pl.multiple_of(z * m, m), m), :]
    for s in range(1, zs):
        to = lax.rem(z + s, zs)
        z_refs[s - 1][...] = gn[pl.ds(pl.multiple_of(to * m, m), m), :]
    pair.wait_recv()
    kept_ref[...] = dense[f, y, c] + dense_in[f, y]
    at = 0
    for df in range(fs):
        for dy in range(2):
            if df or dy:
                fp = lax.rem(f + df, fs)
                yp = y if dy == 0 else 1 - y
                g_refs[at][...] = (dense[fp, yp, c] + dense_in[fp, yp]).astype(BF)
                at += 1
    for cp in (swap, cross, pair):
        cp.wait_send()


def expert_body(back, fs, *refs):
    if back:
        (s_ref, up_ref, upx_ref, dn_ref, dnx_ref, gp_ref, st_ref,
         rb_ref, h_ref, r_ref, sto_ref,
         wu, wd, ps, pr, ret, stin, wsem, d_s, d_r, x_s, x_r, b_s, b_r, t_s, t_r) = refs
    else:
        (s_ref, up_ref, upx_ref, dn_ref, dnx_ref,
         rb_ref, h_ref, r_ref, gp_ref,
         wu, wd, ps, pr, ret, wsem, d_s, d_r, x_s, x_r, b_s, b_r) = refs
    f, i, z = lax.axis_index("fsdp"), lax.axis_index("ctx"), lax.axis_index("tp")
    y, c = lax.div(i, 2), lax.rem(i, 2)
    me = f * 4 + i
    half, width = wu.shape[0], up_ref.shape[1]
    sources, _, dh = r_ref.shape
    cap = CAP
    n = sources * cap
    peers = group_peers(fs)
    across = (f, (1 - y) * 2 + c, z)

    own = pl.ds(pl.multiple_of(c * width, 64), width)
    other = pl.ds(pl.multiple_of((1 - c) * width, 64), width)
    mine = pl.ds(c * half, half)
    loads = [
        pltpu.make_async_copy(up_ref.at[mine], wu.at[:, own, :], wsem.at[0]),
        pltpu.make_async_copy(upx_ref, wu.at[:, other, :], wsem.at[1]),
        pltpu.make_async_copy(dn_ref.at[mine], wd.at[:, own, :], wsem.at[2]),
        pltpu.make_async_copy(dnx_ref, wd.at[:, other, :], wsem.at[3]),
        pltpu.make_async_copy(s_ref.at[f, y, c], r_ref.at[me], wsem.at[4]),
    ]
    for cp in loads:
        cp.start()
    greet([p[3] for p in peers])
    out = []
    for k, (fp, yp, cp_, peer) in enumerate(peers):
        cp = remote(s_ref.at[fp, yp, cp_], r_ref.at[me], d_s.at[k], d_r.at[k], peer)
        cp.start()
        out.append(cp)
    stats = []
    if back:
        for k, (fp, yp, cp_, peer) in enumerate(peers):
            cp = remote(st_ref, stin.at[me], t_s.at[k], t_r.at[k], peer)
            cp.start()
            stats.append(cp)
    for cp in loads:
        cp.wait()
    for cp in out:
        cp.wait_recv()

    def cross(e):
        return remote(ps.at[e], pr.at[e], x_s.at[e], x_r.at[e], across)

    def rows_of(e):
        return r_ref[:, pl.ds(pl.multiple_of(e * cap, cap), cap), :].reshape(n, dh)

    @pl.loop(0, half)
    def _(e):
        rows = rows_of(e)
        if back:
            part = nn(rows, wd[e])
        else:
            part = nn(rows, wu[e])
        ps[e] = part.astype(BF)
        cross(e).start()

    @pl.loop(0, half)
    def _(e):
        cross(e).wait_recv()
        total = ps[e].astype(F32) + pr[e].astype(F32)
        if back:
            grad = (total * gp_ref[e].astype(F32)).astype(BF)
            h_ref[e] = grad
            rows = nt(grad, wu[e])
        else:
            phi = 0.5 * (1.0 + lax.erf(total * math.sqrt(0.5)))
            act = (total * phi).astype(BF)
            h_ref[e] = act
            bell = jnp.exp(-0.5 * total * total) * (1.0 / math.sqrt(2.0 * math.pi))
            gp_ref[e] = (phi + total * bell).astype(BF)
            rows = nt(act, wd[e])
        ret[:, pl.ds(pl.multiple_of(e * cap, cap), cap), :] = rows.astype(BF).reshape(sources, cap, dh)

    keep = pltpu.make_async_copy(ret.at[me], rb_ref.at[me], wsem.at[5])
    keep.start()
    returns = []
    for k, (fp, yp, cp_, peer) in enumerate(peers):
        cp = remote(ret.at[fp * 4 + yp * 2 + cp_], rb_ref.at[me], b_s.at[k], b_r.at[k], peer)
        cp.start()
        returns.append(cp)
    if back:
        stin[me] = st_ref[...]
        for cp in stats:
            cp.wait_recv()
        total = stin[0]
        for k in range(1, sources):
            total = total + stin[k]
        sto_ref[...] = total
    keep.wait()
    for cp in returns:
        cp.wait_recv()
    for cp in out + returns + stats:
        cp.wait_send()

    @pl.loop(0, half)
    def _(e):
        cross(e).wait_send()


def expert_call(back, fs, s, up, upx, dn, dnx, extra, cid):
    experts, width, units = up.shape
    half = experts // 2
    sources = fs * 4
    cap = CAP
    n = sources * cap
    dh = 2 * width
    row = (sources, half * cap, dh)
    hid = (half, n, units)
    outs = [sds(row, BF), sds(hid, BF), sds(row, BF)]
    outs.append(sds((8, 128), F32) if back else sds(hid, BF))
    peers = sources - 1
    dma = pltpu.SemaphoreType.DMA
    scratch = [
        VMEM((half, dh, units), BF),
        VMEM((half, dh, units), BF),
        VMEM(hid, BF),
        VMEM(hid, BF),
        VMEM(row, BF),
    ]
    if back:
        scratch.append(VMEM((sources, 8, 128), F32))
    scratch += [dma((6,))] + [dma((peers,))] * 2 + [dma((half,))] * 2 + [dma((peers,))] * 2
    if back:
        scratch += [dma((peers,))] * 2
    anyspec = pl.BlockSpec(memory_space=ANY)
    return pl.pallas_call(
        partial(expert_body, back, fs),
        out_shape=outs,
        in_specs=[vspec()] + [anyspec] * 4 + [vspec()] * len(extra),
        out_specs=[vspec()] * len(outs),
        scratch_shapes=scratch,
        compiler_params=params(cid),
        name="experts_back" if back else "experts",
    )(s, up, upx, dn, dnx, *extra)


def per_device(tokens, mixing_weight, output_weight, first_gain, second_gain, centroids, expert_up,
               expert_down, prefix_length, assignment, validity, teacher, cotangent):
    fs, zs = lax.axis_size("fsdp"), lax.axis_size("tp")
    f, i, z = lax.axis_index("fsdp"), lax.axis_index("ctx"), lax.axis_index("tp")
    c = lax.rem(i, 2)
    n, d = tokens.shape[1], tokens.shape[2]
    rows, k = mixing_weight.shape[0], mixing_weight.shape[2]
    local_experts, width, units = expert_up.shape
    half = local_experts // 2
    experts = centroids.shape[0]
    sources = fs * 4
    heads = k // HD
    dma = pltpu.SemaphoreType.DMA
    smem = pl.BlockSpec(memory_space=pltpu.SMEM)
    anyspec = pl.BlockSpec(memory_space=ANY)
    core_pairs = [(0, 1), (1, 0), (2, 3), (3, 2)]

    def core_swap(v):
        return lax.ppermute(v, "ctx", core_pairs)

    down = expert_down.transpose(0, 2, 1)
    mixing = mixing_weight.transpose(1, 0, 2)
    tok = tokens[0]
    chosen = assignment.reshape(1, n)
    small = jnp.concatenate(
        [
            jnp.pad(jnp.concatenate([centroids, first_gain[None], second_gain[None]]), ((0, 0), (0, n - rows))),
            validity.astype(BF),
            jnp.zeros((TAB - experts - 3, n), BF),
        ]
    )
    swapped = (half, width, units)
    row_shape = (fs, 2, 2, half * CAP, d // 2)
    weight_shapes = [sds((3, d, k), BF), sds((d, k), BF), sds((TAB, d), BF), sds((sources, n), F32)]
    swap_shapes = [sds(swapped, BF)] * 2
    token_shapes = [
        sds((n, d), BF), sds((k, n), BF), sds((4, n, 2 * k), BF), sds((heads, 4, n, n), BF), sds((n, k), BF),
        sds((n, d), F32), sds((n, d), BF), sds((n, 1), F32), sds(row_shape, BF),
    ]
    summed = [VMEM((n, d), BF)] + sum_scratch(zs, n, d)
    exchange = [VMEM((n, d), BF)] + summed + [dma((2,))] * 2 + [dma((3,))] * 2
    gather = rows % 16 == 0
    if gather:
        head_in = (prefix_length, tok, mixing, output_weight, small, chosen, expert_up, down)
        out_shapes = weight_shapes + swap_shapes + token_shapes
        out_specs = [vspec()] * 4 + [anyspec] * 2 + [vspec()] * 9
        scratch = [VMEM((sources, TAB, n), BF)] + exchange + [dma((2 * fs - 1, 3))] * 2 + [dma((2 * fs, 3))] * 2
    else:
        everyone = ("fsdp", "ctx")
        w3 = lax.all_gather(mixing, everyone, axis=1, tiled=True)
        wo = lax.all_gather(output_weight, everyone, axis=1, tiled=True).T
        table = lax.all_gather(small, everyone, axis=0)
        valid_all = table[:, experts + 2, :].astype(F32)
        table = table[:, :, :rows].transpose(1, 0, 2).reshape(TAB, d)
        head_in = (prefix_length, tok, w3, wo, table, valid_all, chosen, expert_up, down)
        out_shapes = swap_shapes + token_shapes
        out_specs = [anyspec] * 2 + [vspec()] * 9
        scratch = exchange
    results = pl.pallas_call(
        partial(head_body, fs, zs, gather),
        out_shape=out_shapes,
        in_specs=[smem] + [vspec()] * (len(head_in) - 3) + [anyspec] * 2,
        out_specs=out_specs,
        scratch_shapes=scratch,
        compiler_params=params(1),
        name="head",
    )(*head_in)
    if gather:
        w3, wo, table, valid_all = results[:4]
        results = results[4:]
    up_x, dn_x, normed, qt, kv, pt, ctx, residual, mixed_in, gate, slots = results

    back_rows, act, received, gelu_slope = expert_call(False, fs, slots, expert_up, up_x, down, dn_x, (), 2)
    act_x, rec_x = core_swap(act), core_swap(received)
    activations, grad_mixed, grad_logit, stat, grad_slots = pl.pallas_call(
        partial(loss_body, zs),
        out_shape=[sds((n, d), BF), sds((n, d), F32), sds((n, 1), F32), sds((8, 128), F32), sds(row_shape, BF)],
        in_specs=[vspec()] * 7,
        out_specs=[vspec()] * 5,
        scratch_shapes=[VMEM((n, d), BF)] + summed,
        compiler_params=params(3),
        name="losses",
    )(back_rows, residual, gate, chosen, valid_all, teacher[0], cotangent[0])
    back_grads, grad_hidden, grad_received, stats = expert_call(
        True, fs, grad_slots, expert_up, up_x, down, dn_x, (gelu_slope, stat), 4
    )
    gh_x, grec_x = core_swap(grad_hidden), core_swap(grad_received)
    all_tokens = float(n * sources)
    share = stats[0, :experts] / all_tokens - 1.0 / experts
    balance = experts * experts * jnp.sum(share * stats[1, :experts] / all_tokens)
    distill = stats[2, 0]

    padded = rows + (-rows % 16) + 16
    columns = 4 * k + experts
    piece = (padded, columns)
    m = n // zs
    results = pl.pallas_call(
        partial(back_body, fs, zs, rows),
        out_shape=[sds((n, d), F32)] + [sds((m, d), BF)] * zs + [sds(piece, F32)] + [sds(piece, BF)] * (2 * fs - 1),
        in_specs=[vspec()] * 15,
        out_specs=[vspec()] * (1 + zs + 2 * fs),
        scratch_shapes=[
            VMEM((n, d), BF), VMEM((n, d), BF), VMEM((zs - 1, m, d), BF),
            VMEM((2, n, 2 * k), F32), VMEM((2, n, 2 * k), F32), VMEM((2, n, 2 * k), F32),
            VMEM((n, 2 * k), BF), VMEM((n, 2 * k), BF), VMEM((n, d), BF),
            VMEM((fs, 2, 2) + piece, F32), VMEM((fs, 2) + piece, F32),
            dma((2, zs - 1)), dma((2, zs - 1)), dma((3,)), dma((3,)),
        ],
        compiler_params=params(5),
        name="back",
    )(back_grads, residual, mixed_in, grad_mixed, grad_logit, chosen, tok, table, w3, wo, normed, qt, kv, pt, ctx)
    grad_residual, own, kept = results[0], results[1], results[1 + zs]
    z_out, g_out = results[2 : 1 + zs], results[2 + zs :]

    def z_shift(v, s):
        return lax.ppermute(v, "tp", [(a, (a + s) % zs) for a in range(zs)])

    z_in = [z_shift(v, s + 1) for s, v in enumerate(z_out)]
    g_in = []
    for df in range(fs):
        for dy in range(2):
            if df or dy:
                moves = [
                    (a * 4 + b, (a + df) % fs * 4 + (b + 2 * dy) % 4) for a in range(fs) for b in range(4)
                ]
                g_in.append(lax.ppermute(g_out[len(g_in)], ("fsdp", "ctx"), moves))
    up_gradient = expert_grads(c, received, rec_x, grad_hidden, gh_x, "up_grads")
    chunk, mix_part, out_part, cen_part, g2_part = pl.pallas_call(
        partial(reduce_body, zs, fs, rows, k, experts),
        out_shape=[
            sds((m + 16, d), BF), sds((3, rows, k), F32), sds((k, rows), F32), sds((experts, rows), F32),
            sds((1, rows), F32),
        ],
        in_specs=[vspec()] * (zs + 2 * fs),
        out_specs=[vspec()] * 5,
        compiler_params=params(),
        name="reduce",
    )(own, *z_in, kept, *g_in)
    chunks = [chunk] + [z_shift(chunk, s) for s in range(1, zs)]
    down_gradient = expert_grads(c, grad_received, grec_x, act, act_x, "down_grads")
    tokens_gradient, g1_part = pl.pallas_call(
        partial(finish_body, zs),
        out_shape=[sds((n, d), BF), sds((1, rows), F32)],
        in_specs=[smem] + [vspec()] * (3 + zs),
        out_specs=[vspec()] * 2,
        scratch_shapes=[VMEM((n, d), F32)],
        compiler_params=params(),
        name="finish",
    )(z.reshape(1), tok, table, grad_residual, *chunks)

    return (
        activations[None],
        tokens_gradient[None],
        mix_part.transpose(1, 0, 2),
        out_part,
        g1_part[0],
        g2_part[0],
        cen_part,
        up_gradient,
        down_gradient.transpose(0, 2, 1),
        balance,
        distill,
    )


def solution(mesh):
    in_specs = (
        P("fsdp", "ctx", None),
        P(("fsdp", "ctx"), None, "tp"),
        P("tp", ("fsdp", "ctx")),
        P(("fsdp", "ctx")),
        P(("fsdp", "ctx")),
        P(None, ("fsdp", "ctx")),
        P("fsdp", "ctx", "tp"),
        P("fsdp", "tp", "ctx"),
        P("fsdp"),
        P("fsdp", "ctx", None),
        P("fsdp", "ctx"),
        P("fsdp", "ctx", None),
        P("fsdp", "ctx", None),
    )
    out_specs = (
        P("fsdp", "ctx", None),
        P("fsdp", "ctx", None),
        P(("fsdp", "ctx"), None, "tp"),
        P("tp", ("fsdp", "ctx")),
        P(("fsdp", "ctx")),
        P(("fsdp", "ctx")),
        P(None, ("fsdp", "ctx")),
        P("fsdp", "ctx", "tp"),
        P("fsdp", "tp", "ctx"),
        P(),
        P(),
    )
    return jax.shard_map(
        per_device, mesh=mesh, in_specs=in_specs, out_specs=out_specs, check_vma=False
    )
```

time: 432 us -> 337 us (0.78)
  local copies, waits for them, and re-layouts: 55.2 us -> 5.66 us
  waiting for transfers between devices: 74.2 us -> 29 us
  between operations: 16.8 us -> 3.19 us
  starting transfers between devices: 6.49 us -> 17.4 us
  Pallas kernels: 269 us -> 277 us
  other arithmetic: 8.32 us -> 3.47 us
    unnamed x3 -> x0, waiting for transfers between devices: 34.6 us -> none
    unnamed x39 -> x25, local copies, waits for them, and re-layouts: 29.6 us -> 4.38 us
    all_gather x1 -> x0, waiting for transfers between devices: 23.1 us -> none  [per_device(): lax.all_gather(jnp.concatenate([packed, last], axis=0), ('fsdp', 'ctx'),...]
    ppermute x4 -> x9, waiting for transfers between devices: 11.5 us -> 29 us  [the longest x6 17.4 us: z_shift(): return lax.ppermute(v, 'tp', [(a, (a + s) % zs) for a in range(zs)])]
    ppermute x4 -> x9, starting transfers between devices: 4.8 us -> 16 us  [the longest x6 11.6 us: z_shift(): return lax.ppermute(v, 'tp', [(a, (a + s) % zs) for a in range(zs)])]
    pallas_call x9 -> x7, Pallas kernels: 143 us -> 152 us  [the longest x1 51.1 us: per_device(): pl.pallas_call(partial(head_body, fs, zs, gather), out_shape=out_shapes,...]
    dynamic_slice x5 -> x0, local copies, waits for them, and re-layouts: 7.36 us -> none  [the longest x1 3.38 us: per_device(): lax.dynamic_slice_in_dim(expert_down, (1 - c) * half, half, 0)]
    ppermute x2 -> x0, local copies, waits for them, and re-layouts: 6.34 us -> none  [core_swap(): return lax.ppermute(v, 'ctx', core_pairs)]
  transfers between devices with their start and end apart: 15 -> 13, of which waited for: 6 -> 8; matrix products, arithmetic and copies ran while one was open for 11% -> 1% of each run, Pallas kernels for 18% -> 45%
where the time goes in v2:
time: 337 us; the launch traced here: 336 us
  Pallas kernels  277 us (82%)
  waiting for transfers between devices  29 us (9%)
  starting transfers between devices  17.4 us (5%)
  local copies, waits for them, and re-layouts  5.66 us (2%)
  other arithmetic  3.47 us (1%)
    pallas_call x2, Pallas kernels, expert_call(): pl.pallas_call(partial(expert_body, back, fs), out_shape=outs, in_specs=[...  125 us
    pallas_call x1, Pallas kernels, per_device(): pl.pallas_call(partial(head_body, fs, zs, gather), out_shape=out_shapes,...  51.1 us
    pallas_call x1, Pallas kernels, per_device(): pl.pallas_call(partial(back_body, fs, zs, rows), out_shape=[sds((n, d), F...  43.4 us
    pallas_call x2, Pallas kernels, expert_grads(): pl.pallas_call(lambda c_ref, *refs: expert_grad_body(c_ref, half, *refs),...  27.9 us
    pallas_call x1, Pallas kernels, per_device(): pl.pallas_call(partial(loss_body, zs), out_shape=[sds((n, d), BF), sds((n...  24.7 us
    ppermute x6, waiting for transfers between devices, z_shift(): return lax.ppermute(v, 'tp', [(a, (a + s) % zs) for a in range(zs)])  17.4 us
    ppermute x3, waiting for transfers between devices, per_device(): g_in.append(lax.ppermute(g_out[len(g_in)], ('fsdp', 'ctx'), moves))  11.6 us
    ppermute x6, starting transfers between devices, z_shift(): return lax.ppermute(v, 'tp', [(a, (a + s) % zs) for a in range(zs)])  11.6 us
  transfers between devices with their start and end apart: 13, of which 8 were waited for; matrix products, arithmetic and copies ran while one was open for 1% of the time, Pallas kernels for 45%

profile of v2, /device:TPU:0, one launch (start us, length us, event | category | flops | bytes accessed | tf_op | source)
XLA Modules:
  0.0 335.8 jit_solution(2875578409607369756)
XLA Ops:
  1.3 0.7 convert_element_type.5
  2.0 0.1 pad.7.clone
  2.1 0.7 fusion.4
  2.8 0.7 maximum_maximum_fusion.refs_4_
  3.5 51.1 %head.1 = (bf16[3,768,192]{2,1,0:T(8,128)(2,1)}, bf16[768,192]{1,0:T(8,128)(2,1)}, bf16[48,768]{1,0:T(8,128)(2,1)}, f32[8,256]{1,0:T(8,128)}, bf16[8,192,768]{2,...) custom-call(s32[1]{0:T(128)S(6)} %copy.25.refs_0_, ...), custom_call_target="tpu_custom_call" | custom-call | tf_op jit(solution)/shard_map/head/pallas_call | solution.py:750
  54.6 61.9 %experts.1 = (bf16[8,128,384]{2,1,0:T(8,128)(2,1)}, bf16[8,128,768]{2,1,0:T(8,128)(2,1)}, bf16[8,128,384]{2,1,0:T(8,128)(2,1)}, bf16[8,128,768]{2,1,0:T(8,128)(2,1)}) custom-call(bf16[2,2,2,128,384]{4,3,2,1,0:T(8,128)(2,1)} %get-tuple-element.55.refs_0_, bf16[16,192,768]{2,1,0:T(8,128)(2,1)} %refs_1_.3, bf16[8,192,768]{2,1,0:T(8,128)(2,1)} %get-tuple-element.56.refs_2_, ...), custom_call_target="tpu_custom_call" | custom-call | tf_op jit(solution)/shard_map/experts/pallas_call | solution.py:681
  116.5 0.8 collective-permute-start.12
  117.2 24.7 %losses.1 = (bf16[256,768]{1,0:T(8,128)(2,1)}, f32[256,768]{1,0:T(8,128)}, f32[256,1]{1,0:T(8,128)}, f32[8,128]{1,0:T(8,128)}, bf16[2,2,2,128,384]{4,3,2,1,0:T(8,128)(2,1)}) custom-call(bf16[8,128,384]{2,1,0:T(8,128)(2,1)} %get-tuple-element.58.rb_ref, f32[256,768]{1,0:T(8,128)} %get-tuple-element.59.res_ref, f32[256,1]{1,0:T(8,128)} %get-tuple-element.60.gate_ref, ...), custom_call_target="tpu_custom_call" | custom-call | tf_op jit(solution)/shard_map/losses/pallas_call | solution.py:766
  141.9 63.1 %experts_back.1 = (bf16[8,128,384]{2,1,0:T(8,128)(2,1)}, bf16[8,128,768]{2,1,0:T(8,128)(2,1)}, bf16[8,128,384]{2,1,0:T(8,128)(2,1)}, f32[8,128]{1,0:T(8,128)}) custom-call(bf16[2,2,2,128,384]{4,3,2,1,0:T(8,128)(2,1)} %get-tuple-element.64.refs_0_, bf16[16,192,768]{2,1,0:T(8,128)(2,1)} %refs_1_.3, bf16[8,192,768]{2,1,0:T(8,128)(2,1)} %get-tuple-element.56.refs_2_, ...), custom_call_target="tpu_custom_call" | custom-call | tf_op jit(solution)/shard_map/experts_back/pallas_call | solution.py:681
  205.0 0.6 collective-permute-start.10
  205.6 43.4 %back.1 = (f32[256,768]{1,0:T(8,128)}, bf16[64,768]{1,0:T(8,128)(2,1)}, bf16[64,768]{1,0:T(8,128)(2,1)}, bf16[64,768]{1,0:T(8,128)(2,1)}, bf16[64,768]{1,0:T(8,1...) custom-call(bf16[8,128,384]{2,1,0:T(8,128)(2,1)} %get-tuple-element., ...), custom_call_target="tpu_custom_call" | custom-call | tf_op jit(solution)/shard_map/back/pallas_call | solution.py:788
  249.1 2.7 collective-permute-start
  251.8 2.9 collective-permute-start.1
  254.7 1.7 collective-permute-start.3
  256.4 1.7 collective-permute-done.refs_1_
  258.1 0.0 copy-start.9
  258.1 2.4 collective-permute-start.2
  260.5 1.5 collective-permute-done.1.refs_2_
  262.0 0.0 copy-start.10
  262.0 0.0 collective-permute-start.11
  262.0 2.0 collective-permute-done.2.refs_3_
  264.0 0.0 copy-start.11
  264.0 0.9 collective-permute-start.4
  264.9 0.0 collective-permute-done.3.refs_5_
  264.9 0.0 copy-start.3
  264.9 0.0 collective-permute-start.9
  264.9 6.2 %collective-permute-done.4.refs_6_ = bf16[112,800]{1,0:T(8,128)(2,1)S(1)} collective-permute-done((bf16[112,800]{1,0:T(8,128)(2,1)}, bf16[112,800]{1,0:T(8,128)(2,1)S(1)}, u32[]{:S(2)}, u32[]{:S(2)}) %collective-permute-start.4) | collective-permute-done | bytes 179232 | tf_op jit(solution)/shard_map/ppermute | solution.py:817
  271.1 0.0 copy-start.4
  271.1 1.7 collective-permute-start.5
  272.9 5.4 %collective-permute-done.5.refs_7_ = bf16[112,800]{1,0:T(8,128)(2,1)S(1)} collective-permute-done((bf16[112,800]{1,0:T(8,128)(2,1)}, bf16[112,800]{1,0:T(8,128)(2,1)S(1)}, u32[]{:S(2)}, u32[]{:S(2)}) %collective-permute-start.5) | collective-permute-done | bytes 179232 | tf_op jit(solution)/shard_map/ppermute | solution.py:817
  278.3 0.0 copy-start.5
  278.3 0.0 copy-done.9
  278.3 0.0 copy-done.10
  278.3 0.0 copy-done.11
  278.3 0.0 copy-done.3
  278.3 0.0 copy-done.4
  278.3 0.6 copy-done.5
  279.0 2.3 reduce.2
  281.3 1.6 collective-permute-start.8
  282.9 4.0 %collective-permute-done.8.refs_3_ = bf16[80,768]{1,0:T(8,128)(2,1)S(1)} collective-permute-done((bf16[80,768]{1,0:T(8,128)(2,1)}, bf16[80,768]{1,0:T(8,128)(2,1)S(1)}, u32[]{:S(2)}, u32[]{:S(2)}) %collective-permute-start.8) | collective-permute-done | bytes 122912 | tf_op jit(solution)/shard_map/ppermute | solution.py:807
  286.9 0.0 copy-start.6
  286.9 0.0 collective-permute-start.7
  286.9 6.0 %collective-permute-done.7.refs_2_ = bf16[80,768]{1,0:T(8,128)(2,1)S(1)} collective-permute-done((bf16[80,768]{1,0:T(8,128)(2,1)}, bf16[80,768]{1,0:T(8,128)(2,1)S(1)}, u32[]{:S(2)}, u32[]{:S(2)}) %collective-permute-start.7) | collective-permute-done | bytes 122912 | tf_op jit(solution)/shard_map/ppermute | solution.py:807
  292.8 0.0 copy-start.7
  292.8 1.9 collective-permute-start.6
  294.7 1.2 slice.11
  295.9 1.4 multiply_reduce_fusion
  297.9 2.3 collective-permute-done.6.refs_1_
  300.3 0.0 copy-done.6
  300.3 0.0 copy-done.7
  300.3 0.6 copy-done.8
  300.9 2.8 finish.1
  303.7 0.0 collective-permute-done.11.refs_1_
  303.7 0.0 collective-permute-done.12.refs_3_
  303.7 0.0 copy-start
  303.7 1.1 copy-done
  304.8 13.9 %down_grads.1 = f32[16,192,768]{2,1,0:T(8,128)} custom-call(s32[1]{0:T(128)} %bitcast.14.c_ref, bf16[8,128,384]{2,1,0:T(8,128)(2,1)} %get-tuple-element.96.refs_0_, bf16[8,128,384]{2,1,0:T(8,128)(2,1)} %collective-permute-done.11.refs_1_, bf16[8,128,768]{2,1,0:T(8,128)(2,1)} %get-tuple-element.97.refs_2_, bf16[8,128,768]{2,1,0:T(8,128)(2,1)} %copy-done), custom_call_target="tpu_custom_call" | custom-call | flops 1207959552 | bytes 14155776 | tf_op jit(solution)/shard_map/down_grads/pallas_call | solution.py:272
  318.8 0.0 collective-permute-done.9.refs_1_
  318.8 0.0 collective-permute-done.10.refs_3_
  318.8 0.0 copy-start.1
  318.8 1.2 copy-done.1
  320.0 13.9 %up_grads.1 = f32[16,192,768]{2,1,0:T(8,128)} custom-call(s32[1]{0:T(128)} %bitcast.14.c_ref, bf16[8,128,384]{2,1,0:T(8,128)(2,1)} %get-tuple-element.94.refs_0_, bf16[8,128,384]{2,1,0:T(8,128)(2,1)} %collective-permute-done.9.refs_1_, bf16[8,128,768]{2,1,0:T(8,128)(2,1)} %get-tuple-element.95.refs_2_, bf16[8,128,768]{2,1,0:T(8,128)(2,1)} %copy-done.1), custom_call_target="tpu_custom_call" | custom-call | flops 1207959552 | bytes 14155776 | tf_op jit(solution)/shard_map/up_grads/pallas_call | solution.py:272
  333.9 0.0 copy-done.2
  333.9 0.7 copy.26
  (3 shorter events, 0.0 us)
Async XLA Ops:
  116.5 187.2 %collective-permute-start.12 = (bf16[8,128,768]{2,1,0:T(8,128)(2,1)}, bf16[8,128,768]{2,1,0:T(8,128)(2,1)S(1)}, u32[]{:S(2)}, u32[]{:S(2)}) collective-permute-start(bf16[8,128,768]{2,1,0:T(8,128)(2,1)} %get-tuple-element.97.refs_2_), channel_id=1, source_target_pairs={{0,4},{4,0},{8,12},{12,8},{1,5},{5,1},{9,13},{13,9},{2,6},{6,2},{1... | collective-permute-start | bytes 4718600 | tf_op jit(solution)/shard_map/ppermute | solution.py:710
  205.0 113.8 %collective-permute-start.10 = (bf16[8,128,768]{2,1,0:T(8,128)(2,1)}, bf16[8,128,768]{2,1,0:T(8,128)(2,1)S(1)}, u32[]{:S(2)}, u32[]{:S(2)}) collective-permute-start(bf16[8,128,768]{2,1,0:T(8,128)(2,1)} %get-tuple-element.95.refs_2_), channel_id=1, source_target_pairs={{0,4},{4,0},{8,12},{12,8},{1,5},{5,1},{9,13},{13,9},{2,6},{6,2},{1... | collective-permute-start | bytes 4718600 | tf_op jit(solution)/shard_map/ppermute | solution.py:710
  249.1 9.0 %collective-permute-start = (bf16[64,768]{1,0:T(8,128)(2,1)}, bf16[64,768]{1,0:T(8,128)(2,1)S(1)}, u32[]{:S(2)}, u32[]{:S(2)}) collective-permute-start(bf16[64,768]{1,0:T(8,128)(2,1)} %get-tuple-element.80), channel_id=1, source_target_pairs={{0,1},{1,2},{2,3},{3,0},{4,5},{5,6},{6,7},{7,4},{8,9},{9,10},{10,1... | collective-permute-start | bytes 294920 | tf_op jit(solution)/shard_map/ppermute | solution.py:807
  251.8 10.2 %collective-permute-start.1 = (bf16[64,768]{1,0:T(8,128)(2,1)}, bf16[64,768]{1,0:T(8,128)(2,1)S(1)}, u32[]{:S(2)}, u32[]{:S(2)}) collective-permute-start(bf16[64,768]{1,0:T(8,128)(2,1)} %get-tuple-element.81), channel_id=1, source_target_pairs={{0,2},{1,3},{2,0},{3,1},{4,6},{5,7},{6,4},{7,5},{8,10},{9,11},{10,... | collective-permute-start | bytes 294920 | tf_op jit(solution)/shard_map/ppermute | solution.py:807
  254.7 10.2 %collective-permute-start.3 = (bf16[112,800]{1,0:T(8,128)(2,1)}, bf16[112,800]{1,0:T(8,128)(2,1)S(1)}, u32[]{:S(2)}, u32[]{:S(2)}) collective-permute-start(bf16[112,800]{1,0:T(8,128)(2,1)} %get-tuple-element.84), channel_id=1, source_target_pairs={{0,8},{4,12},{8,0},{12,4},{16,24},{20,28},{24,16},{28,20},{1,9},{5... | collective-permute-start | bytes 537608 | tf_op jit(solution)/shard_map/ppermute | solution.py:817
  258.1 20.2 %copy-start.9 = (bf16[64,768]{1,0:T(8,128)(2,1)}, bf16[64,768]{1,0:T(8,128)(2,1)S(1)}, u32[]{:S(2)}) copy-start(bf16[64,768]{1,0:T(8,128)(2,1)S(1)} %collective-permute-done.refs_1_) | copy-start | bytes 294916
  258.1 5.9 %collective-permute-start.2 = (bf16[64,768]{1,0:T(8,128)(2,1)}, bf16[64,768]{1,0:T(8,128)(2,1)S(1)}, u32[]{:S(2)}, u32[]{:S(2)}) collective-permute-start(bf16[64,768]{1,0:T(8,128)(2,1)} %get-tuple-element.82), channel_id=1, source_target_pairs={{0,3},{1,0},{2,1},{3,2},{4,7},{5,4},{6,5},{7,6},{8,11},{9,8},{10,9... | collective-permute-start | bytes 294920 | tf_op jit(solution)/shard_map/ppermute | solution.py:807
  262.0 16.3 %copy-start.10 = (bf16[64,768]{1,0:T(8,128)(2,1)}, bf16[64,768]{1,0:T(8,128)(2,1)S(1)}, u32[]{:S(2)}) copy-start(bf16[64,768]{1,0:T(8,128)(2,1)S(1)} %collective-permute-done.1.refs_2_) | copy-start | bytes 294916
  262.0 41.7 %collective-permute-start.11 = (bf16[8,128,384]{2,1,0:T(8,128)(2,1)}, bf16[8,128,384]{2,1,0:T(8,128)(2,1)}, u32[]{:S(2)}, u32[]{:S(2)}) collective-permute-start(bf16[8,128,384]{2,1,0:T(8,128)(2,1)} %get-tuple-element.96.refs_0_), channel_id=1, source_target_pairs={{0,4},{4,0},{8,12},{12,8},{1,5},{5,1},{9,13},{13,9},{2,6},{6,2},{1... | collective-permute-start | bytes 2359304 | tf_op jit(solution)/shard_map/ppermute | solution.py:710
  264.0 14.3 %copy-start.11 = (bf16[64,768]{1,0:T(8,128)(2,1)}, bf16[64,768]{1,0:T(8,128)(2,1)S(1)}, u32[]{:S(2)}) copy-start(bf16[64,768]{1,0:T(8,128)(2,1)S(1)} %collective-permute-done.2.refs_3_) | copy-start | bytes 294916
  264.0 7.1 %collective-permute-start.4 = (bf16[112,800]{1,0:T(8,128)(2,1)}, bf16[112,800]{1,0:T(8,128)(2,1)S(1)}, u32[]{:S(2)}, u32[]{:S(2)}) collective-permute-start(bf16[112,800]{1,0:T(8,128)(2,1)} %get-tuple-element.85), channel_id=1, source_target_pairs={{0,16},{4,20},{8,24},{12,28},{16,0},{20,4},{24,8},{28,12},{1,17},{... | collective-permute-start | bytes 537608 | tf_op jit(solution)/shard_map/ppermute | solution.py:817
  264.9 13.4 %copy-start.3 = (bf16[112,800]{1,0:T(8,128)(2,1)}, bf16[112,800]{1,0:T(8,128)(2,1)S(1)}, u32[]{:S(2)}) copy-start(bf16[112,800]{1,0:T(8,128)(2,1)S(1)} %collective-permute-done.3.refs_5_) | copy-start | bytes 537604
  264.9 53.9 %collective-permute-start.9 = (bf16[8,128,384]{2,1,0:T(8,128)(2,1)}, bf16[8,128,384]{2,1,0:T(8,128)(2,1)}, u32[]{:S(2)}, u32[]{:S(2)}) collective-permute-start(bf16[8,128,384]{2,1,0:T(8,128)(2,1)} %get-tuple-element.94.refs_0_), channel_id=1, source_target_pairs={{0,4},{4,0},{8,12},{12,8},{1,5},{5,1},{9,13},{13,9},{2,6},{6,2},{1... | collective-permute-start | bytes 2359304 | tf_op jit(solution)/shard_map/ppermute | solution.py:710
  271.1 7.2 %copy-start.4 = (bf16[112,800]{1,0:T(8,128)(2,1)}, bf16[112,800]{1,0:T(8,128)(2,1)S(1)}, u32[]{:S(2)}) copy-start(bf16[112,800]{1,0:T(8,128)(2,1)S(1)} %collective-permute-done.4.refs_6_) | copy-start | bytes 537604
  271.1 7.2 %collective-permute-start.5 = (bf16[112,800]{1,0:T(8,128)(2,1)}, bf16[112,800]{1,0:T(8,128)(2,1)S(1)}, u32[]{:S(2)}, u32[]{:S(2)}) collective-permute-start(bf16[112,800]{1,0:T(8,128)(2,1)} %get-tuple-element.86), channel_id=1, source_target_pairs={{0,24},{4,28},{8,16},{12,20},{16,8},{20,12},{24,0},{28,4},{1,25},{... | collective-permute-start | bytes 537608 | tf_op jit(solution)/shard_map/ppermute | solution.py:817
  278.3 0.7 copy-start.5
  281.3 5.6 %collective-permute-start.8 = (bf16[80,768]{1,0:T(8,128)(2,1)}, bf16[80,768]{1,0:T(8,128)(2,1)S(1)}, u32[]{:S(2)}, u32[]{:S(2)}) collective-permute-start(bf16[80,768]{1,0:T(8,128)(2,1)} %get-tuple-element.87.refs_0_), channel_id=1, source_target_pairs={{0,3},{1,0},{2,1},{3,2},{4,7},{5,4},{6,5},{7,6},{8,11},{9,8},{10,9... | collective-permute-start | bytes 368648 | tf_op jit(solution)/shard_map/ppermute | solution.py:807
  286.9 13.4 %copy-start.6 = (bf16[80,768]{1,0:T(8,128)(2,1)}, bf16[80,768]{1,0:T(8,128)(2,1)S(1)}, u32[]{:S(2)}) copy-start(bf16[80,768]{1,0:T(8,128)(2,1)S(1)} %collective-permute-done.8.refs_3_) | copy-start | bytes 368644
  286.9 6.0 %collective-permute-start.7 = (bf16[80,768]{1,0:T(8,128)(2,1)}, bf16[80,768]{1,0:T(8,128)(2,1)S(1)}, u32[]{:S(2)}, u32[]{:S(2)}) collective-permute-start(bf16[80,768]{1,0:T(8,128)(2,1)} %get-tuple-element.87.refs_0_), channel_id=1, source_target_pairs={{0,2},{1,3},{2,0},{3,1},{4,6},{5,7},{6,4},{7,5},{8,10},{9,11},{10,... | collective-permute-start | bytes 368648 | tf_op jit(solution)/shard_map/ppermute | solution.py:807
  292.8 7.4 %copy-start.7 = (bf16[80,768]{1,0:T(8,128)(2,1)}, bf16[80,768]{1,0:T(8,128)(2,1)S(1)}, u32[]{:S(2)}) copy-start(bf16[80,768]{1,0:T(8,128)(2,1)S(1)} %collective-permute-done.7.refs_2_) | copy-start | bytes 368644
  292.8 7.4 %collective-permute-start.6 = (bf16[80,768]{1,0:T(8,128)(2,1)}, bf16[80,768]{1,0:T(8,128)(2,1)S(1)}, u32[]{:S(2)}, u32[]{:S(2)}) collective-permute-start(bf16[80,768]{1,0:T(8,128)(2,1)} %get-tuple-element.87.refs_0_), channel_id=1, source_target_pairs={{0,1},{1,2},{2,3},{3,0},{4,5},{5,6},{6,7},{7,4},{8,9},{9,10},{10,1... | collective-permute-start | bytes 368648 | tf_op jit(solution)/shard_map/ppermute | solution.py:807
  300.3 0.6 copy-start.8
  303.7 1.1 copy-start
  318.8 15.1 %copy-start.2 = (bf16[256,768]{1,0:T(8,128)(2,1)S(1)}, bf16[256,768]{1,0:T(8,128)(2,1)}, u32[]{:S(2)}) copy-start(bf16[256,768]{1,0:T(8,128)(2,1)} %get-tuple-element.62) | copy-start | bytes 1179652
  318.8 1.2 copy-start.1

commit v3 on v2

v3 whole, which is shorter than its diff:
```python
from functools import partial
import math

import jax
import jax.numpy as jnp
from jax import lax
from jax.experimental import pallas as pl
from jax.experimental.pallas import tpu as pltpu
from jax.sharding import PartitionSpec as P

HD = 64
EPSILON = 1e-05
BF = jnp.bfloat16
F32 = jnp.float32
MESH = pl.DeviceIdType.MESH
TOP = lax.Precision.HIGHEST
VMEM = pltpu.VMEM
ANY = pl.ANY
CAP = 16
EXP = 32
TAB = 48


def _dot(a, b, ca, cb, precision=None):
    return lax.dot_general(
        a, b, (((ca,), (cb,)), ((), ())), preferred_element_type=F32, precision=precision
    )


def nn(a, b):
    return _dot(a, b, 1, 0)


def nt(a, b):
    return _dot(a, b, 1, 1)


def tn(a, b):
    return _dot(a, b, 0, 0)


def vspec():
    return pl.BlockSpec(memory_space=VMEM)


def sds(shape, dtype):
    return jax.ShapeDtypeStruct(shape, dtype)


def params(cid=None, mib=56):
    if cid is None:
        return pltpu.CompilerParams(vmem_limit_bytes=mib * 2**20)
    return pltpu.CompilerParams(
        vmem_limit_bytes=mib * 2**20, collective_id=cid, has_side_effects=True
    )


def iota(shape, dim):
    return lax.broadcasted_iota(jnp.int32, shape, dim)


def to_col(row):
    n = row.shape[1]
    return jnp.sum(jnp.where(iota((n, n), 0) == iota((n, n), 1), row, 0.0), axis=1, keepdims=True)


def to_row(col):
    n = col.shape[0]
    return jnp.sum(jnp.where(iota((n, n), 0) == iota((n, n), 1), col, 0.0), axis=0, keepdims=True)


def norm_parts(x):
    c = x - jnp.mean(x, axis=-1, keepdims=True)
    inv = lax.rsqrt(jnp.mean(c * c, axis=-1, keepdims=True) + EPSILON)
    return c * inv, inv


def norm_back(grad, xhat, inv, gain):
    gx = grad * gain
    return inv * (
        gx
        - jnp.mean(gx, axis=-1, keepdims=True)
        - xhat * jnp.mean(gx * xhat, axis=-1, keepdims=True)
    )


def shifted(v, by):
    return lax.shift_right_logical(v, by)


class Route:
    def __init__(self, chosen, zs, z):
        n = chosen.shape[1]
        m = n // zs
        per = CAP // zs
        chosen = to_col(chosen.astype(F32))
        self.hot = (chosen == iota((n, EXP), 1).astype(F32)).astype(BF)
        lower = (iota((n, n), 1) < iota((n, n), 0)).astype(BF)
        rank = jnp.sum(nn(lower, self.hot) * self.hot.astype(F32), axis=1, keepdims=True)
        turn = jnp.floor(rank * (1.0 / zs))
        owner = rank - zs * turn
        owned = (owner == iota((n, zs), 1).astype(F32)).astype(BF)
        place = jnp.sum(nn(lower, owned) * owned.astype(F32), axis=1, keepdims=True)
        self.at = owner * m + place
        self.at_row = to_row(self.at)
        mine = iota((m, n), 0).astype(F32) + lax.convert_element_type(z * m, F32) == self.at_row
        self.mine = mine.astype(BF)
        self.mine_mask = mine
        self.slot = self.own_col(to_row(chosen * per + turn))
        self.own_hot = nn(self.mine, self.hot).astype(BF)
        self.slots = EXP * per
        self.n, self.m = n, m

    def own_col(self, row):
        return jnp.sum(jnp.where(self.mine_mask, row, 0.0), axis=1, keepdims=True)

    def own(self, rows):
        return nn(self.mine, rows)

    def sort(self, rows):
        return nn((iota((self.n, self.n), 0).astype(F32) == self.at_row).astype(BF), rows).astype(BF)

    def unsort(self, rows):
        return nn((iota((self.n, self.n), 1).astype(F32) == self.at).astype(BF), rows).astype(BF)

    def fill(self, rows, s_ref):
        place = (iota((self.slots, self.m), 0).astype(F32) == to_row(self.slot)).astype(BF)
        filled = nn(place, rows).astype(BF)
        fs, _, _, r, h = s_ref.shape
        for f in range(fs):
            for c in range(2):
                at = (f * 2 + c) * r
                for y in range(2):
                    s_ref[f, y, c] = filled[at : at + r, y * h : (y + 1) * h]

    def collect(self, rb_ref):
        parts = []
        for f in range(rb_ref.shape[0] // 4):
            for c in range(2):
                parts.append(jnp.concatenate([rb_ref[f * 4 + c], rb_ref[f * 4 + 2 + c]], axis=1))
        rows = jnp.concatenate(parts, axis=0)
        place = (iota((self.m, self.slots), 1).astype(F32) == self.slot).astype(BF)
        return nn(place, rows)


def z_peers(zs):
    f, i, z = lax.axis_index("fsdp"), lax.axis_index("ctx"), lax.axis_index("tp")
    return [(f, i, lax.rem(z + s, zs)) for s in range(1, zs)]


def greet(peers):
    barrier = pltpu.get_barrier_semaphore()
    for peer in peers:
        pl.semaphore_signal(barrier, inc=1, device_id=peer, device_id_type=MESH)
    pl.semaphore_wait(barrier, len(peers))


def remote(src, dst, send, recv, peer):
    return pltpu.make_async_remote_copy(
        src_ref=src, dst_ref=dst, send_sem=send, recv_sem=recv, device_id=peer, device_id_type=MESH
    )


def scatter_z(zs, x_ref, parts, send, recv):
    z = lax.axis_index("tp")
    n = x_ref.shape[0] // zs
    copies = []
    for s, peer in enumerate(z_peers(zs)):
        to = lax.rem(z + s + 1, zs)
        cp = remote(x_ref.at[span(to, n)], parts.at[s], send.at[s], recv.at[s], peer)
        cp.start()
        copies.append(cp)
    total = x_ref[span(z, n), :].astype(F32)
    for s, cp in enumerate(copies):
        cp.wait_recv()
        total = total + parts[s].astype(F32)
    return total, copies


def gather_z(zs, x_ref, n, send, recv):
    z = lax.axis_index("tp")
    copies = []
    for s, peer in enumerate(z_peers(zs)):
        cp = remote(x_ref.at[span(z, n)], x_ref.at[span(z, n)], send.at[s], recv.at[s], peer)
        cp.start()
        copies.append(cp)
    return copies


def span(at, n):
    return pl.ds(pl.multiple_of(at * n, n), n)


def group_peers(fs):
    f, i, z = lax.axis_index("fsdp"), lax.axis_index("ctx"), lax.axis_index("tp")
    y, c = lax.div(i, 2), lax.rem(i, 2)
    out = []
    for df in range(fs):
        for dy in range(2):
            for dc in range(2):
                if df or dy or dc:
                    fp = lax.rem(f + df, fs)
                    yp = y if dy == 0 else 1 - y
                    cp = c if dc == 0 else 1 - c
                    out.append((fp, yp, cp, (fp, yp * 2 + cp, z)))
    return out


def attend(mine, prefix, offsets, qt_ref, kv_ref, valid_ref, row0, pt_ref):
    k, n = qt_ref.shape
    query = iota((n, n), 1) + mine * n
    allowed = []
    for j in range(4):
        key = iota((n, n), 0) + offsets[j] * n
        col = to_col(valid_ref[pl.ds(row0 + offsets[j], 1), :])
        allowed.append(((key <= query) | (key < prefix)) & ((col > 0.5) | (key == query)))
    outs = []
    for h in range(k // HD):
        lo = h * HD
        qt = qt_ref[lo : lo + HD, :]
        scores = [
            jnp.where(allowed[j], nn(kv_ref[j, :, lo : lo + HD], qt) * (1.0 / math.sqrt(HD)), -1e30)
            for j in range(4)
        ]
        top = jnp.max(scores[0], axis=0, keepdims=True)
        for j in range(1, 4):
            top = jnp.maximum(top, jnp.max(scores[j], axis=0, keepdims=True))
        exps = [jnp.exp(s - top) for s in scores]
        share = 1.0 / sum(jnp.sum(e, axis=0, keepdims=True) for e in exps)
        acc = jnp.zeros((HD, n), F32)
        for j in range(4):
            w = (exps[j] * share).astype(BF)
            pt_ref[h, j] = w
            acc = acc + tn(kv_ref[j, :, k + lo : k + lo + HD], w)
        outs.append(acc)
    return jnp.transpose(jnp.concatenate(outs, axis=0)).astype(BF)


def attend_back(gct, qt_ref, kv_ref, pt_ref, near_ref, away_ref):
    k, n = qt_ref.shape
    scale = 1.0 / math.sqrt(HD)
    dqs = []
    for h in range(k // HD):
        lo = h * HD
        dot_ = gct[lo : lo + HD, :]
        qt = qt_ref[lo : lo + HD, :]
        ws = [pt_ref[h, j] for j in range(4)]
        dps = [nn(kv_ref[j, :, k + lo : k + lo + HD], dot_) for j in range(4)]
        mean = sum(jnp.sum(ws[j].astype(F32) * dps[j], axis=0, keepdims=True) for j in range(4))
        dq = jnp.zeros((HD, n), F32)
        for j in range(4):
            ds = (ws[j].astype(F32) * (dps[j] - mean)).astype(BF)
            dq = dq + tn(kv_ref[j, :, lo : lo + HD], ds)
            target = near_ref if j < 2 else away_ref
            target[j % 2, :, lo : lo + HD] = nt(ds, qt) * scale
            target[j % 2, :, k + lo : k + lo + HD] = nt(ws[j], dot_)
        dqs.append(dq * scale)
    return jnp.transpose(jnp.concatenate(dqs, axis=0)).astype(BF)


def expert_grads_body(c_ref, *refs):
    ins, outs = refs[:8], refs[8:]
    c = c_ref[0]
    for out_ref, at in zip(outs, (0, 4)):
        q = out_ref.shape[2]
        for core, (left_ref, right_ref) in ((c, ins[at : at + 2]), (1 - c, ins[at + 2 : at + 4])):
            for e in range(left_ref.shape[0]):
                left = jnp.where(c == 0, left_ref[e, :, :q], left_ref[e, :, q:])
                out_ref[core, e] = tn(left, right_ref[e])


def expert_grads(c, *pairs):
    half, n, dh = pairs[0].shape
    units = pairs[1].shape[2]
    step = 2 if half % 2 == 0 else 1
    block = lambda e, c_ref: (e, 0, 0)
    out = sds((2, half, dh // 2, units), F32)
    up, down = pl.pallas_call(
        expert_grads_body,
        grid_spec=pltpu.PrefetchScalarGridSpec(
            num_scalar_prefetch=1,
            grid=(half // step,),
            in_specs=[pl.BlockSpec((step, n, dh), block), pl.BlockSpec((step, n, units), block)] * 4,
            out_specs=[pl.BlockSpec((2, step, dh // 2, units), lambda e, c_ref: (0, e, 0, 0))] * 2,
        ),
        out_shape=[out, out],
        compiler_params=params(),
        name="expert_grads",
    )(c.reshape(1), *pairs)
    return up.reshape(2 * half, dh // 2, units), down.reshape(2 * half, dh // 2, units)


def whereabouts():
    f, i, z = lax.axis_index("fsdp"), lax.axis_index("ctx"), lax.axis_index("tp")
    return f, i, z, lax.div(i, 2), lax.rem(i, 2)


def head_body(fs, zs, gather, *refs):
    if gather:
        (prefix_ref, tok_ref, mix_ref, ow_ref, small_ref, as_ref, up_ref, dn_ref,
         w3_ref, wo_ref, t_ref, valid_ref, upx_ref, dnx_ref,
         normed_ref, qt_ref, kv_ref, pt_ref, ctx_ref, res_ref, mi_ref, gate_ref, s_ref,
         small_all, branch, parts, send, recv, wx_s, wx_r, kv_s, kv_r, p_s, p_r, q_s, q_r) = refs
    else:
        (prefix_ref, tok_ref, w3_ref, wo_ref, t_ref, valid_ref, as_ref, up_ref, dn_ref,
         upx_ref, dnx_ref,
         normed_ref, qt_ref, kv_ref, pt_ref, ctx_ref, res_ref, mi_ref, gate_ref, s_ref,
         branch, parts, send, recv, wx_s, wx_r, kv_s, kv_r) = refs
    f, i, z, y, c = whereabouts()
    me = f * 4 + i
    half = upx_ref.shape[0]
    k = qt_ref.shape[0]
    sibling = (f, y * 2 + 1 - c, z)
    across = (f, (1 - y) * 2 + c, z)
    same = []
    for df in range(fs):
        for dy in range(2):
            if df or dy:
                fp = lax.rem(f + df, fs)
                yp = y if dy == 0 else 1 - y
                same.append(((fp, yp * 2 + c, z), df, dy))
    greeted = same if gather else [s for s in same if s[1] == 0]
    greet([s[0] for s in greeted] + [sibling] + z_peers(zs))

    give = pl.ds((1 - c) * half, half)
    swaps = [
        remote(up_ref.at[give], upx_ref, wx_s.at[0], wx_r.at[0], sibling),
        remote(dn_ref.at[give], dnx_ref, wx_s.at[1], wx_r.at[1], sibling),
    ]
    waits = []
    xhat, _ = norm_parts(tok_ref[...].astype(F32))
    if gather:
        rows = mix_ref.shape[1]

        def places(at):
            return [w3_ref.at[:, span(at, rows), :], wo_ref.at[span(at, rows), :], small_all.at[at]]

        w3_ref[:, span(me, rows), :] = mix_ref[...]
        wo_ref[span(me, rows), :] = jnp.transpose(ow_ref[...].astype(F32)).astype(BF)
        small_all[me] = small_ref[...]
        sends, relays = [], []
        for n_, (peer, df, dy) in enumerate(same):
            for m, ref in enumerate(places(me)):
                cp = remote(ref, ref, p_s.at[n_, m], p_r.at[n_, m], peer)
                cp.start()
                sends.append(cp)
        for m, ref in enumerate(places(me)):
            cp = remote(ref, ref, q_s.at[0, m], q_r.at[0, m], sibling)
            cp.start()
            relays.append(cp)
        for n_, (peer, df, dy) in enumerate(same):
            fp = lax.rem(f - df + fs, fs)
            yp = y if dy == 0 else 1 - y
            for m, ref in enumerate(places(fp * 4 + yp * 2 + c)):
                sends[n_ * 3 + m].wait_recv()
                cp = remote(ref, ref, q_s.at[n_ + 1, m], q_r.at[n_ + 1, m], sibling)
                cp.start()
                relays.append(cp)
        for cp in relays:
            cp.wait_recv()
        sources = fs * 4
        t_ref[...] = jnp.concatenate([small_all[s, :, :rows] for s in range(sources)], axis=1)
        for s in range(sources):
            valid_ref[s : s + 1, :] = small_all[s, 34:35, :].astype(F32)
        waits += sends + relays
    for cp in swaps:
        cp.start()
    normed = (xhat * t_ref[32:33, :].astype(F32)).astype(BF)
    normed_ref[...] = normed
    kv_ref[0, :, :k] = nn(normed, w3_ref[1]).astype(BF)
    kv_ref[0, :, k:] = nn(normed, w3_ref[2]).astype(BF)
    far = remote(kv_ref.at[0], kv_ref.at[1], kv_s.at[0], kv_r.at[0], across)
    sib = remote(kv_ref.at[0], kv_ref.at[2], kv_s.at[1], kv_r.at[1], sibling)
    far.start()
    sib.start()
    qt_ref[...] = jnp.transpose(nn(normed, w3_ref[0])).astype(BF)
    far.wait_recv()
    relay = remote(kv_ref.at[1], kv_ref.at[3], kv_s.at[2], kv_r.at[2], sibling)
    relay.start()
    sib.wait_recv()
    relay.wait_recv()
    offsets = [i, (1 - y) * 2 + c, y * 2 + 1 - c, (1 - y) * 2 + 1 - c]
    ctx = attend(i, prefix_ref[0], offsets, qt_ref, kv_ref, valid_ref, f * 4, pt_ref)
    ctx_ref[...] = ctx
    route = Route(as_ref[...], zs, z)
    branch[...] = route.sort(nt(ctx, wo_ref[...]).astype(BF))
    total, sums = scatter_z(zs, branch, parts, send, recv)
    residual = route.own(tok_ref[...]) + total
    res_ref[...] = residual
    xhat, _ = norm_parts(residual)
    mixed_in = (xhat * t_ref[33:34, :].astype(F32)).astype(BF)
    mi_ref[...] = mixed_in
    logit = jnp.sum(mixed_in.astype(F32) * nn(route.own_hot, t_ref[0:EXP, :]), axis=-1, keepdims=True)
    gate_ref[...] = jax.nn.sigmoid(logit)
    route.fill(mixed_in, s_ref)
    for cp in swaps:
        cp.wait_recv()
    for cp in waits + swaps + sums + [far, sib, relay]:
        cp.wait_send()


def log2(v):
    return v.bit_length() - 1


def reorder(sources, half, per, inverse):
    n = sources * half * per
    i, o = iota((n, n), 1), iota((n, n), 0)
    if inverse:
        i, o = o, i
    ls, lh, lp = log2(sources), log2(half), log2(per)
    slot = o & (per - 1)
    source = shifted(o, lp) & (sources - 1)
    expert = shifted(o, lp + ls)
    return (i == source * (half * per) + expert * per + slot).astype(BF)


def expert_pass(back, fs, zs, s_ref, w_in, w_out, x_ref, h_ref, gp_ref, rb_ref, buffers, sems, waiting):
    rq, xg, ps, pr, res, rin, ret = buffers
    d_s, d_r, a_s, a_r, x_s, x_r, r_s, r_r, b_s, b_r, own_sem = sems
    f, i, z, y, c = whereabouts()
    me = f * 4 + i
    sources, r, dh = rq.shape
    half, n, _ = x_ref.shape
    per = r // half
    m = sources * per
    across = (f, (1 - y) * 2 + c, z)
    peers = group_peers(fs)
    zp = z_peers(zs)

    keep = pltpu.make_async_copy(s_ref.at[f, y, c], rq.at[me], own_sem.at[0])
    keep.start()
    copies = []
    for k, (fp, yp, cp_, peer) in enumerate(peers):
        cp = remote(s_ref.at[fp, yp, cp_], rq.at[me], d_s.at[k], d_r.at[k], peer)
        cp.start()
        copies.append(cp)
    for cp in waiting:
        cp.wait()
    keep.wait()
    for cp in copies:
        cp.wait_recv()
    rows = rq[...].reshape(sources * r, dh)
    xg[...] = nn(reorder(sources, half, per, False), rows).astype(BF).reshape(half, m, dh)

    def share(e, s):
        return remote(xg.at[e], x_ref.at[e, span(z, m), :], a_s.at[e, s], a_r.at[e, s], zp[s])

    def cross(e):
        return remote(ps.at[e], pr.at[e], x_s.at[e], x_r.at[e], across)

    def scatter(e, s):
        to = lax.rem(z + s + 1, zs)
        return remote(res.at[e, span(to, m), :], rin.at[e, s], r_s.at[e, s], r_r.at[e, s], zp[s])

    @pl.loop(0, half)
    def _(e):
        for s in range(zs - 1):
            share(e, s).start()
        x_ref[e, span(z, m), :] = xg[e]

    @pl.loop(0, half)
    def _(e):
        for s in range(zs - 1):
            share(e, s).wait_recv()
        ps[e] = nn(x_ref[e], w_in[e]).astype(BF)
        cross(e).start()

    @pl.loop(0, half)
    def _(e):
        cross(e).wait_recv()
        total = ps[e].astype(F32) + pr[e].astype(F32)
        if back:
            h_ref[e] = (total * gp_ref[e].astype(F32)).astype(BF)
        else:
            phi = 0.5 * (1.0 + lax.erf(total * math.sqrt(0.5)))
            h_ref[e] = (total * phi).astype(BF)
            bell = jnp.exp(-0.5 * total * total) * (1.0 / math.sqrt(2.0 * math.pi))
            gp_ref[e] = (phi + total * bell).astype(BF)
        res[e] = nt(h_ref[e], w_out[e]).astype(BF)
        for s in range(zs - 1):
            scatter(e, s).start()

    @pl.loop(0, half)
    def _(e):
        total = res[e, span(z, m), :].astype(F32)
        for s in range(zs - 1):
            scatter(e, s).wait_recv()
            total = total + rin[e, s].astype(F32)
            share(e, s).wait_send()
        xg[e] = total.astype(BF)

    rows = nn(reorder(sources, half, per, True), xg[...].reshape(half * m, dh))
    ret[...] = rows.astype(BF).reshape(sources, r, dh)
    keep = pltpu.make_async_copy(ret.at[me], rb_ref.at[me], own_sem.at[1])
    keep.start()
    for k, (fp, yp, cp_, peer) in enumerate(peers):
        cp = remote(ret.at[fp * 4 + yp * 2 + cp_], rb_ref.at[me], b_s.at[k], b_r.at[k], peer)
        cp.start()
        copies.append(cp)
    keep.wait()
    for cp in copies[len(peers) :]:
        cp.wait_recv()
    for cp in copies:
        cp.wait_send()

    @pl.loop(0, half)
    def _(e):
        cross(e).wait_send()
        for s in range(zs - 1):
            scatter(e, s).wait_send()


def pass_sems(fs, zs, half):
    dma = pltpu.SemaphoreType.DMA
    peers = 4 * fs - 1
    out = []
    for shape in ((peers,), (half, zs - 1), (half,), (half, zs - 1), (peers,)):
        out += [dma(shape)] * 2
    return out + [dma((2,))]


def middle_body(fs, zs, s_ref, res_ref, gate_ref, as_ref, valid_ref, tea_ref, cot_ref, up_ref, upx_ref, dn_ref, dnx_ref,
                x_ref, act_ref, gx_ref, gh_ref, out_ref, gm_ref, gl_ref, gb_ref, stat_ref, *refs):
    wu, wd, gp, gs, rb, rb_back, sorted_out, stat_in, stat_all = refs[:9]
    buffers = refs[9:16]
    sems = refs[16:27], refs[27:38]
    wsem, o_s, o_r, t_s, t_r, u_s, u_r = refs[38:]
    f, i, z, y, c = whereabouts()
    me = f * 4 + i
    half, width = wu.shape[0], up_ref.shape[1]
    group = group_peers(fs)
    own = pl.ds(pl.multiple_of(c * width, 64), width)
    other = pl.ds(pl.multiple_of((1 - c) * width, 64), width)
    mine = pl.ds(c * half, half)
    loads = [
        pltpu.make_async_copy(up_ref.at[mine], wu.at[:, own, :], wsem.at[0]),
        pltpu.make_async_copy(upx_ref, wu.at[:, other, :], wsem.at[1]),
        pltpu.make_async_copy(dn_ref.at[mine], wd.at[:, own, :], wsem.at[2]),
        pltpu.make_async_copy(dnx_ref, wd.at[:, other, :], wsem.at[3]),
    ]
    for cp in loads:
        cp.start()
    greet([p[3] for p in group] + z_peers(zs))
    expert_pass(False, fs, zs, s_ref, wu, wd, x_ref, act_ref, gp, rb, buffers, sems[0], loads)

    route = Route(as_ref[...], zs, z)
    returned = route.collect(rb)
    gate = gate_ref[...]
    m, d = returned.shape
    mixed = res_ref[...] + gate * returned
    diff = mixed - route.own(tea_ref[...])
    valid = route.own_col(valid_ref[pl.ds(me, 1), :])
    scale = 1.0 / (jnp.sum(valid_ref[...]) * d)
    weighted = valid * diff
    grad = route.own(cot_ref[...]) + 2.0 * weighted * scale
    route.fill((gate * grad).astype(BF), gs)
    sorted_out[span(z, m), :] = mixed.astype(BF)
    hot = route.own_hot.astype(F32)
    stat_ref[...] = jnp.zeros_like(stat_ref)
    stat_ref[0:1, 0:EXP] = jnp.sum(hot, axis=0, keepdims=True)
    stat_ref[1:2, 0:EXP] = jnp.sum(hot * gate, axis=0, keepdims=True)
    stat_ref[2:3, :] = jnp.broadcast_to(jnp.sum(weighted * diff * scale), (1, 128))
    stats = []
    for s, peer in enumerate(z_peers(zs)):
        cp = remote(stat_ref, stat_in.at[s], t_s.at[s], t_r.at[s], peer)
        cp.start()
        stats.append(cp)
    outs = gather_z(zs, sorted_out, m, o_s, o_r)
    gm_ref[...] = grad
    grad_gate = jnp.sum(grad * returned, axis=-1, keepdims=True)
    gl_ref[...] = grad_gate * gate * (1.0 - gate)
    total = stat_ref[...]
    for s, cp in enumerate(stats):
        cp.wait_recv()
        total = total + stat_in[s]
    stat_all[me] = total
    for k, (_, _, _, peer) in enumerate(group):
        cp = remote(stat_all.at[me], stat_all.at[me], u_s.at[k], u_r.at[k], peer)
        cp.start()
        stats.append(cp)

    expert_pass(True, fs, zs, gs, wd, wu, gx_ref, gh_ref, gp, rb_back, buffers, sems[1], [])
    gb_ref[...] = route.collect(rb_back)
    for cp in outs:
        cp.wait_recv()
    out_ref[...] = route.unsort(sorted_out[...])
    for cp in stats[zs - 1 :]:
        cp.wait_recv()
    for cp in outs + stats:
        cp.wait_send()
    total = stat_all[0]
    for k in range(1, fs * 4):
        total = total + stat_all[k]
    stat_ref[...] = total


def back_body(fs, zs, rows, gb_ref, res_ref, mi_ref, gm_ref, gl_ref, as_ref, tok_ref, t_ref, w3_ref, wo_ref,
              normed_ref, qt_ref, kv_ref, pt_ref, ctx_ref,
              tg_ref, mix_ref, og_ref, sm_ref,
              sorted_gb, near, away, away_in, far_out, far_in, gn, parts, sorted_tg, dense, dense_in, give, taken, sm_in,
              a_s, a_r, s_s, s_r, t_s, t_r, v_s, v_r, k_s, k_r, g_s, g_r):
    f, i, z, y, c = whereabouts()
    sibling = (f, y * 2 + 1 - c, z)
    across = (f, (1 - y) * 2 + c, z)
    same = []
    for df in range(fs):
        for dy in range(2):
            if df or dy:
                fp = lax.rem(f + df, fs)
                yp = y if dy == 0 else 1 - y
                same.append((fp, yp, (fp, yp * 2 + c, z)))
    greet(z_peers(zs) + [sibling] + [s[2] for s in same])
    route = Route(as_ref[...], zs, z)
    k = qt_ref.shape[0]
    gl = gl_ref[...]
    grad_in = gb_ref[...] + gl * nn(route.own_hot, t_ref[0:EXP, :])
    m, d = grad_in.shape
    xhat, inv = norm_parts(res_ref[...])
    grad = gm_ref[...] + norm_back(grad_in, xhat, inv, t_ref[33:34, :].astype(F32))
    sorted_gb[span(z, m), :] = grad.astype(BF)
    gathers = gather_z(zs, sorted_gb, m, a_s, a_r)
    g2 = jnp.sum(grad_in * xhat, axis=0, keepdims=True)
    cg = _dot(route.own_hot.astype(F32) * gl, mi_ref[...].astype(F32), 0, 0, TOP)
    all_tok = norm_parts(tok_ref[...].astype(F32))[0]
    own_tok, own_inv = norm_parts(route.own(tok_ref[...]))
    for cp in gathers:
        cp.wait_recv()
    gb = route.unsort(sorted_gb[...])
    gct = jnp.transpose(nn(gb, wo_ref[...])).astype(BF)
    dq = attend_back(gct, qt_ref, kv_ref, pt_ref, near, away)
    swap = remote(away, away_in, k_s.at[0], k_r.at[0], sibling)
    swap.start()
    og = tn(gb, ctx_ref[...])
    swap.wait_recv()
    far_out[...] = (near[1] + away_in[1]).astype(BF)
    cross = remote(far_out, far_in, k_s.at[1], k_r.at[1], across)
    cross.start()
    normed = normed_ref[...]
    mg = [tn(normed, dq), None, None]
    gq = nt(dq, w3_ref[0])
    cross.wait_recv()
    kvg = (near[0] + away_in[0] + far_in[...].astype(F32)).astype(BF)
    partial_normed = gq + nt(kvg[:, :k], w3_ref[1]) + nt(kvg[:, k:], w3_ref[2])
    gn[...] = route.sort(partial_normed.astype(BF))
    n = gn.shape[0]
    scat = []
    for s, peer in enumerate(z_peers(zs)):
        cp = remote(gn.at[span(lax.rem(z + s + 1, zs), m)], parts.at[s], s_s.at[s], s_r.at[s], peer)
        cp.start()
        scat.append(cp)
    mg[1] = tn(normed, kvg[:, :k])
    mg[2] = tn(normed, kvg[:, k:])
    g1 = jnp.sum(partial_normed * all_tok, axis=0, keepdims=True)
    last = dense.shape[3] - TAB
    small = jnp.concatenate([cg, g1, g2, jnp.zeros((TAB - EXP - 2, d), F32)], axis=0)
    for s in range(4 * fs):
        at = (s // 4, s % 4 // 2, s % 2)
        lo = s * rows
        for j in range(3):
            dense[at[0], at[1], at[2], 0:rows, j * k : (j + 1) * k] = mg[j][lo : lo + rows, :]
        dense[at[0], at[1], at[2], 0:rows, 3 * k : 4 * k] = og[lo : lo + rows, :]
        dense[at[0], at[1], at[2], last : last + TAB, 0:rows] = small[:, lo : lo + rows]
    pair = remote(dense.at[:, :, 1 - c], dense_in, k_s.at[2], k_r.at[2], sibling)
    pair.start()
    pair.wait_recv()
    shares = []
    for s, (fp, yp, peer) in enumerate(same):
        give[s] = (dense[fp, yp, c] + dense_in[fp, yp]).astype(BF)
        cp = remote(give.at[s], taken.at[s], g_s.at[s], g_r.at[s], peer)
        cp.start()
        shares.append(cp)
    total = gn[span(z, m), :].astype(F32)
    for s, cp in enumerate(scat):
        cp.wait_recv()
        total = total + parts[s].astype(F32)
    tg = grad + norm_back(total, own_tok, own_inv, t_ref[32:33, :].astype(F32))
    sorted_tg[span(z, m), :] = tg.astype(BF)
    ends = gather_z(zs, sorted_tg, m, t_s, t_r)
    kept = dense[f, y, c] + dense_in[f, y]
    for s, cp in enumerate(shares):
        cp.wait_recv()
        kept = kept + taken[s].astype(F32)
    sm_ref[...] = kept[last:, :128]
    smalls = []
    for s, peer in enumerate(z_peers(zs)):
        cp = remote(sm_ref, sm_in.at[s], v_s.at[s], v_r.at[s], peer)
        cp.start()
        smalls.append(cp)
    for j in range(3):
        mix_ref[j] = kept[:rows, j * k : (j + 1) * k]
    og_ref[...] = jnp.transpose(kept[:rows, 3 * k :])
    for cp in ends:
        cp.wait_recv()
    tg_ref[...] = route.unsort(sorted_tg[...])
    for cp in smalls:
        cp.wait()
    total = sm_ref[...]
    for s in range(zs - 1):
        total = total + sm_in[s]
    sm_ref[...] = total
    for cp in gathers + [swap, cross, pair] + scat + shares + ends:
        cp.wait_send()


def per_device(tokens, mixing_weight, output_weight, first_gain, second_gain, centroids, expert_up,
               expert_down, prefix_length, assignment, validity, teacher, cotangent):
    fs, zs = lax.axis_size("fsdp"), lax.axis_size("tp")
    f, i, z = lax.axis_index("fsdp"), lax.axis_index("ctx"), lax.axis_index("tp")
    c = lax.rem(i, 2)
    n, d = tokens.shape[1], tokens.shape[2]
    rows, k = mixing_weight.shape[0], mixing_weight.shape[2]
    local_experts, width, units = expert_up.shape
    half = local_experts // 2
    experts = centroids.shape[0]
    sources = fs * 4
    heads = k // HD
    dma = pltpu.SemaphoreType.DMA
    smem = pl.BlockSpec(memory_space=pltpu.SMEM)
    anyspec = pl.BlockSpec(memory_space=ANY)
    core_pairs = [(0, 1), (1, 0), (2, 3), (3, 2)]

    def core_swap(v):
        return lax.ppermute(v, "ctx", core_pairs)

    down = expert_down.transpose(0, 2, 1)
    mixing = mixing_weight.transpose(1, 0, 2)
    tok = tokens[0]
    chosen = assignment.reshape(1, n)
    small = jnp.concatenate(
        [
            jnp.pad(jnp.concatenate([centroids, first_gain[None], second_gain[None]]), ((0, 0), (0, n - rows))),
            validity.astype(BF),
            jnp.zeros((TAB - experts - 3, n), BF),
        ]
    )
    swapped = (half, width, units)
    per = CAP // zs
    m = n // zs
    r = half * per
    row_shape = (fs, 2, 2, r, d // 2)
    weight_shapes = [sds((3, d, k), BF), sds((d, k), BF), sds((TAB, d), BF), sds((sources, n), F32)]
    swap_shapes = [sds(swapped, BF)] * 2
    token_shapes = [
        sds((n, d), BF), sds((k, n), BF), sds((4, n, 2 * k), BF), sds((heads, 4, n, n), BF), sds((n, k), BF),
        sds((m, d), F32), sds((m, d), BF), sds((m, 1), F32), sds(row_shape, BF),
    ]
    scattered = [VMEM((n, d), BF), VMEM((zs - 1, m, d), BF)]
    exchange = scattered + [dma((zs - 1,))] * 2 + [dma((2,))] * 2 + [dma((3,))] * 2
    gather = rows % 16 == 0
    if gather:
        head_in = (prefix_length, tok, mixing, output_weight, small, chosen, expert_up, down)
        out_shapes = weight_shapes + swap_shapes + token_shapes
        out_specs = [vspec()] * 4 + [anyspec] * 2 + [vspec()] * 9
        scratch = [VMEM((sources, TAB, n), BF)] + exchange + [dma((2 * fs - 1, 3))] * 2 + [dma((2 * fs, 3))] * 2
    else:
        everyone = ("fsdp", "ctx")
        w3 = lax.all_gather(mixing, everyone, axis=1, tiled=True)
        wo = lax.all_gather(output_weight, everyone, axis=1, tiled=True).T
        table = lax.all_gather(small, everyone, axis=0)
        valid_all = table[:, experts + 2, :].astype(F32)
        table = table[:, :, :rows].transpose(1, 0, 2).reshape(TAB, d)
        head_in = (prefix_length, tok, w3, wo, table, valid_all, chosen, expert_up, down)
        out_shapes = swap_shapes + token_shapes
        out_specs = [anyspec] * 2 + [vspec()] * 9
        scratch = exchange
    results = pl.pallas_call(
        partial(head_body, fs, zs, gather),
        out_shape=out_shapes,
        in_specs=[smem] + [vspec()] * (len(head_in) - 3) + [anyspec] * 2,
        out_specs=out_specs,
        scratch_shapes=scratch,
        compiler_params=params(1),
        name="head",
    )(*head_in)
    if gather:
        w3, wo, table, valid_all = results[:4]
        results = results[4:]
    up_x, dn_x, normed, qt, kv, pt, ctx, residual, mixed_in, gate, slots = results

    slots_in = sources * CAP
    dh = d // 2
    hidden = (half, slots_in, units)
    received = (half, slots_in, dh)
    x, act, gx, gh, activations, grad_mixed, grad_logit, grad_back, stats = pl.pallas_call(
        partial(middle_body, fs, zs),
        out_shape=[
            sds(received, BF), sds(hidden, BF), sds(received, BF), sds(hidden, BF), sds((n, d), BF),
            sds((m, d), F32), sds((m, 1), F32), sds((m, d), F32), sds((8, 128), F32),
        ],
        in_specs=[vspec()] * 7 + [anyspec] * 4,
        out_specs=[vspec()] * 9,
        scratch_shapes=[
            VMEM((half, dh, units), BF), VMEM((half, dh, units), BF), VMEM(hidden, BF), VMEM(row_shape, BF),
            VMEM((sources, r, dh), BF), VMEM((sources, r, dh), BF), VMEM((n, d), BF),
            VMEM((zs - 1, 8, 128), F32), VMEM((sources, 8, 128), F32),
            VMEM((sources, r, dh), BF), VMEM((half, sources * per, dh), BF), VMEM(hidden, BF), VMEM(hidden, BF),
            VMEM(received, BF), VMEM((half, zs - 1, sources * per, dh), BF), VMEM((sources, r, dh), BF),
        ]
        + pass_sems(fs, zs, half) * 2
        + [dma((4,))] + [dma((zs - 1,))] * 4 + [dma((sources - 1,))] * 2,
        compiler_params=params(2),
        name="middle",
    )(slots, residual, gate, chosen, valid_all, teacher[0], cotangent[0], expert_up, up_x, down, dn_x)
    x_x, act_x, gx_x, gh_x = core_swap(x), core_swap(act), core_swap(gx), core_swap(gh)
    all_tokens = float(n * sources)
    share = stats[0, :experts] / all_tokens - 1.0 / experts
    balance = experts * experts * jnp.sum(share * stats[1, :experts] / all_tokens)
    distill = stats[2, 0]

    piece = (rows + (-rows % 16) + TAB, 4 * k)
    others = 2 * fs - 1
    tokens_gradient, mix_part, out_part, small_part = pl.pallas_call(
        partial(back_body, fs, zs, rows),
        out_shape=[sds((n, d), BF), sds((3, rows, k), F32), sds((k, rows), F32), sds((TAB, 128), F32)],
        in_specs=[vspec()] * 15,
        out_specs=[vspec()] * 4,
        scratch_shapes=[
            VMEM((n, d), BF), VMEM((2, n, 2 * k), F32), VMEM((2, n, 2 * k), F32), VMEM((2, n, 2 * k), F32),
            VMEM((n, 2 * k), BF), VMEM((n, 2 * k), BF), VMEM((n, d), BF), VMEM((zs - 1, m, d), BF), VMEM((n, d), BF),
            VMEM((fs, 2, 2) + piece, F32), VMEM((fs, 2) + piece, F32),
            VMEM((others,) + piece, BF), VMEM((others,) + piece, BF), VMEM((zs - 1, TAB, 128), F32),
        ]
        + [dma((zs - 1,))] * 8 + [dma((3,))] * 2 + [dma((others,))] * 2,
        compiler_params=params(3),
        name="back",
    )(grad_back, residual, mixed_in, grad_mixed, grad_logit, chosen, tok, table, w3, wo, normed, qt, kv, pt, ctx)
    up_gradient, down_gradient = expert_grads(c, x, gh, x_x, gh_x, gx, act, gx_x, act_x)

    return (
        activations[None],
        tokens_gradient[None],
        mix_part.transpose(1, 0, 2),
        out_part,
        small_part[experts, :rows],
        small_part[experts + 1, :rows],
        small_part[:experts, :rows],
        up_gradient,
        down_gradient.transpose(0, 2, 1),
        balance,
        distill,
    )


def solution(mesh):
    in_specs = (
        P("fsdp", "ctx", None),
        P(("fsdp", "ctx"), None, "tp"),
        P("tp", ("fsdp", "ctx")),
        P(("fsdp", "ctx")),
        P(("fsdp", "ctx")),
        P(None, ("fsdp", "ctx")),
        P("fsdp", "ctx", "tp"),
        P("fsdp", "tp", "ctx"),
        P("fsdp"),
        P("fsdp", "ctx", None),
        P("fsdp", "ctx"),
        P("fsdp", "ctx", None),
        P("fsdp", "ctx", None),
    )
    out_specs = (
        P("fsdp", "ctx", None),
        P("fsdp", "ctx", None),
        P(("fsdp", "ctx"), None, "tp"),
        P("tp", ("fsdp", "ctx")),
        P(("fsdp", "ctx")),
        P(("fsdp", "ctx")),
        P(None, ("fsdp", "ctx")),
        P("fsdp", "ctx", "tp"),
        P("fsdp", "tp", "ctx"),
        P(),
        P(),
    )
    return jax.shard_map(
        per_device, mesh=mesh, in_specs=in_specs, out_specs=out_specs, check_vma=False
    )
```

time: 337 us -> 242 us (0.72)
  Pallas kernels: 277 us -> 226 us
  waiting for transfers between devices: 29 us -> 0.01 us
  starting transfers between devices: 17.4 us -> 1.09 us
    pallas_call x8 -> x3, Pallas kernels: 226 us -> 183 us  [the longest x1 123 us: per_device(): pl.pallas_call(partial(middle_body, fs, zs), out_shape=[sds(received, BF)...]
    ppermute x9 -> x0, waiting for transfers between devices: 29 us -> none  [the longest x6 17.4 us: z_shift(): return lax.ppermute(v, 'tp', [(a, (a + s) % zs) for a in range(zs)])]
    ppermute x9 -> x0, starting transfers between devices: 16 us -> none  [the longest x6 11.6 us: z_shift(): return lax.ppermute(v, 'tp', [(a, (a + s) % zs) for a in range(zs)])]
    pallas_call x1, Pallas kernels: 51.1 us -> 42.4 us  [per_device(): pl.pallas_call(partial(head_body, fs, zs, gather), out_shape=out_shapes,...]
  transfers between devices with their start and end apart: 13 -> 4, of which waited for: 8 -> 0; matrix products, arithmetic and copies ran while one was open for 1% -> 2% of each run, Pallas kernels for 45% -> 20%
where the time goes in v3:
time: 242 us
  Pallas kernels  226 us (93%)
  local copies, waits for them, and re-layouts  8.34 us (3%)
  other arithmetic  3.46 us (1%)
  between operations  3.15 us (1%)
    pallas_call x1, Pallas kernels, per_device(): pl.pallas_call(partial(middle_body, fs, zs), out_shape=[sds(received, BF)...  123 us
    pallas_call x1, Pallas kernels, per_device(): pl.pallas_call(partial(back_body, fs, zs, rows), out_shape=[sds((n, d), B...  49 us
    pallas_call x1, Pallas kernels, per_device(): pl.pallas_call(partial(head_body, fs, zs, gather), out_shape=out_shapes,...  42.4 us
    pallas_call x1, Pallas kernels, expert_grads(): pl.pallas_call(expert_grads_body, grid_spec=pltpu.PrefetchScalarGridSpec(...  11.6 us
  transfers between devices with their start and end apart: 4, of which 0 were waited for; matrix products, arithmetic and copies ran while one was open for 2% of the time, Pallas kernels for 20%

profile of v3, /device:TPU:0, one launch (start us, length us, event | category | flops | bytes accessed | tf_op | source)
XLA Modules:
  0.0 241.6 jit_solution(4376578935739995180)
XLA Ops:
  1.3 0.7 convert_element_type.5
  2.0 0.1 pad.7.clone
  2.1 0.7 fusion.4
  2.8 0.7 maximum_maximum_fusion.refs_4_
  3.5 42.4 %head.1 = (bf16[3,768,192]{2,1,0:T(8,128)(2,1)}, bf16[768,192]{1,0:T(8,128)(2,1)}, bf16[48,768]{1,0:T(8,128)(2,1)}, f32[8,256]{1,0:T(8,128)}, bf16[8,192,768]{2,...) custom-call(s32[1]{0:T(128)S(6)} %copy.28.refs_0_, ...), custom_call_target="tpu_custom_call" | custom-call | tf_op jit(solution)/shard_map/head/pallas_call | solution.py:767
  45.9 122.5 %middle.1 = (bf16[8,128,384]{2,1,0:T(8,128)(2,1)}, bf16[8,128,768]{2,1,0:T(8,128)(2,1)}, bf16[8,128,384]{2,1,0:T(8,128)(2,1)}, bf16[8,128,768]{2,1,0:T(8,128)(2,...) custom-call(bf16[2,2,2,32,384]{4,3,2,1,0:T(8,128)(2,1)} %get-tuple-e, ...), custom_call_target="tpu_custom_call" | custom-call | tf_op jit(solution)/shard_map/middle/pallas_call | solution.py:785
  168.4 0.2 collective-permute-start.1
  168.6 0.4 collective-permute-start.3
  169.0 0.1 collective-permute-start
  169.1 0.4 collective-permute-start.2
  169.5 1.2 slice.23
  170.7 49.0 %back.1 = (bf16[256,768]{1,0:T(8,128)(2,1)}, f32[3,96,192]{2,1,0:T(8,128)}, f32[192,96]{1,0:T(8,128)}, f32[48,128]{1,0:T(8,128)}) custom-call(f32[64,768]{1,0:T(8,128)} %get-tuple-element.48.gb_ref, f32[64,768]{1,0:T(8,128)} %get-tuple-element.42.res_ref, bf16[64,768]{1,0:T(8,128)(2,1)} %get-tuple-element.49.mi_ref, f32[64,768]{1,0:T(8,128)} %get-tuple-element.50.gm_ref, ...), custom_call_target="tpu_custom_call" | custom-call | tf_op jit(solution)/shard_map/back/pallas_call | solution.py:813
  219.7 1.3 slice.20
  221.0 1.4 multiply_reduce_fusion
  223.0 1.3 slice_bitcast_fusion
  224.3 0.0 collective-permute-done.refs_2_
  224.3 0.0 collective-permute-done.2.refs_6_
  224.3 0.0 collective-permute-done.1.refs_3_
  224.3 0.0 copy-start
  224.3 0.0 collective-permute-done.3.refs_7_
  224.3 0.0 copy-start.1
  224.3 1.2 copy-done
  225.5 0.4 copy-done.1
  226.0 0.0 copy-start.2
  226.0 0.0 copy-start.3
  226.0 0.0 copy-start.4
  226.0 0.0 copy-start.5
  226.0 11.6 %expert_grads.1 = (f32[2,8,192,768]{3,2,1,0:T(8,128)}, f32[2,8,192,768]{3,2,1,0:T(8,128)}) custom-call(s32[1]{0:T(128)} %bitcast.13.c_ref, bf16[8,128,384]{2,1,0:T(8,128)(2,1)} %get-tuple-element.64.refs_0_, bf16[8,128,768]{2,1,0:T(8,128)(2,1)} %get-tuple-element.65.refs_1_, bf16[8,128,384]{2,1,0:T(8,128)(2,1)} %collective-permute-done.refs_2_, ...), custom_call_target="tpu_custom_call" | custom-call | tf_op jit(solution)/shard_map/expert_grads/pallas_call | solution.py:278
  237.6 0.0 copy-done.2
  237.6 0.7 copy.29
  238.3 0.0 copy-done.3
  238.4 0.7 copy.30
  239.1 0.0 copy-done.4
  239.1 0.7 copy.31
  239.8 0.0 copy-done.5
  239.8 0.6 copy.32
  (1 shorter events, 0.0 us)
Async XLA Ops:
  168.4 55.9 %collective-permute-start.1 = (bf16[8,128,768]{2,1,0:T(8,128)(2,1)}, bf16[8,128,768]{2,1,0:T(8,128)(2,1)S(1)}, u32[]{:S(2)}, u32[]{:S(2)}) collective-permute-start(bf16[8,128,768]{2,1,0:T(8,128)(2,1)} %get-tuple-element.65.refs_1_), channel_id=1, source_target_pairs={{0,4},{4,0},{8,12},{12,8},{1,5},{5,1},{9,13},{13,9},{2,6},{6,2},{1... | collective-permute-start | bytes 4718600 | tf_op jit(solution)/shard_map/ppermute | solution.py:724
  168.6 55.7 %collective-permute-start.3 = (bf16[8,128,768]{2,1,0:T(8,128)(2,1)}, bf16[8,128,768]{2,1,0:T(8,128)(2,1)S(1)}, u32[]{:S(2)}, u32[]{:S(2)}) collective-permute-start(bf16[8,128,768]{2,1,0:T(8,128)(2,1)} %get-tuple-element.67.refs_5_), channel_id=1, source_target_pairs={{0,4},{4,0},{8,12},{12,8},{1,5},{5,1},{9,13},{13,9},{2,6},{6,2},{1... | collective-permute-start | bytes 4718600 | tf_op jit(solution)/shard_map/ppermute | solution.py:724
  169.0 55.3 %collective-permute-start = (bf16[8,128,384]{2,1,0:T(8,128)(2,1)}, bf16[8,128,384]{2,1,0:T(8,128)(2,1)}, u32[]{:S(2)}, u32[]{:S(2)}) collective-permute-start(bf16[8,128,384]{2,1,0:T(8,128)(2,1)} %get-tuple-element.64.refs_0_), channel_id=1, source_target_pairs={{0,4},{4,0},{8,12},{12,8},{1,5},{5,1},{9,13},{13,9},{2,6},{6,2},{1... | collective-permute-start | bytes 2359304 | tf_op jit(solution)/shard_map/ppermute | solution.py:724
  169.1 55.2 %collective-permute-start.2 = (bf16[8,128,384]{2,1,0:T(8,128)(2,1)}, bf16[8,128,384]{2,1,0:T(8,128)(2,1)}, u32[]{:S(2)}, u32[]{:S(2)}) collective-permute-start(bf16[8,128,384]{2,1,0:T(8,128)(2,1)} %get-tuple-element.66.refs_4_), channel_id=1, source_target_pairs={{0,4},{4,0},{8,12},{12,8},{1,5},{5,1},{9,13},{13,9},{2,6},{6,2},{1... | collective-permute-start | bytes 2359304 | tf_op jit(solution)/shard_map/ppermute | solution.py:724
  224.3 1.2 copy-start
  224.3 1.6 copy-start.1
  226.0 11.6 %copy-start.2 = (bf16[256,768]{1,0:T(8,128)(2,1)S(1)}, bf16[256,768]{1,0:T(8,128)(2,1)}, u32[]{:S(2)}) copy-start(bf16[256,768]{1,0:T(8,128)(2,1)} %get-tuple-element.47) | copy-start | bytes 1179652
  226.0 12.4 %copy-start.3 = (bf16[256,768]{1,0:T(8,128)(2,1)S(1)}, bf16[256,768]{1,0:T(8,128)(2,1)}, u32[]{:S(2)}) copy-start(bf16[256,768]{1,0:T(8,128)(2,1)} %get-tuple-element.60) | copy-start | bytes 1179652
  226.0 13.1 %copy-start.4 = (f32[3,96,192]{2,1,0:T(8,128)S(1)}, f32[3,96,192]{2,1,0:T(8,128)}, u32[]{:S(2)}) copy-start(f32[3,96,192]{2,1,0:T(8,128)} %get-tuple-element.61) | copy-start | bytes 663556
  226.0 13.9 %copy-start.5 = (f32[192,96]{1,0:T(8,128)S(1)}, f32[192,96]{1,0:T(8,128)}, u32[]{:S(2)}) copy-start(f32[192,96]{1,0:T(8,128)} %get-tuple-element.87) | copy-start | bytes 221188

commit v4 on v3

--- a/solution.py
+++ b/solution.py
@@ -84,12 +84,16 @@
     )
 
 
+def log2(v):
+    return v.bit_length() - 1
+
+
 def shifted(v, by):
     return lax.shift_right_logical(v, by)
 
 
 class Route:
-    def __init__(self, chosen, zs, z):
+    def __init__(self, chosen, zs, z, width=0):
         n = chosen.shape[1]
         m = n // zs
         per = CAP // zs
@@ -109,7 +113,7 @@
         self.slot = self.own_col(to_row(chosen * per + turn))
         self.own_hot = nn(self.mine, self.hot).astype(BF)
         self.slots = EXP * per
-        self.n, self.m = n, m
+        self.n, self.m, self.width = n, m, width
 
     def own_col(self, row):
         return jnp.sum(jnp.where(self.mine_mask, row, 0.0), axis=1, keepdims=True)
@@ -126,12 +130,15 @@
     def fill(self, rows, s_ref):
         place = (iota((self.slots, self.m), 0).astype(F32) == to_row(self.slot)).astype(BF)
         filled = nn(place, rows).astype(BF)
-        fs, _, _, r, h = s_ref.shape
+        fs, _, _, r, _ = s_ref.shape
+        h = self.width // 2
         for f in range(fs):
             for c in range(2):
                 at = (f * 2 + c) * r
                 for y in range(2):
-                    s_ref[f, y, c] = filled[at : at + r, y * h : (y + 1) * h]
+                    s_ref[f, y, c, :, :h] = filled[at : at + r, y * h : (y + 1) * h]
+                    if rows.shape[1] > self.width:
+                        s_ref[f, y, c, :, h:] = filled[at : at + r, self.width :]
 
     def collect(self, rb_ref):
         parts = []
@@ -297,14 +304,14 @@
 
 def head_body(fs, zs, gather, *refs):
     if gather:
-        (prefix_ref, tok_ref, mix_ref, ow_ref, small_ref, as_ref, up_ref, dn_ref,
+        (prefix_ref, tok_ref, mix_ref, ow_ref, small_ref, as_ref, tea_ref, cot_ref, up_ref, dn_ref,
          w3_ref, wo_ref, t_ref, valid_ref, upx_ref, dnx_ref,
-         normed_ref, qt_ref, kv_ref, pt_ref, ctx_ref, res_ref, mi_ref, gate_ref, s_ref,
+         normed_ref, qt_ref, kv_ref, pt_ref, ctx_ref, res_ref, mi_ref, gate_ref, s_ref, sg_ref,
          small_all, branch, parts, send, recv, wx_s, wx_r, kv_s, kv_r, p_s, p_r, q_s, q_r) = refs
     else:
-        (prefix_ref, tok_ref, w3_ref, wo_ref, t_ref, valid_ref, as_ref, up_ref, dn_ref,
+        (prefix_ref, tok_ref, w3_ref, wo_ref, t_ref, valid_ref, as_ref, tea_ref, cot_ref, up_ref, dn_ref,
          upx_ref, dnx_ref,
-         normed_ref, qt_ref, kv_ref, pt_ref, ctx_ref, res_ref, mi_ref, gate_ref, s_ref,
+         normed_ref, qt_ref, kv_ref, pt_ref, ctx_ref, res_ref, mi_ref, gate_ref, s_ref, sg_ref,
          branch, parts, send, recv, wx_s, wx_r, kv_s, kv_r) = refs
     f, i, z, y, c = whereabouts()
     me = f * 4 + i
@@ -382,8 +389,12 @@
     offsets = [i, (1 - y) * 2 + c, y * 2 + 1 - c, (1 - y) * 2 + 1 - c]
     ctx = attend(i, prefix_ref[0], offsets, qt_ref, kv_ref, valid_ref, f * 4, pt_ref)
     ctx_ref[...] = ctx
-    route = Route(as_ref[...], zs, z)
+    d = tok_ref.shape[1]
+    route = Route(as_ref[...], zs, z, d)
     branch[...] = route.sort(nt(ctx, wo_ref[...]).astype(BF))
+    teacher, cotangent = route.own(tea_ref[...]), route.own(cot_ref[...])
+    valid = route.own_col(valid_ref[pl.ds(me, 1), :])
+    weight = 2.0 * valid / (jnp.sum(valid_ref[...]) * d)
     total, sums = scatter_z(zs, branch, parts, send, recv)
     residual = route.own(tok_ref[...]) + total
     res_ref[...] = residual
@@ -391,16 +402,16 @@
     mixed_in = (xhat * t_ref[33:34, :].astype(F32)).astype(BF)
     mi_ref[...] = mixed_in
     logit = jnp.sum(mixed_in.astype(F32) * nn(route.own_hot, t_ref[0:EXP, :]), axis=-1, keepdims=True)
-    gate_ref[...] = jax.nn.sigmoid(logit)
+    gate = jax.nn.sigmoid(logit)
+    gate_ref[...] = gate
     route.fill(mixed_in, s_ref)
+    known = gate * (cotangent + weight * (residual - teacher))
+    slope = jnp.broadcast_to(gate * gate * weight, (known.shape[0], 128))
+    route.fill(jnp.concatenate([known, slope], axis=1).astype(BF), sg_ref)
     for cp in swaps:
         cp.wait_recv()
     for cp in waits + swaps + sums + [far, sib, relay]:
         cp.wait_send()
-
-
-def log2(v):
-    return v.bit_length() - 1
 
 
 def reorder(sources, half, per, inverse):
@@ -415,180 +426,261 @@
     return (i == source * (half * per) + expert * per + slot).astype(BF)
 
 
-def expert_pass(back, fs, zs, s_ref, w_in, w_out, x_ref, h_ref, gp_ref, rb_ref, buffers, sems, waiting):
-    rq, xg, ps, pr, res, rin, ret = buffers
-    d_s, d_r, a_s, a_r, x_s, x_r, r_s, r_r, b_s, b_r, own_sem = sems
+class Pass:
+    def __init__(self, back, zs, w_in, w_out, xg, x_ref, ps, pr, h_ref, gp_ref, res, rin, sems):
+        self.back, self.zs, self.w_in, self.w_out = back, zs, w_in, w_out
+        self.xg, self.x_ref, self.ps, self.pr = xg, x_ref, ps, pr
+        self.h_ref, self.gp_ref, self.res, self.rin = h_ref, gp_ref, res, rin
+        self.a_s, self.a_r, self.x_s, self.x_r, self.r_s, self.r_r = sems
+        f, i, z, y, c = whereabouts()
+        self.z = z
+        self.m = xg.shape[1]
+        self.across = (f, (1 - y) * 2 + c, z)
+        self.peers = z_peers(zs)
+
+    def share(self, e, s):
+        to = self.x_ref.at[e, span(self.z, self.m), :]
+        return remote(self.xg.at[e], to, self.a_s.at[e, s], self.a_r.at[e, s], self.peers[s])
+
+    def cross(self, e):
+        return remote(self.ps.at[e], self.pr.at[e], self.x_s.at[e], self.x_r.at[e], self.across)
+
+    def scatter(self, e, s):
+        to = lax.rem(self.z + s + 1, self.zs)
+        return remote(
+            self.res.at[e, span(to, self.m), :], self.rin.at[e, s], self.r_s.at[e, s], self.r_r.at[e, s], self.peers[s]
+        )
+
+    def spread(self, e, rows):
+        self.xg[e] = rows
+        for s in range(self.zs - 1):
+            self.share(e, s).start()
+        self.x_ref[e, span(self.z, self.m), :] = rows
+
+    def first(self, e):
+        for s in range(self.zs - 1):
+            self.share(e, s).wait_recv()
+        self.ps[e] = nn(self.x_ref[e], self.w_in[e]).astype(BF)
+
+    def second(self, e):
+        self.cross(e).wait_recv()
+        total = self.ps[e].astype(F32) + self.pr[e].astype(F32)
+        if self.back:
+            self.h_ref[e] = (total * self.gp_ref[e].astype(F32)).astype(BF)
+        else:
+            phi = 0.5 * (1.0 + lax.erf(total * math.sqrt(0.5)))
+            self.h_ref[e] = (total * phi).astype(BF)
+            bell = jnp.exp(-0.5 * total * total) * (1.0 / math.sqrt(2.0 * math.pi))
+            self.gp_ref[e] = (phi + total * bell).astype(BF)
+        self.res[e] = nt(self.h_ref[e], self.w_out[e]).astype(BF)
+        for s in range(self.zs - 1):
+            self.scatter(e, s).start()
+
+    def total(self, e):
+        total = self.res[e, span(self.z, self.m), :].astype(F32)
+        for s in range(self.zs - 1):
+            self.scatter(e, s).wait_recv()
+            total = total + self.rin[e, s].astype(F32)
+        return total.astype(BF)
+
+    def settle(self, e):
+        self.cross(e).wait_send()
+        for s in range(self.zs - 1):
+            self.share(e, s).wait_send()
+            self.scatter(e, s).wait_send()
+
+
+def give_back(fs, total, ret, rb_ref, own_sem, send, recv):
     f, i, z, y, c = whereabouts()
     me = f * 4 + i
-    sources, r, dh = rq.shape
-    half, n, _ = x_ref.shape
-    per = r // half
-    m = sources * per
-    across = (f, (1 - y) * 2 + c, z)
-    peers = group_peers(fs)
-    zp = z_peers(zs)
-
-    keep = pltpu.make_async_copy(s_ref.at[f, y, c], rq.at[me], own_sem.at[0])
+    sources, r, dh = ret.shape
+    half = total.shape[0]
+    rows = total[...].reshape(sources * r, dh)
+    ret[...] = nn(reorder(sources, half, r // half, True), rows).astype(BF).reshape(sources, r, dh)
+    keep = pltpu.make_async_copy(ret.at[me], rb_ref.at[me], own_sem)
     keep.start()
     copies = []
-    for k, (fp, yp, cp_, peer) in enumerate(peers):
-        cp = remote(s_ref.at[fp, yp, cp_], rq.at[me], d_s.at[k], d_r.at[k], peer)
+    for k, (fp, yp, cp_, peer) in enumerate(group_peers(fs)):
+        cp = remote(ret.at[fp * 4 + yp * 2 + cp_], rb_ref.at[me], send.at[k], recv.at[k], peer)
         cp.start()
         copies.append(cp)
-    for cp in waiting:
-        cp.wait()
+    return keep, copies
+
+
+def arrived(given):
+    keep, copies = given
     keep.wait()
     for cp in copies:
         cp.wait_recv()
-    rows = rq[...].reshape(sources * r, dh)
-    xg[...] = nn(reorder(sources, half, per, False), rows).astype(BF).reshape(half, m, dh)
-
-    def share(e, s):
-        return remote(xg.at[e], x_ref.at[e, span(z, m), :], a_s.at[e, s], a_r.at[e, s], zp[s])
-
-    def cross(e):
-        return remote(ps.at[e], pr.at[e], x_s.at[e], x_r.at[e], across)
-
-    def scatter(e, s):
-        to = lax.rem(z + s + 1, zs)
-        return remote(res.at[e, span(to, m), :], rin.at[e, s], r_s.at[e, s], r_r.at[e, s], zp[s])
-
-    @pl.loop(0, half)
-    def _(e):
-        for s in range(zs - 1):
-            share(e, s).start()
-        x_ref[e, span(z, m), :] = xg[e]
-
-    @pl.loop(0, half)
-    def _(e):
-        for s in range(zs - 1):
-            share(e, s).wait_recv()
-        ps[e] = nn(x_ref[e], w_in[e]).astype(BF)
-        cross(e).start()
-
-    @pl.loop(0, half)
-    def _(e):
-        cross(e).wait_recv()
-        total = ps[e].astype(F32) + pr[e].astype(F32)
-        if back:
-            h_ref[e] = (total * gp_ref[e].astype(F32)).astype(BF)
-        else:
-            phi = 0.5 * (1.0 + lax.erf(total * math.sqrt(0.5)))
-            h_ref[e] = (total * phi).astype(BF)
-            bell = jnp.exp(-0.5 * total * total) * (1.0 / math.sqrt(2.0 * math.pi))
-            gp_ref[e] = (phi + total * bell).astype(BF)
-        res[e] = nt(h_ref[e], w_out[e]).astype(BF)
-        for s in range(zs - 1):
-            scatter(e, s).start()
-
-    @pl.loop(0, half)
-    def _(e):
-        total = res[e, span(z, m), :].astype(F32)
-        for s in range(zs - 1):
-            scatter(e, s).wait_recv()
-            total = total + rin[e, s].astype(F32)
-            share(e, s).wait_send()
-        xg[e] = total.astype(BF)
-
-    rows = nn(reorder(sources, half, per, True), xg[...].reshape(half * m, dh))
-    ret[...] = rows.astype(BF).reshape(sources, r, dh)
-    keep = pltpu.make_async_copy(ret.at[me], rb_ref.at[me], own_sem.at[1])
-    keep.start()
-    for k, (fp, yp, cp_, peer) in enumerate(peers):
-        cp = remote(ret.at[fp * 4 + yp * 2 + cp_], rb_ref.at[me], b_s.at[k], b_r.at[k], peer)
-        cp.start()
-        copies.append(cp)
-    keep.wait()
-    for cp in copies[len(peers) :]:
-        cp.wait_recv()
-    for cp in copies:
-        cp.wait_send()
-
-    @pl.loop(0, half)
-    def _(e):
-        cross(e).wait_send()
-        for s in range(zs - 1):
-            scatter(e, s).wait_send()
-
-
-def pass_sems(fs, zs, half):
+
+
+def pass_sems(zs, half):
     dma = pltpu.SemaphoreType.DMA
-    peers = 4 * fs - 1
-    out = []
-    for shape in ((peers,), (half, zs - 1), (half,), (half, zs - 1), (peers,)):
-        out += [dma(shape)] * 2
-    return out + [dma((2,))]
-
-
-def middle_body(fs, zs, s_ref, res_ref, gate_ref, as_ref, valid_ref, tea_ref, cot_ref, up_ref, upx_ref, dn_ref, dnx_ref,
+    return [dma((half, zs - 1))] * 2 + [dma((half,))] * 2 + [dma((half, zs - 1))] * 2
+
+
+def middle_body(fs, zs, s_ref, sg_ref, res_ref, gate_ref, as_ref, valid_ref, tea_ref, cot_ref,
+                up_ref, upx_ref, dn_ref, dnx_ref,
                 x_ref, act_ref, gx_ref, gh_ref, out_ref, gm_ref, gl_ref, gb_ref, stat_ref, *refs):
-    wu, wd, gp, gs, rb, rb_back, sorted_out, stat_in, stat_all = refs[:9]
-    buffers = refs[9:16]
-    sems = refs[16:27], refs[27:38]
-    wsem, o_s, o_r, t_s, t_r, u_s, u_r = refs[38:]
+    (wu, wd, gp, rq, rg, grads, results, ret, ret_back, rb, rb_back, sorted_out, stat_in, stat_all,
+     xg, xg_back, ps, pr, pr_back, res, rin) = refs[:21]
+    sems = refs[21:27], refs[27:33]
+    wsem, d_s, d_r, g_s, g_r, b_s, b_r, c_s, c_r, o_s, o_r, t_s, t_r, u_s, u_r = refs[33:]
     f, i, z, y, c = whereabouts()
     me = f * 4 + i
     half, width = wu.shape[0], up_ref.shape[1]
+    sources, r, dh = rq.shape
+    m = sources * r // half
     group = group_peers(fs)
     own = pl.ds(pl.multiple_of(c * width, 64), width)
     other = pl.ds(pl.multiple_of((1 - c) * width, 64), width)
     mine = pl.ds(c * half, half)
     loads = [
-        pltpu.make_async_copy(up_ref.at[mine], wu.at[:, own, :], wsem.at[0]),
-        pltpu.make_async_copy(upx_ref, wu.at[:, other, :], wsem.at[1]),
-        pltpu.make_async_copy(dn_ref.at[mine], wd.at[:, own, :], wsem.at[2]),
-        pltpu.make_async_copy(dnx_ref, wd.at[:, other, :], wsem.at[3]),
+        pltpu.make_async_copy(s_ref.at[f, y, c], rq.at[me], wsem.at[0]),
+        pltpu.make_async_copy(sg_ref.at[f, y, c], rg.at[me], wsem.at[1]),
+        pltpu.make_async_copy(up_ref.at[mine], wu.at[:, own, :], wsem.at[2]),
+        pltpu.make_async_copy(upx_ref, wu.at[:, other, :], wsem.at[3]),
+        pltpu.make_async_copy(dn_ref.at[mine], wd.at[:, own, :], wsem.at[4]),
+        pltpu.make_async_copy(dnx_ref, wd.at[:, other, :], wsem.at[5]),
     ]
     for cp in loads:
         cp.start()
     greet([p[3] for p in group] + z_peers(zs))
-    expert_pass(False, fs, zs, s_ref, wu, wd, x_ref, act_ref, gp, rb, buffers, sems[0], loads)
-
+    sends, sends_g = [], []
+    for out, src, dst, send, recv in ((sends, s_ref, rq, d_s, d_r), (sends_g, sg_ref, rg, g_s, g_r)):
+        for k, (fp, yp, cp_, peer) in enumerate(group):
+            cp = remote(src.at[fp, yp, cp_], dst.at[me], send.at[k], recv.at[k], peer)
+            cp.start()
+            out.append(cp)
+    one = Pass(False, zs, wu, wd, xg, x_ref, ps, pr, act_ref, gp, res, rin, sems[0])
+    two = Pass(True, zs, wd, wu, xg_back, gx_ref, ps, pr_back, gh_ref, gp, res, rin, sems[1])
+    order = reorder(sources, half, r // half, False)
+
+    loads[0].wait()
+    for cp in sends:
+        cp.wait_recv()
+    rows = nn(order, rq[...].reshape(sources * r, dh)).astype(BF).reshape(half, m, dh)
+    for e in range(half):
+        one.spread(e, rows[e])
+    for cp in loads[2:]:
+        cp.wait()
+
+    @pl.loop(0, half)
+    def _(e):
+        one.first(e)
+        one.cross(e).start()
+
+    loads[1].wait()
+    for cp in sends_g:
+        cp.wait_recv()
+    grads[...] = nn(order, rg[...].reshape(sources * r, dh + 128)).astype(BF).reshape(half, m, dh + 128)
+
+    def turn(e):
+        result = one.total(e)
+        results[e] = result
+        scale = grads[e, :, dh:].astype(F32)[:, :1]
+        two.spread(e, (grads[e, :, :dh].astype(F32) + scale * result.astype(F32)).astype(BF))
+
+    lag, lag2 = 2, 4
+    start = max(half, lag2 + 1)
+    ahead = 3
+
+    def step(t, fixed=True):
+        if not fixed or t < half:
+            one.second(t)
+        if fixed and t - start >= 0 and t - start < half:
+            two.second(t - start)
+        if not fixed or 0 <= t - lag < half:
+            turn(t - lag)
+        if not fixed or 0 <= t - lag2 < half:
+            one.settle(t - lag2)
+            two.first(t - lag2)
+
+    begun = 0
+    t = 0
+    while t < lag2:
+        step(t)
+        t += 1
+    safe = max(t, start - ahead)
+    if safe > t and half > t:
+        stop = min(safe, half)
+
+        @pl.loop(t, stop)
+        def _(k):
+            step(k, False)
+
+        t = stop
+    given = None
+    pending = []
+
+    def report():
+        route = Route(as_ref[...], zs, z)
+        returned = route.collect(rb)
+        gate = gate_ref[...]
+        n, d = returned.shape
+        mixed = res_ref[...] + gate * returned
+        diff = mixed - route.own(tea_ref[...])
+        valid = route.own_col(valid_ref[pl.ds(me, 1), :])
+        scale = 1.0 / (jnp.sum(valid_ref[...]) * d)
+        weighted = valid * diff
+        grad = route.own(cot_ref[...]) + 2.0 * weighted * scale
+        sorted_out[span(z, n), :] = mixed.astype(BF)
+        pending.extend(gather_z(zs, sorted_out, n, o_s, o_r))
+        hot = route.own_hot.astype(F32)
+        stat_ref[...] = jnp.zeros_like(stat_ref)
+        stat_ref[0:1, 0:EXP] = jnp.sum(hot, axis=0, keepdims=True)
+        stat_ref[1:2, 0:EXP] = jnp.sum(hot * gate, axis=0, keepdims=True)
+        stat_ref[2:3, :] = jnp.broadcast_to(jnp.sum(weighted * diff * scale), (1, 128))
+        for s, peer in enumerate(z_peers(zs)):
+            cp = remote(stat_ref, stat_in.at[s], t_s.at[s], t_r.at[s], peer)
+            cp.start()
+            pending.append(cp)
+        gm_ref[...] = grad
+        grad_gate = jnp.sum(grad * returned, axis=-1, keepdims=True)
+        gl_ref[...] = grad_gate * gate * (1.0 - gate)
+
+    def publish():
+        total = stat_ref[...]
+        for s, cp in enumerate(pending[zs - 1 :]):
+            cp.wait_recv()
+            total = total + stat_in[s]
+        stat_all[me] = total
+        for k, (_, _, _, peer) in enumerate(group):
+            cp = remote(stat_all.at[me], stat_all.at[me], u_s.at[k], u_r.at[k], peer)
+            cp.start()
+            pending.append(cp)
+
+    while t < start + half + 1:
+        step(t)
+        if given is None and t - lag >= half - 1:
+            given = give_back(fs, results, ret, rb, wsem.at[6], b_s, b_r)
+        while begun < half and begun <= t - start + ahead and begun <= t - lag2:
+            two.cross(begun).start()
+            begun += 1
+        if 0 <= t - 1 - start < half:
+            xg[t - 1 - start] = two.total(t - 1 - start)
+        if t == start + half - 2 or (half == 1 and t == start):
+            arrived(given)
+            report()
+        if t == start + half - 1:
+            publish()
+        t += 1
+    given_back = give_back(fs, xg, ret_back, rb_back, wsem.at[7], c_s, c_r)
     route = Route(as_ref[...], zs, z)
-    returned = route.collect(rb)
-    gate = gate_ref[...]
-    m, d = returned.shape
-    mixed = res_ref[...] + gate * returned
-    diff = mixed - route.own(tea_ref[...])
-    valid = route.own_col(valid_ref[pl.ds(me, 1), :])
-    scale = 1.0 / (jnp.sum(valid_ref[...]) * d)
-    weighted = valid * diff
-    grad = route.own(cot_ref[...]) + 2.0 * weighted * scale
-    route.fill((gate * grad).astype(BF), gs)
-    sorted_out[span(z, m), :] = mixed.astype(BF)
-    hot = route.own_hot.astype(F32)
-    stat_ref[...] = jnp.zeros_like(stat_ref)
-    stat_ref[0:1, 0:EXP] = jnp.sum(hot, axis=0, keepdims=True)
-    stat_ref[1:2, 0:EXP] = jnp.sum(hot * gate, axis=0, keepdims=True)
-    stat_ref[2:3, :] = jnp.broadcast_to(jnp.sum(weighted * diff * scale), (1, 128))
-    stats = []
-    for s, peer in enumerate(z_peers(zs)):
-        cp = remote(stat_ref, stat_in.at[s], t_s.at[s], t_r.at[s], peer)
-        cp.start()
-        stats.append(cp)
-    outs = gather_z(zs, sorted_out, m, o_s, o_r)
-    gm_ref[...] = grad
-    grad_gate = jnp.sum(grad * returned, axis=-1, keepdims=True)
-    gl_ref[...] = grad_gate * gate * (1.0 - gate)
-    total = stat_ref[...]
-    for s, cp in enumerate(stats):
-        cp.wait_recv()
-        total = total + stat_in[s]
-    stat_all[me] = total
-    for k, (_, _, _, peer) in enumerate(group):
-        cp = remote(stat_all.at[me], stat_all.at[me], u_s.at[k], u_r.at[k], peer)
-        cp.start()
-        stats.append(cp)
-
-    expert_pass(True, fs, zs, gs, wd, wu, gx_ref, gh_ref, gp, rb_back, buffers, sems[1], [])
+    for cp in pending[: zs - 1]:
+        cp.wait_recv()
+    out_ref[...] = route.unsort(sorted_out[...])
+    arrived(given_back)
     gb_ref[...] = route.collect(rb_back)
-    for cp in outs:
-        cp.wait_recv()
-    out_ref[...] = route.unsort(sorted_out[...])
-    for cp in stats[zs - 1 :]:
-        cp.wait_recv()
-    for cp in outs + stats:
+    for cp in pending[2 * (zs - 1) :]:
+        cp.wait_recv()
+    for cp in pending + sends + sends_g + given[1] + given_back[1]:
         cp.wait_send()
+
+    @pl.loop(0, half)
+    def _(e):
+        two.settle(e)
+
     total = stat_all[0]
     for k in range(1, fs * 4):
         total = total + stat_all[k]
@@ -743,15 +835,15 @@
     swap_shapes = [sds(swapped, BF)] * 2
     token_shapes = [
         sds((n, d), BF), sds((k, n), BF), sds((4, n, 2 * k), BF), sds((heads, 4, n, n), BF), sds((n, k), BF),
-        sds((m, d), F32), sds((m, d), BF), sds((m, 1), F32), sds(row_shape, BF),
+        sds((m, d), F32), sds((m, d), BF), sds((m, 1), F32), sds(row_shape, BF), sds(row_shape[:4] + (d // 2 + 128,), BF),
     ]
     scattered = [VMEM((n, d), BF), VMEM((zs - 1, m, d), BF)]
     exchange = scattered + [dma((zs - 1,))] * 2 + [dma((2,))] * 2 + [dma((3,))] * 2
     gather = rows % 16 == 0
     if gather:
-        head_in = (prefix_length, tok, mixing, output_weight, small, chosen, expert_up, down)
+        head_in = (prefix_length, tok, mixing, output_weight, small, chosen, teacher[0], cotangent[0], expert_up, down)
         out_shapes = weight_shapes + swap_shapes + token_shapes
-        out_specs = [vspec()] * 4 + [anyspec] * 2 + [vspec()] * 9
+        out_specs = [vspec()] * 4 + [anyspec] * 2 + [vspec()] * 10
         scratch = [VMEM((sources, TAB, n), BF)] + exchange + [dma((2 * fs - 1, 3))] * 2 + [dma((2 * fs, 3))] * 2
     else:
         everyone = ("fsdp", "ctx")
@@ -760,9 +852,9 @@
         table = lax.all_gather(small, everyone, axis=0)
         valid_all = table[:, experts + 2, :].astype(F32)
         table = table[:, :, :rows].transpose(1, 0, 2).reshape(TAB, d)
-        head_in = (prefix_length, tok, w3, wo, table, valid_all, chosen, expert_up, down)
+        head_in = (prefix_length, tok, w3, wo, table, valid_all, chosen, teacher[0], cotangent[0], expert_up, down)
         out_shapes = swap_shapes + token_shapes
-        out_specs = [anyspec] * 2 + [vspec()] * 9
+        out_specs = [anyspec] * 2 + [vspec()] * 10
         scratch = exchange
     results = pl.pallas_call(
         partial(head_body, fs, zs, gather),
@@ -776,7 +868,7 @@
     if gather:
         w3, wo, table, valid_all = results[:4]
         results = results[4:]
-    up_x, dn_x, normed, qt, kv, pt, ctx, residual, mixed_in, gate, slots = results
+    up_x, dn_x, normed, qt, kv, pt, ctx, residual, mixed_in, gate, slots, slots_g = results
 
     slots_in = sources * CAP
     dh = d // 2
@@ -788,20 +880,23 @@
             sds(received, BF), sds(hidden, BF), sds(received, BF), sds(hidden, BF), sds((n, d), BF),
             sds((m, d), F32), sds((m, 1), F32), sds((m, d), F32), sds((8, 128), F32),
         ],
-        in_specs=[vspec()] * 7 + [anyspec] * 4,
+        in_specs=[vspec()] * 8 + [anyspec] * 4,
         out_specs=[vspec()] * 9,
         scratch_shapes=[
-            VMEM((half, dh, units), BF), VMEM((half, dh, units), BF), VMEM(hidden, BF), VMEM(row_shape, BF),
-            VMEM((sources, r, dh), BF), VMEM((sources, r, dh), BF), VMEM((n, d), BF),
-            VMEM((zs - 1, 8, 128), F32), VMEM((sources, 8, 128), F32),
-            VMEM((sources, r, dh), BF), VMEM((half, sources * per, dh), BF), VMEM(hidden, BF), VMEM(hidden, BF),
-            VMEM(received, BF), VMEM((half, zs - 1, sources * per, dh), BF), VMEM((sources, r, dh), BF),
+            VMEM((half, dh, units), BF), VMEM((half, dh, units), BF), VMEM(hidden, BF),
+            VMEM((sources, r, dh), BF), VMEM((sources, r, dh + 128), BF), VMEM((half, sources * per, dh + 128), BF),
+            VMEM((half, sources * per, dh), BF),
+            VMEM((sources, r, dh), BF), VMEM((sources, r, dh), BF), VMEM((sources, r, dh), BF), VMEM((sources, r, dh), BF),
+            VMEM((n, d), BF), VMEM((zs - 1, 8, 128), F32), VMEM((sources, 8, 128), F32),
+            VMEM((half, sources * per, dh), BF), VMEM((half, sources * per, dh), BF),
+            VMEM(hidden, BF), VMEM(hidden, BF), VMEM(hidden, BF),
+            VMEM(received, BF), VMEM((half, zs - 1, sources * per, dh), BF),
         ]
-        + pass_sems(fs, zs, half) * 2
-        + [dma((4,))] + [dma((zs - 1,))] * 4 + [dma((sources - 1,))] * 2,
+        + pass_sems(zs, half) * 2
+        + [dma((8,))] + [dma((sources - 1,))] * 8 + [dma((zs - 1,))] * 4 + [dma((sources - 1,))] * 2,
         compiler_params=params(2),
         name="middle",
-    )(slots, residual, gate, chosen, valid_all, teacher[0], cotangent[0], expert_up, up_x, down, dn_x)
+    )(slots, slots_g, residual, gate, chosen, valid_all, teacher[0], cotangent[0], expert_up, up_x, down, dn_x)
     x_x, act_x, gx_x, gh_x = core_swap(x), core_swap(act), core_swap(gx), core_swap(gh)
     all_tokens = float(n * sources)
     share = stats[0, :experts] / all_tokens - 1.0 / experts

time: 242 us -> 226 us (0.934)
  Pallas kernels: 226 us -> 209 us
    pallas_call x1, Pallas kernels: 123 us -> 105 us  [per_device(): pl.pallas_call(partial(middle_body, fs, zs), out_shape=[sds(received, BF)...]
  transfers between devices with their start and end apart: 4 -> 4, of which waited for: 0 -> 0; matrix products, arithmetic and copies ran while one was open for 2% -> 2% of each run, Pallas kernels for 20% -> 22%
where the time goes in v4:
time: 226 us; the launch traced here: 225 us
  Pallas kernels  209 us (92%)
  local copies, waits for them, and re-layouts  8.34 us (4%)
  other arithmetic  3.46 us (2%)
  between operations  3.15 us (1%)
    pallas_call x1, Pallas kernels, per_device(): pl.pallas_call(partial(middle_body, fs, zs), out_shape=[sds(received, BF)...  105 us
    pallas_call x1, Pallas kernels, per_device(): pl.pallas_call(partial(back_body, fs, zs, rows), out_shape=[sds((n, d), B...  49.5 us
    pallas_call x1, Pallas kernels, per_device(): pl.pallas_call(partial(head_body, fs, zs, gather), out_shape=out_shapes,...  42.9 us
    pallas_call x1, Pallas kernels, expert_grads(): pl.pallas_call(expert_grads_body, grid_spec=pltpu.PrefetchScalarGridSpec(...  11.6 us
  transfers between devices with their start and end apart: 4, of which 0 were waited for; matrix products, arithmetic and copies ran while one was open for 2% of the time, Pallas kernels for 22%

profile of v4, /device:TPU:0, one launch (start us, length us, event | category | flops | bytes accessed | tf_op | source)
XLA Modules:
  0.0 225.5 jit_solution(16624907375395016926)
XLA Ops:
  1.3 0.7 convert_element_type.5
  2.0 0.1 pad.7.clone
  2.1 0.7 fusion.4
  2.8 0.7 maximum_maximum_fusion.refs_4_
  3.5 42.9 %head.1 = (bf16[3,768,192]{2,1,0:T(8,128)(2,1)}, bf16[768,192]{1,0:T(8,128)(2,1)}, bf16[48,768]{1,0:T(8,128)(2,1)}, f32[8,256]{1,0:T(8,128)}, bf16[8,192,768]{2,...) custom-call(s32[1]{0:T(128)S(6)} %copy.28.refs_0_, ...), custom_call_target="tpu_custom_call" | custom-call | tf_op jit(solution)/shard_map/head/pallas_call | solution.py:859
  46.4 105.4 %middle.1 = (bf16[8,128,384]{2,1,0:T(8,128)(2,1)}, bf16[8,128,768]{2,1,0:T(8,128)(2,1)}, bf16[8,128,384]{2,1,0:T(8,128)(2,1)}, bf16[8,128,768]{2,1,0:T(8,128)(2,...) custom-call(bf16[2,2,2,32,384]{4,3,2,1,0:T(8,128)(2,1)} %get-tuple-e, ...), custom_call_target="tpu_custom_call" | custom-call | tf_op jit(solution)/shard_map/middle/pallas_call | solution.py:877
  151.8 0.2 collective-permute-start.1
  152.0 0.4 collective-permute-start.3
  152.4 0.1 collective-permute-start
  152.5 0.4 collective-permute-start.2
  152.9 1.2 slice.23
  154.1 49.5 %back.1 = (bf16[256,768]{1,0:T(8,128)(2,1)}, f32[3,96,192]{2,1,0:T(8,128)}, f32[192,96]{1,0:T(8,128)}, f32[48,128]{1,0:T(8,128)}) custom-call(f32[64,768]{1,0:T(8,128)} %get-tuple-element.50.gb_ref, f32[64,768]{1,0:T(8,128)} %get-tuple-element.44.res_ref, bf16[64,768]{1,0:T(8,128)(2,1)} %get-tuple-element.51.mi_ref, f32[64,768]{1,0:T(8,128)} %get-tuple-element.52.gm_ref, ...), custom_call_target="tpu_custom_call" | custom-call | tf_op jit(solution)/shard_map/back/pallas_call | solution.py:908
  203.6 1.3 slice.20
  204.9 1.4 multiply_reduce_fusion
  206.9 1.3 slice_bitcast_fusion
  208.2 0.0 collective-permute-done.refs_2_
  208.2 0.0 collective-permute-done.2.refs_6_
  208.2 0.0 collective-permute-done.1.refs_3_
  208.2 0.0 copy-start
  208.2 0.0 collective-permute-done.3.refs_7_
  208.2 0.0 copy-start.1
  208.2 1.2 copy-done
  209.4 0.4 copy-done.1
  209.9 0.0 copy-start.2
  209.9 0.0 copy-start.3
  209.9 0.0 copy-start.4
  209.9 0.0 copy-start.5
  209.9 11.6 %expert_grads.1 = (f32[2,8,192,768]{3,2,1,0:T(8,128)}, f32[2,8,192,768]{3,2,1,0:T(8,128)}) custom-call(s32[1]{0:T(128)} %bitcast.13.c_ref, bf16[8,128,384]{2,1,0:T(8,128)(2,1)} %get-tuple-element.66.refs_0_, bf16[8,128,768]{2,1,0:T(8,128)(2,1)} %get-tuple-element.67.refs_1_, bf16[8,128,384]{2,1,0:T(8,128)(2,1)} %collective-permute-done.refs_2_, ...), custom_call_target="tpu_custom_call" | custom-call | tf_op jit(solution)/shard_map/expert_grads/pallas_call | solution.py:285
  221.5 0.0 copy-done.2
  221.5 0.7 copy.29
  222.3 0.0 copy-done.3
  222.3 0.7 copy.30
  223.0 0.0 copy-done.4
  223.0 0.7 copy.31
  223.7 0.0 copy-done.5
  223.7 0.6 copy.32
  (1 shorter events, 0.0 us)
Async XLA Ops:
  151.8 56.4 %collective-permute-start.1 = (bf16[8,128,768]{2,1,0:T(8,128)(2,1)}, bf16[8,128,768]{2,1,0:T(8,128)(2,1)S(1)}, u32[]{:S(2)}, u32[]{:S(2)}) collective-permute-start(bf16[8,128,768]{2,1,0:T(8,128)(2,1)} %get-tuple-element.67.refs_1_), channel_id=1, source_target_pairs={{0,4},{4,0},{8,12},{12,8},{1,5},{5,1},{9,13},{13,9},{2,6},{6,2},{1... | collective-permute-start | bytes 4718600 | tf_op jit(solution)/shard_map/ppermute | solution.py:816
  152.0 56.2 %collective-permute-start.3 = (bf16[8,128,768]{2,1,0:T(8,128)(2,1)}, bf16[8,128,768]{2,1,0:T(8,128)(2,1)S(1)}, u32[]{:S(2)}, u32[]{:S(2)}) collective-permute-start(bf16[8,128,768]{2,1,0:T(8,128)(2,1)} %get-tuple-element.69.refs_5_), channel_id=1, source_target_pairs={{0,4},{4,0},{8,12},{12,8},{1,5},{5,1},{9,13},{13,9},{2,6},{6,2},{1... | collective-permute-start | bytes 4718600 | tf_op jit(solution)/shard_map/ppermute | solution.py:816
  152.4 55.8 %collective-permute-start = (bf16[8,128,384]{2,1,0:T(8,128)(2,1)}, bf16[8,128,384]{2,1,0:T(8,128)(2,1)}, u32[]{:S(2)}, u32[]{:S(2)}) collective-permute-start(bf16[8,128,384]{2,1,0:T(8,128)(2,1)} %get-tuple-element.66.refs_0_), channel_id=1, source_target_pairs={{0,4},{4,0},{8,12},{12,8},{1,5},{5,1},{9,13},{13,9},{2,6},{6,2},{1... | collective-permute-start | bytes 2359304 | tf_op jit(solution)/shard_map/ppermute | solution.py:816
  152.5 55.7 %collective-permute-start.2 = (bf16[8,128,384]{2,1,0:T(8,128)(2,1)}, bf16[8,128,384]{2,1,0:T(8,128)(2,1)}, u32[]{:S(2)}, u32[]{:S(2)}) collective-permute-start(bf16[8,128,384]{2,1,0:T(8,128)(2,1)} %get-tuple-element.68.refs_4_), channel_id=1, source_target_pairs={{0,4},{4,0},{8,12},{12,8},{1,5},{5,1},{9,13},{13,9},{2,6},{6,2},{1... | collective-permute-start | bytes 2359304 | tf_op jit(solution)/shard_map/ppermute | solution.py:816
  208.2 1.2 copy-start
  208.2 1.6 copy-start.1
  209.9 11.6 %copy-start.2 = (bf16[256,768]{1,0:T(8,128)(2,1)S(1)}, bf16[256,768]{1,0:T(8,128)(2,1)}, u32[]{:S(2)}) copy-start(bf16[256,768]{1,0:T(8,128)(2,1)} %get-tuple-element.49) | copy-start | bytes 1179652
  209.9 12.4 %copy-start.3 = (bf16[256,768]{1,0:T(8,128)(2,1)S(1)}, bf16[256,768]{1,0:T(8,128)(2,1)}, u32[]{:S(2)}) copy-start(bf16[256,768]{1,0:T(8,128)(2,1)} %get-tuple-element.62) | copy-start | bytes 1179652
  209.9 13.1 %copy-start.4 = (f32[3,96,192]{2,1,0:T(8,128)S(1)}, f32[3,96,192]{2,1,0:T(8,128)}, u32[]{:S(2)}) copy-start(f32[3,96,192]{2,1,0:T(8,128)} %get-tuple-element.63) | copy-start | bytes 663556
  209.9 13.9 %copy-start.5 = (f32[192,96]{1,0:T(8,128)S(1)}, f32[192,96]{1,0:T(8,128)}, u32[]{:S(2)}) copy-start(f32[192,96]{1,0:T(8,128)} %get-tuple-element.89) | copy-start | bytes 221188

commit v5 on v4

v5 whole, which is shorter than its diff:
```python
from functools import partial
import math
from types import SimpleNamespace

import jax
import jax.numpy as jnp
from jax import lax
from jax.experimental import pallas as pl
from jax.experimental.pallas import tpu as pltpu
from jax.sharding import PartitionSpec as P

HD = 64
EPSILON = 1e-05
BF = jnp.bfloat16
F32 = jnp.float32
MESH = pl.DeviceIdType.MESH
TOP = lax.Precision.HIGHEST
VMEM = pltpu.VMEM
ANY = pl.ANY
CAP = 16
EXP = 32
TAB = 48


def _dot(a, b, ca, cb, precision=None):
    return lax.dot_general(
        a, b, (((ca,), (cb,)), ((), ())), preferred_element_type=F32, precision=precision
    )


def nn(a, b):
    return _dot(a, b, 1, 0)


def nt(a, b):
    return _dot(a, b, 1, 1)


def tn(a, b):
    return _dot(a, b, 0, 0)


def vspec():
    return pl.BlockSpec(memory_space=VMEM)


def sds(shape, dtype):
    return jax.ShapeDtypeStruct(shape, dtype)


def params(cid=None, mib=56):
    if cid is None:
        return pltpu.CompilerParams(vmem_limit_bytes=mib * 2**20)
    return pltpu.CompilerParams(
        vmem_limit_bytes=mib * 2**20, collective_id=cid, has_side_effects=True
    )


def iota(shape, dim):
    return lax.broadcasted_iota(jnp.int32, shape, dim)


def to_col(row):
    n = row.shape[1]
    return jnp.sum(jnp.where(iota((n, n), 0) == iota((n, n), 1), row, 0.0), axis=1, keepdims=True)


def to_row(col):
    n = col.shape[0]
    return jnp.sum(jnp.where(iota((n, n), 0) == iota((n, n), 1), col, 0.0), axis=0, keepdims=True)


def norm_parts(x):
    c = x - jnp.mean(x, axis=-1, keepdims=True)
    inv = lax.rsqrt(jnp.mean(c * c, axis=-1, keepdims=True) + EPSILON)
    return c * inv, inv


def norm_back(grad, xhat, inv, gain):
    gx = grad * gain
    return inv * (
        gx
        - jnp.mean(gx, axis=-1, keepdims=True)
        - xhat * jnp.mean(gx * xhat, axis=-1, keepdims=True)
    )


def log2(v):
    return v.bit_length() - 1


def shifted(v, by):
    return lax.shift_right_logical(v, by)


class Route:
    def __init__(self, chosen, zs, z, width=0):
        n = chosen.shape[1]
        m = n // zs
        per = CAP // zs
        chosen = to_col(chosen.astype(F32))
        self.hot = (chosen == iota((n, EXP), 1).astype(F32)).astype(BF)
        lower = (iota((n, n), 1) < iota((n, n), 0)).astype(BF)
        rank = jnp.sum(nn(lower, self.hot) * self.hot.astype(F32), axis=1, keepdims=True)
        turn = jnp.floor(rank * (1.0 / zs))
        owner = rank - zs * turn
        owned = (owner == iota((n, zs), 1).astype(F32)).astype(BF)
        place = jnp.sum(nn(lower, owned) * owned.astype(F32), axis=1, keepdims=True)
        self.at = owner * m + place
        self.at_row = to_row(self.at)
        mine = iota((m, n), 0).astype(F32) + lax.convert_element_type(z * m, F32) == self.at_row
        self.mine = mine.astype(BF)
        self.mine_mask = mine
        self.slot = self.own_col(to_row(chosen * per + turn))
        self.own_hot = nn(self.mine, self.hot).astype(BF)
        self.slots = EXP * per
        self.n, self.m, self.width = n, m, width

    def own_col(self, row):
        return jnp.sum(jnp.where(self.mine_mask, row, 0.0), axis=1, keepdims=True)

    def own(self, rows):
        return nn(self.mine, rows)

    def sort(self, rows):
        return nn((iota((self.n, self.n), 0).astype(F32) == self.at_row).astype(BF), rows).astype(BF)

    def unsort(self, rows):
        return nn((iota((self.n, self.n), 1).astype(F32) == self.at).astype(BF), rows).astype(BF)

    def fill(self, rows, s_ref):
        place = (iota((self.slots, self.m), 0).astype(F32) == to_row(self.slot)).astype(BF)
        filled = nn(place, rows).astype(BF)
        fs, _, _, r, _ = s_ref.shape
        h = self.width // 2
        for f in range(fs):
            for c in range(2):
                at = (f * 2 + c) * r
                for y in range(2):
                    s_ref[f, y, c, :, :h] = filled[at : at + r, y * h : (y + 1) * h]
                    if rows.shape[1] > self.width:
                        s_ref[f, y, c, :, h:] = filled[at : at + r, self.width :]

    def collect(self, rb_ref):
        parts = []
        for f in range(rb_ref.shape[0] // 4):
            for c in range(2):
                parts.append(jnp.concatenate([rb_ref[f * 4 + c], rb_ref[f * 4 + 2 + c]], axis=1))
        rows = jnp.concatenate(parts, axis=0)
        place = (iota((self.m, self.slots), 1).astype(F32) == self.slot).astype(BF)
        return nn(place, rows)


def z_peers(zs):
    f, i, z = lax.axis_index("fsdp"), lax.axis_index("ctx"), lax.axis_index("tp")
    return [(f, i, lax.rem(z + s, zs)) for s in range(1, zs)]


def greet(peers):
    barrier = pltpu.get_barrier_semaphore()
    for peer in peers:
        pl.semaphore_signal(barrier, inc=1, device_id=peer, device_id_type=MESH)
    pl.semaphore_wait(barrier, len(peers))


def remote(src, dst, send, recv, peer):
    return pltpu.make_async_remote_copy(
        src_ref=src, dst_ref=dst, send_sem=send, recv_sem=recv, device_id=peer, device_id_type=MESH
    )


def scatter_z(zs, x_ref, parts, send, recv):
    z = lax.axis_index("tp")
    n = x_ref.shape[0] // zs
    copies = []
    for s, peer in enumerate(z_peers(zs)):
        to = lax.rem(z + s + 1, zs)
        cp = remote(x_ref.at[span(to, n)], parts.at[s], send.at[s], recv.at[s], peer)
        cp.start()
        copies.append(cp)
    total = x_ref[span(z, n), :].astype(F32)
    for s, cp in enumerate(copies):
        cp.wait_recv()
        total = total + parts[s].astype(F32)
    return total, copies


def gather_z(zs, x_ref, n, send, recv):
    z = lax.axis_index("tp")
    copies = []
    for s, peer in enumerate(z_peers(zs)):
        cp = remote(x_ref.at[span(z, n)], x_ref.at[span(z, n)], send.at[s], recv.at[s], peer)
        cp.start()
        copies.append(cp)
    return copies


def span(at, n):
    return pl.ds(pl.multiple_of(at * n, n), n)


def group_peers(fs):
    f, i, z = lax.axis_index("fsdp"), lax.axis_index("ctx"), lax.axis_index("tp")
    y, c = lax.div(i, 2), lax.rem(i, 2)
    out = []
    for df in range(fs):
        for dy in range(2):
            for dc in range(2):
                if df or dy or dc:
                    fp = lax.rem(f + df, fs)
                    yp = y if dy == 0 else 1 - y
                    cp = c if dc == 0 else 1 - c
                    out.append((fp, yp, cp, (fp, yp * 2 + cp, z)))
    return out


def attend(mine, prefix, offsets, qt_ref, kv_ref, valid_ref, row0, pt_ref, sc_ref, arrive):
    k, n = qt_ref.shape
    heads = k // HD
    query = iota((n, n), 1) + mine * n
    for j in (0, 2, 1, 3):
        if j == 1:
            arrive()
        key = iota((n, n), 0) + offsets[j] * n
        col = to_col(valid_ref[pl.ds(row0 + offsets[j], 1), :])
        allowed = ((key <= query) | (key < prefix)) & ((col > 0.5) | (key == query))
        for h in range(heads):
            lo = h * HD
            scores = nn(kv_ref[j, :, lo : lo + HD], qt_ref[lo : lo + HD, :]) * (1.0 / math.sqrt(HD))
            sc_ref[h, j] = jnp.where(allowed, scores, -1e30)
    outs = []
    for h in range(heads):
        lo = h * HD
        top = jnp.max(sc_ref[h, 0], axis=0, keepdims=True)
        for j in range(1, 4):
            top = jnp.maximum(top, jnp.max(sc_ref[h, j], axis=0, keepdims=True))
        exps = [jnp.exp(sc_ref[h, j] - top) for j in range(4)]
        share = 1.0 / sum(jnp.sum(e, axis=0, keepdims=True) for e in exps)
        acc = jnp.zeros((HD, n), F32)
        for j in range(4):
            w = (exps[j] * share).astype(BF)
            pt_ref[h, j] = w
            acc = acc + tn(kv_ref[j, :, k + lo : k + lo + HD], w)
        outs.append(acc)
    return jnp.transpose(jnp.concatenate(outs, axis=0)).astype(BF)


def attend_back(gct, qt_ref, kv_ref, pt_ref, near_ref, away_ref):
    k, n = qt_ref.shape
    scale = 1.0 / math.sqrt(HD)
    dqs = []
    for h in range(k // HD):
        lo = h * HD
        dot_ = gct[lo : lo + HD, :]
        qt = qt_ref[lo : lo + HD, :]
        ws = [pt_ref[h, j] for j in range(4)]
        dps = [nn(kv_ref[j, :, k + lo : k + lo + HD], dot_) for j in range(4)]
        mean = sum(jnp.sum(ws[j].astype(F32) * dps[j], axis=0, keepdims=True) for j in range(4))
        dq = jnp.zeros((HD, n), F32)
        for j in range(4):
            ds = (ws[j].astype(F32) * (dps[j] - mean)).astype(BF)
            dq = dq + tn(kv_ref[j, :, lo : lo + HD], ds)
            target = near_ref if j < 2 else away_ref
            target[j % 2, :, lo : lo + HD] = nt(ds, qt) * scale
            target[j % 2, :, k + lo : k + lo + HD] = nt(ws[j], dot_)
        dqs.append(dq * scale)
    return jnp.transpose(jnp.concatenate(dqs, axis=0)).astype(BF)


def finish_body(scalars, c_ref, *refs):
    tg_in, act_in, mix_in, og_in, sm_in, stat_in = refs[8:14]
    up_ref, down_ref, tg_ref, act_ref, mix_ref, og_ref, cen_ref, g1_ref, g2_ref, bal_ref, dis_ref = refs[14:]
    c = c_ref[0]
    for out_ref, at in ((up_ref, 0), (down_ref, 4)):
        for core, (left_ref, right_ref) in ((c, refs[at : at + 2]), (1 - c, refs[at + 2 : at + 4])):
            for e in range(left_ref.shape[0]):
                out_ref[core, e] = nn(left_ref[e], right_ref[e])

    @pl.when(pl.program_id(0) == 0)
    def _():
        tg_ref[...] = tg_in[...]
        act_ref[...] = act_in[...]
        mix_ref[...] = mix_in[...]
        og_ref[...] = og_in[...]
        rows = cen_ref.shape[1]
        cen_ref[...] = sm_in[0:EXP, :rows]
        g1_ref[...] = sm_in[EXP : EXP + 1, :rows]
        g2_ref[...] = sm_in[EXP + 1 : EXP + 2, :rows]
        share = stat_in[0:1, :EXP] / scalars - 1.0 / EXP
        bal_ref[0, 0] = EXP * EXP * jnp.sum(share * stat_in[1:2, :EXP] / scalars)
        dis_ref[0, 0] = jnp.sum(stat_in[2:3, 0:1])


def finish(c, tokens, pairs, small, shapes):
    half, q, n = pairs[0].shape
    units = pairs[1].shape[2]
    step = 2 if half % 2 == 0 else 1
    block = lambda e, c_ref: (e, 0, 0)
    out = sds((2, half, q, units), F32)
    whole = lambda v: pl.BlockSpec(v.shape, lambda e, c_ref: (0,) * len(v.shape))
    smem = pl.BlockSpec(memory_space=pltpu.SMEM)
    scalar = sds((1, 1), F32)
    return pl.pallas_call(
        partial(finish_body, float(tokens)),
        grid_spec=pltpu.PrefetchScalarGridSpec(
            num_scalar_prefetch=1,
            grid=(half // step,),
            in_specs=[pl.BlockSpec((step, q, n), block), pl.BlockSpec((step, n, units), block)] * 4
            + [whole(v) for v in small],
            out_specs=[pl.BlockSpec((2, step, q, units), lambda e, c_ref: (0, e, 0, 0))] * 2
            + [whole(v) for v in shapes] + [smem] * 2,
        ),
        out_shape=[out, out] + shapes + [scalar] * 2,
        compiler_params=params(),
        name="finish",
    )(c.reshape(1), *pairs, *small)


def whereabouts():
    f, i, z = lax.axis_index("fsdp"), lax.axis_index("ctx"), lax.axis_index("tp")
    return f, i, z, lax.div(i, 2), lax.rem(i, 2)


def reorder(sources, half, per, inverse):
    n = sources * half * per
    i, o = iota((n, n), 1), iota((n, n), 0)
    if inverse:
        i, o = o, i
    ls, lh, lp = log2(sources), log2(half), log2(per)
    slot = o & (per - 1)
    source = shifted(o, lp) & (sources - 1)
    expert = shifted(o, lp + ls)
    return (i == source * (half * per) + expert * per + slot).astype(BF)


class Pass:
    def __init__(self, back, zs, w_in, w_out, xg, x_ref, ps, pr, h_ref, gp_ref, res, rin, sems):
        self.back, self.zs, self.w_in, self.w_out = back, zs, w_in, w_out
        self.xg, self.x_ref, self.ps, self.pr = xg, x_ref, ps, pr
        self.h_ref, self.gp_ref, self.res, self.rin = h_ref, gp_ref, res, rin
        self.a_s, self.a_r, self.x_s, self.x_r, self.r_s, self.r_r = sems
        f, i, z, y, c = whereabouts()
        self.z = z
        self.m = xg.shape[1]
        self.across = (f, (1 - y) * 2 + c, z)
        self.peers = z_peers(zs)

    def share(self, e, s):
        to = self.x_ref.at[e, span(self.z, self.m), :]
        return remote(self.xg.at[e], to, self.a_s.at[e, s], self.a_r.at[e, s], self.peers[s])

    def cross(self, e):
        return remote(self.ps.at[e], self.pr.at[e], self.x_s.at[e], self.x_r.at[e], self.across)

    def scatter(self, e, s):
        to = lax.rem(self.z + s + 1, self.zs)
        return remote(
            self.res.at[e, span(to, self.m), :], self.rin.at[e, s], self.r_s.at[e, s], self.r_r.at[e, s], self.peers[s]
        )

    def spread(self, e, rows):
        self.xg[e] = rows
        for s in range(self.zs - 1):
            self.share(e, s).start()
        self.x_ref[e, span(self.z, self.m), :] = rows

    def first(self, e):
        for s in range(self.zs - 1):
            self.share(e, s).wait_recv()
        self.ps[e] = nn(self.x_ref[e], self.w_in[e]).astype(BF)

    def second(self, e):
        self.cross(e).wait_recv()
        total = self.ps[e].astype(F32) + self.pr[e].astype(F32)
        if self.back:
            self.h_ref[e] = (total * self.gp_ref[e].astype(F32)).astype(BF)
        else:
            phi = 0.5 * (1.0 + lax.erf(total * math.sqrt(0.5)))
            self.h_ref[e] = (total * phi).astype(BF)
            bell = jnp.exp(-0.5 * total * total) * (1.0 / math.sqrt(2.0 * math.pi))
            self.gp_ref[e] = (phi + total * bell).astype(BF)
        self.res[e] = nt(self.h_ref[e], self.w_out[e]).astype(BF)
        for s in range(self.zs - 1):
            self.scatter(e, s).start()

    def total(self, e):
        total = self.res[e, span(self.z, self.m), :].astype(F32)
        for s in range(self.zs - 1):
            self.scatter(e, s).wait_recv()
            total = total + self.rin[e, s].astype(F32)
        return total.astype(BF)

    def settle(self, e):
        self.cross(e).wait_send()
        for s in range(self.zs - 1):
            self.share(e, s).wait_send()
            self.scatter(e, s).wait_send()


def give_back(fs, total, ret, rb_ref, own_sem, send, recv):
    f, i, z, y, c = whereabouts()
    me = f * 4 + i
    sources, r, dh = ret.shape
    half = total.shape[0]
    rows = total[...].reshape(sources * r, dh)
    ret[...] = nn(reorder(sources, half, r // half, True), rows).astype(BF).reshape(sources, r, dh)
    keep = pltpu.make_async_copy(ret.at[me], rb_ref.at[me], own_sem)
    keep.start()
    copies = []
    for k, (fp, yp, cp_, peer) in enumerate(group_peers(fs)):
        cp = remote(ret.at[fp * 4 + yp * 2 + cp_], rb_ref.at[me], send.at[k], recv.at[k], peer)
        cp.start()
        copies.append(cp)
    return keep, copies


def arrived(given):
    keep, copies = given
    keep.wait()
    for cp in copies:
        cp.wait_recv()


def head(R, fs, zs, gather):
    f, i, z, y, c = whereabouts()
    me = f * 4 + i
    half, width = R.wu.shape[0], R.up.shape[1]
    k = R.qt.shape[0]
    d = R.tok.shape[1]
    sibling = (f, y * 2 + 1 - c, z)
    across = (f, (1 - y) * 2 + c, z)
    same = same_core(fs)
    waits = []
    mine = pl.ds(c * half, half)
    theirs = pl.ds((1 - c) * half, half)
    own = pl.ds(pl.multiple_of(c * width, 64), width)
    loads = [
        pltpu.make_async_copy(R.up.at[mine], R.wu.at[:, own, :], R.wsem.at[0]),
        pltpu.make_async_copy(R.dn.at[mine], R.wd.at[:, own, :], R.wsem.at[1]),
    ]
    swaps = [
        remote(R.up.at[theirs], R.wu.at[:, own, :], R.wx_s.at[0], R.wx_r.at[0], sibling),
        remote(R.dn.at[theirs], R.wd.at[:, own, :], R.wx_s.at[1], R.wx_r.at[1], sibling),
    ]
    if gather:
        rows = R.mix.shape[1]
        R.small[...] = jnp.zeros(R.small.shape, F32)
        R.small[0:EXP, :rows] = R.cent[...].astype(F32)
        R.small[EXP : EXP + 1, :rows] = R.gain1[...].astype(F32)
        R.small[EXP + 1 : EXP + 2, :rows] = R.gain2[...].astype(F32)
        R.small[EXP + 2 : EXP + 3, :] = R.here[...].astype(F32)
        R.small_all[me] = R.small[...].astype(BF)
        R.w3[:, span(me, rows), :] = R.mix[...]
        R.wo[span(me, rows), :] = jnp.transpose(R.ow[...].astype(F32)).astype(BF)
    greet([p[3] for p in group_peers(fs)] + z_peers(zs))
    for cp in loads:
        cp.start()
    xhat, _ = norm_parts(R.tok[...].astype(F32))
    if gather:

        def places(at):
            rows_ = span(at, rows)
            return [R.w3.at[1:3, rows_, :], R.small_all.at[at], R.w3.at[0:1, rows_, :], R.wo.at[rows_, :]]

        sends = {}
        for m, ref in enumerate(places(me)):
            for n_, (_, _, peer, _) in enumerate(same):
                cp = remote(ref, ref, R.p_s.at[n_, m], R.p_r.at[n_, m], peer)
                cp.start()
                sends[n_, m] = cp
        relays = {}

        def relay(n_, m, at):
            ref = places(at)[m]
            cp = remote(ref, ref, R.q_s.at[n_, m], R.q_r.at[n_, m], sibling)
            cp.start()
            relays[n_, m] = cp

        def pass_on(some):
            for n_, (_, _, _, at) in enumerate(same):
                for m in some:
                    sends[n_, m].wait_recv()
                    relay(n_ + 1, m, at)

        for m in range(4):
            relay(0, m, me)
        pass_on((0, 1))
        for n_ in range(len(same) + 1):
            for m in (0, 1):
                relays[n_, m].wait_recv()
        R.table[...] = jnp.concatenate([R.small_all[s, :, :rows] for s in range(fs * 4)], axis=1)
        for s in range(fs * 4):
            R.valid[s : s + 1, :] = R.small_all[s, EXP + 2 : EXP + 3, :].astype(F32)
    normed = (xhat * R.table[EXP : EXP + 1, :].astype(F32)).astype(BF)
    R.normed[...] = normed
    R.kv[0, :, :k] = nn(normed, R.w3[1]).astype(BF)
    R.kv[0, :, k:] = nn(normed, R.w3[2]).astype(BF)
    far = remote(R.kv.at[0], R.kv.at[1], R.kv_s.at[0], R.kv_r.at[0], across)
    sib = remote(R.kv.at[0], R.kv.at[2], R.kv_s.at[1], R.kv_r.at[1], sibling)
    far.start()
    sib.start()
    if gather:
        pass_on((2, 3))
        for n_ in range(len(same) + 1):
            for m in (2, 3):
                relays[n_, m].wait_recv()
        waits += list(sends.values()) + list(relays.values())
    R.qt[...] = jnp.transpose(nn(normed, R.w3[0])).astype(BF)
    route = Route(R.chosen[...], zs, z, d)
    teacher, cotangent = route.own(R.tea[...]), route.own(R.cot[...])
    own_valid = route.own_col(R.valid[pl.ds(me, 1), :])
    scale = 1.0 / (jnp.sum(R.valid[...]) * d)
    sib.wait_recv()
    last = []

    def arrive():
        far.wait_recv()
        cp = remote(R.kv.at[1], R.kv.at[3], R.kv_s.at[2], R.kv_r.at[2], sibling)
        cp.start()
        for swap in swaps:
            swap.start()
        cp.wait_recv()
        last.append(cp)

    offsets = [i, (1 - y) * 2 + c, y * 2 + 1 - c, (1 - y) * 2 + 1 - c]
    ctx = attend(i, R.prefix[0], offsets, R.qt, R.kv, R.valid, f * 4, R.pt, R.scores, arrive)
    R.ctx[...] = ctx
    R.branch[...] = route.sort(nt(ctx, R.wo[...]).astype(BF))
    total, sums = scatter_z(zs, R.branch, R.parts, R.hz_s, R.hz_r)
    residual = route.own(R.tok[...]) + total
    R.res[...] = residual
    xhat, _ = norm_parts(residual)
    mixed_in = (xhat * R.table[EXP + 1 : EXP + 2, :].astype(F32)).astype(BF)
    R.mi[...] = mixed_in
    logit = jnp.sum(mixed_in.astype(F32) * nn(route.own_hot, R.table[0:EXP, :]), axis=-1, keepdims=True)
    gate = jax.nn.sigmoid(logit)
    route.fill(mixed_in, R.slots)
    weight = 2.0 * own_valid * scale
    known = gate * (cotangent + weight * (residual - teacher))
    slope = jnp.broadcast_to(gate * gate * weight, (known.shape[0], 128))
    route.fill(jnp.concatenate([known, slope], axis=1).astype(BF), R.slots_g)
    waits += swaps + sums + [far, sib] + last
    return SimpleNamespace(route=route, gate=gate, teacher=teacher, cotangent=cotangent, valid=own_valid, scale=scale,
                           loads=loads, swaps=swaps, waits=waits)


def same_core(fs):
    f, i, z, y, c = whereabouts()
    out = []
    for df in range(fs):
        for dy in range(2):
            if df or dy:
                fp, fm = lax.rem(f + df, fs), lax.rem(f - df + fs, fs)
                yp = y if dy == 0 else 1 - y
                out.append((fp, yp, (fp, yp * 2 + c, z), fm * 4 + yp * 2 + c))
    return out


def middle(R, S, fs, zs):
    f, i, z, y, c = whereabouts()
    me = f * 4 + i
    half, width = R.wu.shape[0], R.up.shape[1]
    sources, r, dh = R.rq.shape
    m = sources * r // half
    group = group_peers(fs)
    sibling = (f, y * 2 + 1 - c, z)
    own = pl.ds(pl.multiple_of(c * width, 64), width)
    other = pl.ds(pl.multiple_of((1 - c) * width, 64), width)
    keeps = [
        pltpu.make_async_copy(R.slots.at[f, y, c], R.rq.at[me], R.wsem.at[2]),
        pltpu.make_async_copy(R.slots_g.at[f, y, c], R.rg.at[me], R.wsem.at[3]),
    ]
    for cp in keeps:
        cp.start()
    sends, sends_g = [], []
    for out, src, dst, send, recv in ((sends, R.slots, R.rq, R.d_s, R.d_r), (sends_g, R.slots_g, R.rg, R.g_s, R.g_r)):
        for k, (fp, yp, cp_, peer) in enumerate(group):
            cp = remote(src.at[fp, yp, cp_], dst.at[me], send.at[k], recv.at[k], peer)
            cp.start()
            out.append(cp)
    sems = [[getattr(R, p + n) for n in ("a_s", "a_r", "x_s", "x_r", "r_s", "r_r")] for p in ("one_", "two_")]
    one = Pass(False, zs, R.wu, R.wd, R.xg, R.x, R.ps, R.pr, R.act, R.gp, R.rows, R.rin, sems[0])
    two = Pass(True, zs, R.wd, R.wu, R.xg_back, R.gx, R.ps, R.pr_back, R.gh, R.gp, R.rows, R.rin, sems[1])
    order = reorder(sources, half, r // half, False)
    exports = []

    def export(n, own_src, own_dst, src, dst):
        keep = pltpu.make_async_copy(own_src, own_dst, R.l_s.at[n])
        give = remote(src, dst, R.e_s.at[n], R.e_r.at[n], sibling)
        keep.start()
        give.start()
        exports.append((keep, give))

    for cp in S.loads:
        cp.wait()
    for cp in S.swaps:
        cp.wait_recv()
    keeps[0].wait()
    for cp in sends:
        cp.wait_recv()
    rows = nn(order, R.rq[...].reshape(sources * r, dh)).astype(BF).reshape(half, m, dh)
    for e in range(half):
        one.spread(e, rows[e])

    @pl.loop(0, half)
    def _(e):
        one.first(e)
        one.cross(e).start()

    @pl.loop(0, half)
    def _(e):
        R.xt[e] = jnp.transpose(R.x[e])

    keeps[1].wait()
    for cp in sends_g:
        cp.wait_recv()
    R.grads[...] = nn(order, R.rg[...].reshape(sources * r, dh + 128)).astype(BF).reshape(half, m, dh + 128)
    export(0, R.xt.at[:, own, :], R.xt_own, R.xt.at[:, other, :], R.xt_sib)

    def turn(e):
        result = one.total(e)
        R.results[e] = result
        scale = R.grads[e, :, dh:].astype(F32)[:, :1]
        two.spread(e, (R.grads[e, :, :dh].astype(F32) + scale * result.astype(F32)).astype(BF))

    lag, lag2 = 2, 4
    start = max(half, lag2 + 1)
    ahead = 3

    def step(t, fixed=True):
        if not fixed or t < half:
            one.second(t)
        if fixed and t - start >= 0 and t - start < half:
            two.second(t - start)
        if not fixed or 0 <= t - lag < half:
            turn(t - lag)
        if not fixed or 0 <= t - lag2 < half:
            one.settle(t - lag2)
            two.first(t - lag2)

    begun = 0
    t = 0
    while t < lag2:
        step(t)
        t += 1
    safe = max(t, start - ahead)
    if safe > t and half > t:
        stop = min(safe, half)

        @pl.loop(t, stop)
        def _(k):
            step(k, False)

        t = stop
    given = None
    pending = []

    def report():
        returned = S.route.collect(R.rb)
        n, d = returned.shape
        mixed = R.res[...] + S.gate * returned
        diff = mixed - S.teacher
        weighted = S.valid * diff
        grad = S.cotangent + 2.0 * weighted * S.scale
        R.sorted_out[span(z, n), :] = mixed.astype(BF)
        pending.extend(gather_z(zs, R.sorted_out, n, R.o_s, R.o_r))
        hot = S.route.own_hot.astype(F32)
        R.stat[...] = jnp.zeros_like(R.stat)
        R.stat[0:1, 0:EXP] = jnp.sum(hot, axis=0, keepdims=True)
        R.stat[1:2, 0:EXP] = jnp.sum(hot * S.gate, axis=0, keepdims=True)
        R.stat[2:3, :] = jnp.broadcast_to(jnp.sum(weighted * diff * S.scale), (1, 128))
        for s, peer in enumerate(z_peers(zs)):
            cp = remote(R.stat, R.stat_in.at[s], R.t_s.at[s], R.t_r.at[s], peer)
            cp.start()
            pending.append(cp)
        R.gm[...] = grad
        grad_gate = jnp.sum(grad * returned, axis=-1, keepdims=True)
        R.gl[...] = grad_gate * S.gate * (1.0 - S.gate)

    def publish():
        total = R.stat[...]
        for s, cp in enumerate(pending[zs - 1 :]):
            cp.wait_recv()
            total = total + R.stat_in[s]
        R.stat_all[me] = total
        for k, (_, _, _, peer) in enumerate(group):
            cp = remote(R.stat_all.at[me], R.stat_all.at[me], R.u_s.at[k], R.u_r.at[k], peer)
            cp.start()
            pending.append(cp)

    while t < start + half + 1:
        step(t)
        if given is None and t - lag >= half - 1:
            given = give_back(fs, R.results, R.ret, R.rb, R.wsem.at[4], R.b_s, R.b_r)
            export(1, R.act, R.act_own, R.act, R.act_sib)
        while begun < half and begun <= t - start + ahead and begun <= t - lag2:
            two.cross(begun).start()
            begun += 1
        if 0 <= t - 1 - start < half:
            R.xg[t - 1 - start] = two.total(t - 1 - start)
        if t == max(start + half - 4, start + 1) or (half == 1 and t == start):

            @pl.loop(0, half)
            def _(e):
                R.gxt[e] = jnp.transpose(R.gx[e])

        if t == start + half - 2 or (half == 1 and t == start):
            arrived(given)
            report()
        if t == start + half - 1:
            publish()
        t += 1
    given_back = give_back(fs, R.xg, R.ret_back, R.rb_back, R.wsem.at[5], R.c_s, R.c_r)
    export(2, R.gxt.at[:, own, :], R.gxt_own, R.gxt.at[:, other, :], R.gxt_sib)
    export(3, R.gh, R.gh_own, R.gh, R.gh_sib)
    S.pending, S.exports = pending, exports
    S.waits += pending[: 2 * (zs - 1)] + sends + sends_g + given[1] + given_back[1]
    S.two = two
    arrived(given_back)
    return S.route.collect(R.rb_back)


def back(R, S, grad_back, fs, zs, rows):
    f, i, z, y, c = whereabouts()
    sibling = (f, y * 2 + 1 - c, z)
    across = (f, (1 - y) * 2 + c, z)
    same = same_core(fs)
    route = S.route
    k = R.qt.shape[0]
    gl = R.gl[...]
    grad_in = grad_back + gl * nn(route.own_hot, R.table[0:EXP, :])
    m, d = grad_in.shape
    xhat, inv = norm_parts(R.res[...])
    grad = R.gm[...] + norm_back(grad_in, xhat, inv, R.table[EXP + 1 : EXP + 2, :].astype(F32))
    R.sorted_gb[span(z, m), :] = grad.astype(BF)
    gathers = gather_z(zs, R.sorted_gb, m, R.ba_s, R.ba_r)
    g2 = jnp.sum(grad_in * xhat, axis=0, keepdims=True)
    cg = _dot(route.own_hot.astype(F32) * gl, R.mi[...].astype(F32), 0, 0, TOP)
    all_tok = norm_parts(R.tok[...].astype(F32))[0]
    own_tok, own_inv = norm_parts(route.own(R.tok[...]))
    for cp in S.pending[: zs - 1]:
        cp.wait_recv()
    R.out[...] = route.unsort(R.sorted_out[...])
    for cp in S.pending[2 * (zs - 1) :]:
        cp.wait()
    total = R.stat_all[0]
    for n in range(1, fs * 4):
        total = total + R.stat_all[n]
    R.stat_out[...] = total
    for cp in gathers:
        cp.wait_recv()
    gb = route.unsort(R.sorted_gb[...])
    gct = jnp.transpose(nn(gb, R.wo[...])).astype(BF)
    dq = attend_back(gct, R.qt, R.kv, R.pt, R.near, R.away)
    swap = remote(R.away, R.away_in, R.k_s.at[0], R.k_r.at[0], sibling)
    swap.start()
    og = tn(gb, R.ctx[...])
    swap.wait_recv()
    R.far_out[...] = (R.near[1] + R.away_in[1]).astype(BF)
    cross = remote(R.far_out, R.far_in, R.k_s.at[1], R.k_r.at[1], across)
    cross.start()
    normed = R.normed[...]
    mg = [tn(normed, dq), None, None]
    gq = nt(dq, R.w3[0])
    cross.wait_recv()
    kvg = (R.near[0] + R.away_in[0] + R.far_in[...].astype(F32)).astype(BF)
    partial_normed = gq + nt(kvg[:, :k], R.w3[1]) + nt(kvg[:, k:], R.w3[2])
    R.gn[...] = route.sort(partial_normed.astype(BF))
    scat = []
    for s, peer in enumerate(z_peers(zs)):
        cp = remote(R.gn.at[span(lax.rem(z + s + 1, zs), m)], R.gn_in.at[s], R.bs_s.at[s], R.bs_r.at[s], peer)
        cp.start()
        scat.append(cp)
    mg[1] = tn(normed, kvg[:, :k])
    mg[2] = tn(normed, kvg[:, k:])
    g1 = jnp.sum(partial_normed * all_tok, axis=0, keepdims=True)
    dense = R.dense
    last = dense.shape[3] - TAB
    small = jnp.concatenate([cg, g1, g2, jnp.zeros((TAB - EXP - 2, d), F32)], axis=0)
    for s in range(4 * fs):
        at = (s // 4, s % 4 // 2, s % 2)
        lo = s * rows
        for j in range(3):
            dense[at[0], at[1], at[2], 0:rows, j * k : (j + 1) * k] = mg[j][lo : lo + rows, :]
        dense[at[0], at[1], at[2], 0:rows, 3 * k : 4 * k] = og[lo : lo + rows, :]
        dense[at[0], at[1], at[2], last : last + TAB, 0:rows] = small[:, lo : lo + rows]
    pair = remote(dense.at[:, :, 1 - c], R.dense_in, R.k_s.at[2], R.k_r.at[2], sibling)
    pair.start()
    pair.wait_recv()
    shares = []
    for s, (fp, yp, peer, _) in enumerate(same):
        R.give[s] = (dense[fp, yp, c] + R.dense_in[fp, yp]).astype(BF)
        cp = remote(R.give.at[s], R.taken.at[s], R.bg_s.at[s], R.bg_r.at[s], peer)
        cp.start()
        shares.append(cp)
    total = R.gn[span(z, m), :].astype(F32)
    for s, cp in enumerate(scat):
        cp.wait_recv()
        total = total + R.gn_in[s].astype(F32)
    tg = grad + norm_back(total, own_tok, own_inv, R.table[EXP : EXP + 1, :].astype(F32))
    R.sorted_tg[span(z, m), :] = tg.astype(BF)
    ends = gather_z(zs, R.sorted_tg, m, R.bt_s, R.bt_r)
    kept = dense[f, y, c] + R.dense_in[f, y]
    for s, cp in enumerate(shares):
        cp.wait_recv()
        kept = kept + R.taken[s].astype(F32)
    R.sm[...] = kept[last:, :128]
    smalls = []
    for s, peer in enumerate(z_peers(zs)):
        cp = remote(R.sm, R.sm_in.at[s], R.v_s.at[s], R.v_r.at[s], peer)
        cp.start()
        smalls.append(cp)
    for j in range(3):
        R.mix_out[j] = kept[:rows, j * k : (j + 1) * k]
    R.og_out[...] = jnp.transpose(kept[:rows, 3 * k :])
    for keep, give in S.exports:
        keep.wait()
        give.wait()
    for cp in ends:
        cp.wait_recv()
    R.tg_out[...] = route.unsort(R.sorted_tg[...])
    total = R.sm[...]
    for s, cp in enumerate(smalls):
        cp.wait_recv()
        total = total + R.sm_in[s]
    R.sm_out[...] = total
    for cp in S.waits + gathers + [swap, cross, pair] + scat + shares + ends + smalls:
        cp.wait_send()

    @pl.loop(0, R.wu.shape[0])
    def _(e):
        S.two.settle(e)


def layer_body(names, fs, zs, gather, rows, *refs):
    R = SimpleNamespace(**dict(zip(names, refs)))
    S = head(R, fs, zs, gather)
    grad_back = middle(R, S, fs, zs)
    back(R, S, grad_back, fs, zs, rows)


def per_device(tokens, mixing_weight, output_weight, first_gain, second_gain, centroids, expert_up,
               expert_down, prefix_length, assignment, validity, teacher, cotangent):
    fs, zs = lax.axis_size("fsdp"), lax.axis_size("tp")
    c = lax.rem(lax.axis_index("ctx"), 2)
    n, d = tokens.shape[1], tokens.shape[2]
    rows, k = mixing_weight.shape[0], mixing_weight.shape[2]
    local_experts, width, units = expert_up.shape
    half = local_experts // 2
    experts = centroids.shape[0]
    sources = fs * 4
    heads = k // HD
    dma = pltpu.SemaphoreType.DMA
    per = CAP // zs
    m = n // zs
    r = half * per
    dh = d // 2
    own_rows = sources * per
    slots_in = sources * CAP
    others = 2 * fs - 1
    smem = pl.BlockSpec(memory_space=pltpu.SMEM)
    anyspec = pl.BlockSpec(memory_space=ANY)

    mixing = mixing_weight.transpose(1, 0, 2)
    ins = [("prefix", prefix_length, smem), ("tok", tokens[0], vspec()), ("chosen", assignment.reshape(1, n), vspec()),
           ("tea", teacher[0], vspec()), ("cot", cotangent[0], vspec()),
           ("up", expert_up, anyspec), ("dn", expert_down.transpose(0, 2, 1), anyspec)]
    scratch = []
    weights = [("w3", (3, d, k), BF), ("wo", (d, k), BF), ("table", (TAB, d), BF), ("valid", (sources, n), F32)]
    gather = rows % 16 == 0
    if gather:
        ins += [("mix", mixing, vspec()), ("ow", output_weight, vspec()), ("cent", centroids, vspec()),
                ("gain1", first_gain.reshape(1, rows), vspec()), ("gain2", second_gain.reshape(1, rows), vspec()),
                ("here", validity, vspec())]
        scratch += weights
        scratch += [("small", (TAB, n), F32), ("small_all", (sources, TAB, n), BF)]
        scratch += [(v, (others + w, 4), dma) for v, w in (("p_s", 0), ("p_r", 0), ("q_s", 1), ("q_r", 1))]
    else:
        small = jnp.concatenate(
            [
                jnp.pad(jnp.concatenate([centroids, first_gain[None], second_gain[None]]), ((0, 0), (0, n - rows))),
                validity.astype(BF),
                jnp.zeros((TAB - experts - 3, n), BF),
            ]
        )
        everyone = ("fsdp", "ctx")
        table = lax.all_gather(small, everyone, axis=0)
        full = (
            lax.all_gather(mixing, everyone, axis=1, tiled=True),
            lax.all_gather(output_weight, everyone, axis=1, tiled=True).T,
            table[:, :, :rows].transpose(1, 0, 2).reshape(TAB, d),
            table[:, experts + 2, :].astype(F32),
        )
        ins += [(w[0], v, vspec()) for w, v in zip(weights, full)]
    hidden, received, left = (half, slots_in, units), (half, slots_in, dh), (half, width, slots_in)
    outs = [(name, shape, BF, anyspec) for name, shape in (
        ("xt_own", left), ("xt_sib", left), ("act_own", hidden), ("act_sib", hidden),
        ("gxt_own", left), ("gxt_sib", left), ("gh_own", hidden), ("gh_sib", hidden))]
    outs += [("tg_out", (n, d), BF, vspec()), ("out", (n, d), BF, vspec()), ("mix_out", (3, rows, k), F32, vspec()),
             ("og_out", (k, rows), F32, vspec()), ("sm_out", (TAB, 128), F32, vspec()), ("stat_out", (8, 128), F32, vspec())]
    piece = (rows + (-rows % 16) + TAB, 4 * k)
    slots = (fs, 2, 2, r)
    scratch += [
        ("normed", (n, d), BF), ("qt", (k, n), BF), ("kv", (4, n, 2 * k), BF), ("pt", (heads, 4, n, n), BF),
        ("scores", (heads, 4, n, n), F32), ("ctx", (n, k), BF), ("branch", (n, d), BF), ("parts", (zs - 1, m, d), BF),
        ("res", (m, d), F32), ("mi", (m, d), BF), ("slots", slots + (dh,), BF), ("slots_g", slots + (dh + 128,), BF),
        ("wu", (half, dh, units), BF), ("wd", (half, dh, units), BF), ("gp", hidden, BF),
        ("act", hidden, BF), ("gh", hidden, BF), ("x", received, BF), ("gx", received, BF),
        ("xt", (half, dh, slots_in), BF), ("gxt", (half, dh, slots_in), BF),
        ("rq", (sources, r, dh), BF), ("rg", (sources, r, dh + 128), BF), ("grads", (half, own_rows, dh + 128), BF),
        ("results", (half, own_rows, dh), BF), ("xg", (half, own_rows, dh), BF), ("xg_back", (half, own_rows, dh), BF),
        ("ret", (sources, r, dh), BF), ("ret_back", (sources, r, dh), BF),
        ("rb", (sources, r, dh), BF), ("rb_back", (sources, r, dh), BF),
        ("sorted_out", (n, d), BF), ("stat", (8, 128), F32), ("stat_in", (zs - 1, 8, 128), F32),
        ("stat_all", (sources, 8, 128), F32),
        ("ps", hidden, BF), ("pr", hidden, BF), ("pr_back", hidden, BF), ("rows", received, BF),
        ("rin", (half, zs - 1, own_rows, dh), BF), ("gm", (m, d), F32), ("gl", (m, 1), F32),
        ("sorted_gb", (n, d), BF), ("near", (2, n, 2 * k), F32), ("away", (2, n, 2 * k), F32),
        ("away_in", (2, n, 2 * k), F32), ("far_out", (n, 2 * k), BF), ("far_in", (n, 2 * k), BF), ("gn", (n, d), BF),
        ("gn_in", (zs - 1, m, d), BF), ("sorted_tg", (n, d), BF), ("dense", (fs, 2, 2) + piece, F32),
        ("dense_in", (fs, 2) + piece, F32), ("give", (others,) + piece, BF), ("taken", (others,) + piece, BF),
        ("sm", (TAB, 128), F32), ("sm_in", (zs - 1, TAB, 128), F32),
    ]
    for name, shape in (("hz", (zs - 1,)), ("wx", (2,)), ("kv", (3,)), ("d", (sources - 1,)), ("g", (sources - 1,)),
                        ("b", (sources - 1,)), ("c", (sources - 1,)), ("u", (sources - 1,)), ("o", (zs - 1,)),
                        ("t", (zs - 1,)), ("e", (4,)), ("ba", (zs - 1,)), ("bs", (zs - 1,)), ("bt", (zs - 1,)),
                        ("v", (zs - 1,)), ("k", (3,)), ("bg", (others,)),
                        ("one_a", (half, zs - 1)), ("one_x", (half,)), ("one_r", (half, zs - 1)),
                        ("two_a", (half, zs - 1)), ("two_x", (half,)), ("two_r", (half, zs - 1))):
        scratch += [(name + "_s", shape, dma), (name + "_r", shape, dma)]
    scratch += [("wsem", (6,), dma), ("l_s", (4,), dma)]
    names = [v[0] for v in ins] + [v[0] for v in outs] + [v[0] for v in scratch]
    results = pl.pallas_call(
        partial(layer_body, names, fs, zs, gather, rows),
        out_shape=[sds(v[1], v[2]) for v in outs],
        in_specs=[v[2] for v in ins],
        out_specs=[v[3] for v in outs],
        scratch_shapes=[dma(v[1]) if v[2] is dma else VMEM(v[1], v[2]) for v in scratch],
        compiler_params=params(1, 60),
        name="layer",
    )(*[v[1] for v in ins])
    xt, xt_x, act, act_x, gxt, gxt_x, gh, gh_x = results[:8]
    shapes = [sds((n, d), BF), sds((n, d), BF), sds((3, rows, k), F32), sds((k, rows), F32),
              sds((experts, rows), F32), sds((1, rows), F32), sds((1, rows), F32)]
    up, down, tokens_gradient, activations, mix_part, out_part, cen_part, g1, g2, balance, distill = finish(
        c, n * sources, (xt, gh, xt_x, gh_x, gxt, act, gxt_x, act_x), results[8:], shapes
    )
    return (
        activations[None],
        tokens_gradient[None],
        mix_part.transpose(1, 0, 2),
        out_part,
        g1.reshape(rows),
        g2.reshape(rows),
        cen_part,
        up.reshape(local_experts, width, units),
        down.reshape(local_experts, width, units).transpose(0, 2, 1),
        balance.reshape(()),
        distill.reshape(()),
    )


def solution(mesh):
    in_specs = (
        P("fsdp", "ctx", None),
        P(("fsdp", "ctx"), None, "tp"),
        P("tp", ("fsdp", "ctx")),
        P(("fsdp", "ctx")),
        P(("fsdp", "ctx")),
        P(None, ("fsdp", "ctx")),
        P("fsdp", "ctx", "tp"),
        P("fsdp", "tp", "ctx"),
        P("fsdp"),
        P("fsdp", "ctx", None),
        P("fsdp", "ctx"),
        P("fsdp", "ctx", None),
        P("fsdp", "ctx", None),
    )
    out_specs = (
        P("fsdp", "ctx", None),
        P("fsdp", "ctx", None),
        P(("fsdp", "ctx"), None, "tp"),
        P("tp", ("fsdp", "ctx")),
        P(("fsdp", "ctx")),
        P(("fsdp", "ctx")),
        P(None, ("fsdp", "ctx")),
        P("fsdp", "ctx", "tp"),
        P("fsdp", "tp", "ctx"),
        P(),
        P(),
    )
    return jax.shard_map(
        per_device, mesh=mesh, in_specs=in_specs, out_specs=out_specs, check_vma=False
    )
```

time: 226 us -> 195 us (0.86)
  Pallas kernels: 209 us -> 193 us
  local copies, waits for them, and re-layouts: 8.34 us -> 0 us
  other arithmetic: 3.46 us -> 0 us
    pallas_call x4 -> x2, Pallas kernels: 209 us -> 193 us  [the longest x1 182 us: per_device(): pl.pallas_call(partial(layer_body, names, fs, zs, gather, rows), out_shap...]
    unnamed x16 -> x0, local copies, waits for them, and re-layouts: 4.49 us -> none
    slice x2 -> x0, local copies, waits for them, and re-layouts: 2.5 us -> none  [the longest x1 1.32 us: per_device(): small_part[:experts, :rows]]
  transfers between devices with their start and end apart: 4 -> 0, of which waited for: 0 -> 0; matrix products, arithmetic and copies ran while one was open for 2% -> 0% of each run, Pallas kernels for 22% -> 0%
where the time goes in v5:
time: 195 us
  Pallas kernels  193 us (99%)
    pallas_call x1, Pallas kernels, per_device(): pl.pallas_call(partial(layer_body, names, fs, zs, gather, rows), out_shap...  182 us
    pallas_call x1, Pallas kernels, finish(): pl.pallas_call(partial(finish_body, float(tokens)), grid_spec=pltpu.Prefe...  11.6 us

profile of v5, /device:TPU:0, one launch (start us, length us, event | category | flops | bytes accessed | tf_op | source)
XLA Modules:
  0.0 194.6 jit_solution(8637481563101225010)
XLA Ops:
  1.3 181.5 %layer.1 = (bf16[8,192,128]{2,1,0:T(8,128)(2,1)}, bf16[8,192,128]{2,1,0:T(8,128)(2,1)}, bf16[8,128,768]{2,1,0:T(8,128)(2,1)}, bf16[8,128,768]{2,1,0:T(8,128)(2,1...) custom-call(s32[1]{0:T(128)S(6)} %copy.24.refs_0_, ...), custom_call_target="tpu_custom_call" | custom-call | tf_op jit(solution)/shard_map/layer/pallas_call | solution.py:933
  182.8 11.6 %finish.1 = (f32[2,8,192,768]{3,2,1,0:T(8,128)}, f32[2,8,192,768]{3,2,1,0:T(8,128)}, bf16[256,768]{1,0:T(8,128)(2,1)}, bf16[256,768]{1,0:T(8,128)(2,1)}, f32[3,9...) custom-call(s32[1]{0:T(128)} %bitcast.c_ref, ...), custom_call_target="tpu_custom_call" | custom-call | tf_op jit(solution)/shard_map/finish/pallas_call | solution.py:303

commit v6 on v5

--- a/solution.py
+++ b/solution.py
@@ -91,6 +91,10 @@
 
 def shifted(v, by):
     return lax.shift_right_logical(v, by)
+
+
+def owners(zs):
+    return sorted(range(1, zs), key=lambda s: (-min(s, zs - s), s)) + [0]
 
 
 class Route:
@@ -106,15 +110,22 @@
         owner = rank - zs * turn
         owned = (owner == iota((n, zs), 1).astype(F32)).astype(BF)
         place = jnp.sum(nn(lower, owned) * owned.astype(F32), axis=1, keepdims=True)
-        self.at = owner * m + place
+        ahead = owner - lax.convert_element_type(z, F32)
+        ahead = jnp.where(ahead < 0, ahead + zs, ahead)
+        order = sum(jnp.where(ahead == step, float(k), 0.0) for k, step in enumerate(owners(zs)))
+        self.at = order * m + place
         self.at_row = to_row(self.at)
-        mine = iota((m, n), 0).astype(F32) + lax.convert_element_type(z * m, F32) == self.at_row
+        mine = iota((m, n), 0).astype(F32) + float((zs - 1) * m) == self.at_row
         self.mine = mine.astype(BF)
         self.mine_mask = mine
         self.slot = self.own_col(to_row(chosen * per + turn))
         self.own_hot = nn(self.mine, self.hot).astype(BF)
         self.slots = EXP * per
         self.n, self.m, self.width = n, m, width
+
+    def positions(self):
+        n = self.n
+        return jnp.sum(jnp.where(self.at == iota((n, n), 1).astype(F32), iota((n, n), 0).astype(F32), 0.0), axis=0, keepdims=True)
 
     def own_col(self, row):
         return jnp.sum(jnp.where(self.mine_mask, row, 0.0), axis=1, keepdims=True)
@@ -169,27 +180,39 @@
     )
 
 
-def scatter_z(zs, x_ref, parts, send, recv):
-    z = lax.axis_index("tp")
-    n = x_ref.shape[0] // zs
+class Scatter:
+    def __init__(self, zs, x_ref, parts, send, recv):
+        self.zs, self.x_ref, self.parts, self.send, self.recv = zs, x_ref, parts, send, recv
+        self.m = x_ref.shape[0] // zs
+        self.copies = []
+
+    def start(self, lo, hi):
+        peers = z_peers(self.zs)
+        for k, step in list(enumerate(owners(self.zs)))[lo:hi]:
+            if step:
+                cp = remote(
+                    self.x_ref.at[pl.ds(k * self.m, self.m)], self.parts.at[step - 1],
+                    self.send.at[step - 1], self.recv.at[step - 1], peers[step - 1],
+                )
+                cp.start()
+                self.copies.append((step, cp))
+
+    def finish(self):
+        total = self.x_ref[pl.ds((self.zs - 1) * self.m, self.m), :].astype(F32)
+        for step, cp in sorted(self.copies, key=lambda v: v[0]):
+            cp.wait_recv()
+            total = total + self.parts[step - 1].astype(F32)
+        return total
+
+
+def gather_z(zs, x_ref, m, send, recv):
     copies = []
+    order = owners(zs)
     for s, peer in enumerate(z_peers(zs)):
-        to = lax.rem(z + s + 1, zs)
-        cp = remote(x_ref.at[span(to, n)], parts.at[s], send.at[s], recv.at[s], peer)
-        cp.start()
-        copies.append(cp)
-    total = x_ref[span(z, n), :].astype(F32)
-    for s, cp in enumerate(copies):
-        cp.wait_recv()
-        total = total + parts[s].astype(F32)
-    return total, copies
-
-
-def gather_z(zs, x_ref, n, send, recv):
-    z = lax.axis_index("tp")
-    copies = []
-    for s, peer in enumerate(z_peers(zs)):
-        cp = remote(x_ref.at[span(z, n)], x_ref.at[span(z, n)], send.at[s], recv.at[s], peer)
+        to = order.index(zs - s - 1)
+        cp = remote(
+            x_ref.at[pl.ds((zs - 1) * m, m)], x_ref.at[pl.ds(to * m, m)], send.at[s], recv.at[s], peer
+        )
         cp.start()
         copies.append(cp)
     return copies
@@ -214,57 +237,76 @@
     return out
 
 
-def attend(mine, prefix, offsets, qt_ref, kv_ref, valid_ref, row0, pt_ref, sc_ref, arrive):
-    k, n = qt_ref.shape
-    heads = k // HD
-    query = iota((n, n), 1) + mine * n
-    for j in (0, 2, 1, 3):
-        if j == 1:
-            arrive()
-        key = iota((n, n), 0) + offsets[j] * n
-        col = to_col(valid_ref[pl.ds(row0 + offsets[j], 1), :])
+class Attention:
+    def __init__(self, R, mine, offsets, row0, positions):
+        self.R = R
+        self.k, self.n = R.qt.shape
+        self.heads = self.k // HD
+        self.offsets, self.row0 = offsets, row0
+        self.query = positions + lax.convert_element_type(mine * self.n, F32)
+
+    def lanes(self, half):
+        return slice(half * (self.n // 2), (half + 1) * (self.n // 2))
+
+    def scores(self, half, j):
+        R, at, w = self.R, self.lanes(half), self.n // 2
+        key = (iota((self.n, w), 0) + self.offsets[j] * self.n).astype(F32)
+        col = to_col(R.valid[pl.ds(self.row0 + self.offsets[j], 1), :])
+        query = self.query[:, at]
+        prefix = lax.convert_element_type(R.prefix[0], F32)
         allowed = ((key <= query) | (key < prefix)) & ((col > 0.5) | (key == query))
-        for h in range(heads):
+        for h in range(self.heads):
             lo = h * HD
-            scores = nn(kv_ref[j, :, lo : lo + HD], qt_ref[lo : lo + HD, :]) * (1.0 / math.sqrt(HD))
-            sc_ref[h, j] = jnp.where(allowed, scores, -1e30)
-    outs = []
-    for h in range(heads):
-        lo = h * HD
-        top = jnp.max(sc_ref[h, 0], axis=0, keepdims=True)
-        for j in range(1, 4):
-            top = jnp.maximum(top, jnp.max(sc_ref[h, j], axis=0, keepdims=True))
-        exps = [jnp.exp(sc_ref[h, j] - top) for j in range(4)]
-        share = 1.0 / sum(jnp.sum(e, axis=0, keepdims=True) for e in exps)
-        acc = jnp.zeros((HD, n), F32)
-        for j in range(4):
-            w = (exps[j] * share).astype(BF)
-            pt_ref[h, j] = w
-            acc = acc + tn(kv_ref[j, :, k + lo : k + lo + HD], w)
-        outs.append(acc)
-    return jnp.transpose(jnp.concatenate(outs, axis=0)).astype(BF)
-
-
-def attend_back(gct, qt_ref, kv_ref, pt_ref, near_ref, away_ref):
-    k, n = qt_ref.shape
-    scale = 1.0 / math.sqrt(HD)
-    dqs = []
-    for h in range(k // HD):
-        lo = h * HD
-        dot_ = gct[lo : lo + HD, :]
-        qt = qt_ref[lo : lo + HD, :]
-        ws = [pt_ref[h, j] for j in range(4)]
-        dps = [nn(kv_ref[j, :, k + lo : k + lo + HD], dot_) for j in range(4)]
-        mean = sum(jnp.sum(ws[j].astype(F32) * dps[j], axis=0, keepdims=True) for j in range(4))
-        dq = jnp.zeros((HD, n), F32)
-        for j in range(4):
-            ds = (ws[j].astype(F32) * (dps[j] - mean)).astype(BF)
-            dq = dq + tn(kv_ref[j, :, lo : lo + HD], ds)
-            target = near_ref if j < 2 else away_ref
-            target[j % 2, :, lo : lo + HD] = nt(ds, qt) * scale
-            target[j % 2, :, k + lo : k + lo + HD] = nt(ws[j], dot_)
-        dqs.append(dq * scale)
-    return jnp.transpose(jnp.concatenate(dqs, axis=0)).astype(BF)
+            scores = nn(R.kv[j, :, lo : lo + HD], R.qt[lo : lo + HD, at]) * (1.0 / math.sqrt(HD))
+            R.scores[h, j, :, at] = jnp.where(allowed, scores, -1e30)
+
+    def context(self, half):
+        R, at, w, k = self.R, self.lanes(half), self.n // 2, self.k
+        outs = []
+        for h in range(self.heads):
+            lo = h * HD
+            top = jnp.max(R.scores[h, 0, :, at], axis=0, keepdims=True)
+            for j in range(1, 4):
+                top = jnp.maximum(top, jnp.max(R.scores[h, j, :, at], axis=0, keepdims=True))
+            exps = [jnp.exp(R.scores[h, j, :, at] - top) for j in range(4)]
+            share = 1.0 / sum(jnp.sum(e, axis=0, keepdims=True) for e in exps)
+            acc = jnp.zeros((HD, w), F32)
+            for j in range(4):
+                weights = (exps[j] * share).astype(BF)
+                R.pt[h, j, :, at] = weights
+                acc = acc + tn(R.kv[j, :, k + lo : k + lo + HD], weights)
+            outs.append(acc)
+        return jnp.transpose(jnp.concatenate(outs, axis=0)).astype(BF)
+
+    def back(self, half, gct, fresh, made):
+        R, at, k = self.R, self.lanes(half), self.k
+        scale = 1.0 / math.sqrt(HD)
+        means, dqs = [], []
+        for h in range(self.heads):
+            lo = h * HD
+            mean = 0.0
+            for j in range(4):
+                dp = nn(R.kv[j, :, k + lo : k + lo + HD], gct[lo : lo + HD, :])
+                R.scores[h, j, :, at] = dp
+                mean = mean + jnp.sum(R.pt[h, j, :, at].astype(F32) * dp, axis=0, keepdims=True)
+            means.append(mean)
+            dqs.append(jnp.zeros((HD, self.n // 2), F32))
+        for j in (3, 1, 2, 0):
+            target = R.near if j < 2 else R.away
+            for h in range(self.heads):
+                lo = h * HD
+                w = R.pt[h, j, :, at]
+                ds = (w.astype(F32) * (R.scores[h, j, :, at] - means[h])).astype(BF)
+                dqs[h] = dqs[h] + tn(R.kv[j, :, lo : lo + HD], ds)
+                dk = nt(ds, R.qt[lo : lo + HD, at]) * scale
+                dv = nt(w, gct[lo : lo + HD, :])
+                if not fresh:
+                    dk = dk + target[j % 2, :, lo : lo + HD]
+                    dv = dv + target[j % 2, :, k + lo : k + lo + HD]
+                target[j % 2, :, lo : lo + HD] = dk
+                target[j % 2, :, k + lo : k + lo + HD] = dv
+            made(j)
+        return jnp.concatenate(dqs, axis=0) * scale
 
 
 def finish_body(scalars, c_ref, *refs):
@@ -505,29 +547,36 @@
             for m in (2, 3):
                 relays[n_, m].wait_recv()
         waits += list(sends.values()) + list(relays.values())
-    R.qt[...] = jnp.transpose(nn(normed, R.w3[0])).astype(BF)
     route = Route(R.chosen[...], zs, z, d)
+    R.qt[...] = jnp.transpose(route.sort(nn(normed, R.w3[0]).astype(BF)).astype(F32)).astype(BF)
     teacher, cotangent = route.own(R.tea[...]), route.own(R.cot[...])
+    own_tokens = route.own(R.tok[...])
     own_valid = route.own_col(R.valid[pl.ds(me, 1), :])
     scale = 1.0 / (jnp.sum(R.valid[...]) * d)
     sib.wait_recv()
-    last = []
-
-    def arrive():
-        far.wait_recv()
-        cp = remote(R.kv.at[1], R.kv.at[3], R.kv_s.at[2], R.kv_r.at[2], sibling)
-        cp.start()
-        for swap in swaps:
-            swap.start()
-        cp.wait_recv()
-        last.append(cp)
-
     offsets = [i, (1 - y) * 2 + c, y * 2 + 1 - c, (1 - y) * 2 + 1 - c]
-    ctx = attend(i, R.prefix[0], offsets, R.qt, R.kv, R.valid, f * 4, R.pt, R.scores, arrive)
-    R.ctx[...] = ctx
-    R.branch[...] = route.sort(nt(ctx, R.wo[...]).astype(BF))
-    total, sums = scatter_z(zs, R.branch, R.parts, R.hz_s, R.hz_r)
-    residual = route.own(R.tok[...]) + total
+    attention = Attention(R, i, offsets, f * 4, route.positions())
+    for j in (0, 2):
+        for half_ in range(2):
+            attention.scores(half_, j)
+    far.wait_recv()
+    last = remote(R.kv.at[1], R.kv.at[3], R.kv_s.at[2], R.kv_r.at[2], sibling)
+    last.start()
+    for swap in swaps:
+        swap.start()
+    attention.scores(0, 1)
+    attention.scores(1, 1)
+    last.wait_recv()
+    sums = Scatter(zs, R.branch, R.parts, R.hz_s, R.hz_r)
+    n = R.tok.shape[0]
+    for half_ in range(2):
+        attention.scores(half_, 3)
+        rows_ = pl.ds(half_ * (n // 2), n // 2)
+        ctx = attention.context(half_)
+        R.ctx[rows_, :] = ctx
+        R.branch[rows_, :] = nt(ctx, R.wo[...]).astype(BF)
+        sums.start(half_ * (zs // 2), (half_ + 1) * (zs // 2))
+    residual = own_tokens + sums.finish()
     R.res[...] = residual
     xhat, _ = norm_parts(residual)
     mixed_in = (xhat * R.table[EXP + 1 : EXP + 2, :].astype(F32)).astype(BF)
@@ -535,13 +584,26 @@
     logit = jnp.sum(mixed_in.astype(F32) * nn(route.own_hot, R.table[0:EXP, :]), axis=-1, keepdims=True)
     gate = jax.nn.sigmoid(logit)
     route.fill(mixed_in, R.slots)
+    sends = dispatch(fs, R.slots, R.rq, R.d_s, R.d_r, R.wsem.at[2])
     weight = 2.0 * own_valid * scale
     known = gate * (cotangent + weight * (residual - teacher))
     slope = jnp.broadcast_to(gate * gate * weight, (known.shape[0], 128))
     route.fill(jnp.concatenate([known, slope], axis=1).astype(BF), R.slots_g)
-    waits += swaps + sums + [far, sib] + last
-    return SimpleNamespace(route=route, gate=gate, teacher=teacher, cotangent=cotangent, valid=own_valid, scale=scale,
+    sends_g = dispatch(fs, R.slots_g, R.rg, R.g_s, R.g_r, R.wsem.at[3])
+    waits += swaps + [v[1] for v in sums.copies] + [far, sib, last]
+    return SimpleNamespace(route=route, attention=attention, own_tokens=own_tokens, sends=sends, sends_g=sends_g, gate=gate, teacher=teacher, cotangent=cotangent, valid=own_valid, scale=scale,
                            loads=loads, swaps=swaps, waits=waits)
+
+
+def dispatch(fs, src, dst, send, recv, own_sem):
+    f, i, z, y, c = whereabouts()
+    me = f * 4 + i
+    copies = [pltpu.make_async_copy(src.at[f, y, c], dst.at[me], own_sem)]
+    for k, (fp, yp, cp_, peer) in enumerate(group_peers(fs)):
+        copies.append(remote(src.at[fp, yp, cp_], dst.at[me], send.at[k], recv.at[k], peer))
+    for cp in copies:
+        cp.start()
+    return copies
 
 
 def same_core(fs):
@@ -566,18 +628,6 @@
     sibling = (f, y * 2 + 1 - c, z)
     own = pl.ds(pl.multiple_of(c * width, 64), width)
     other = pl.ds(pl.multiple_of((1 - c) * width, 64), width)
-    keeps = [
-        pltpu.make_async_copy(R.slots.at[f, y, c], R.rq.at[me], R.wsem.at[2]),
-        pltpu.make_async_copy(R.slots_g.at[f, y, c], R.rg.at[me], R.wsem.at[3]),
-    ]
-    for cp in keeps:
-        cp.start()
-    sends, sends_g = [], []
-    for out, src, dst, send, recv in ((sends, R.slots, R.rq, R.d_s, R.d_r), (sends_g, R.slots_g, R.rg, R.g_s, R.g_r)):
-        for k, (fp, yp, cp_, peer) in enumerate(group):
-            cp = remote(src.at[fp, yp, cp_], dst.at[me], send.at[k], recv.at[k], peer)
-            cp.start()
-            out.append(cp)
     sems = [[getattr(R, p + n) for n in ("a_s", "a_r", "x_s", "x_r", "r_s", "r_r")] for p in ("one_", "two_")]
     one = Pass(False, zs, R.wu, R.wd, R.xg, R.x, R.ps, R.pr, R.act, R.gp, R.rows, R.rin, sems[0])
     two = Pass(True, zs, R.wd, R.wu, R.xg_back, R.gx, R.ps, R.pr_back, R.gh, R.gp, R.rows, R.rin, sems[1])
@@ -595,9 +645,7 @@
         cp.wait()
     for cp in S.swaps:
         cp.wait_recv()
-    keeps[0].wait()
-    for cp in sends:
-        cp.wait_recv()
+    arrived((S.sends[0], S.sends[1:]))
     rows = nn(order, R.rq[...].reshape(sources * r, dh)).astype(BF).reshape(half, m, dh)
     for e in range(half):
         one.spread(e, rows[e])
@@ -611,9 +659,7 @@
     def _(e):
         R.xt[e] = jnp.transpose(R.x[e])
 
-    keeps[1].wait()
-    for cp in sends_g:
-        cp.wait_recv()
+    arrived((S.sends_g[0], S.sends_g[1:]))
     R.grads[...] = nn(order, R.rg[...].reshape(sources * r, dh + 128)).astype(BF).reshape(half, m, dh + 128)
     export(0, R.xt.at[:, own, :], R.xt_own, R.xt.at[:, other, :], R.xt_sib)
 
@@ -662,7 +708,7 @@
         diff = mixed - S.teacher
         weighted = S.valid * diff
         grad = S.cotangent + 2.0 * weighted * S.scale
-        R.sorted_out[span(z, n), :] = mixed.astype(BF)
+        R.sorted_out[pl.ds((zs - 1) * n, n), :] = mixed.astype(BF)
         pending.extend(gather_z(zs, R.sorted_out, n, R.o_s, R.o_r))
         hot = S.route.own_hot.astype(F32)
         R.stat[...] = jnp.zeros_like(R.stat)
@@ -714,7 +760,7 @@
     export(2, R.gxt.at[:, own, :], R.gxt_own, R.gxt.at[:, other, :], R.gxt_sib)
     export(3, R.gh, R.gh_own, R.gh, R.gh_sib)
     S.pending, S.exports = pending, exports
-    S.waits += pending[: 2 * (zs - 1)] + sends + sends_g + given[1] + given_back[1]
+    S.waits += pending[: 2 * (zs - 1)] + S.sends[1:] + S.sends_g[1:] + given[1] + given_back[1]
     S.two = two
     arrived(given_back)
     return S.route.collect(R.rb_back)
@@ -732,12 +778,12 @@
     m, d = grad_in.shape
     xhat, inv = norm_parts(R.res[...])
     grad = R.gm[...] + norm_back(grad_in, xhat, inv, R.table[EXP + 1 : EXP + 2, :].astype(F32))
-    R.sorted_gb[span(z, m), :] = grad.astype(BF)
+    R.sorted_gb[pl.ds((zs - 1) * m, m), :] = grad.astype(BF)
     gathers = gather_z(zs, R.sorted_gb, m, R.ba_s, R.ba_r)
     g2 = jnp.sum(grad_in * xhat, axis=0, keepdims=True)
     cg = _dot(route.own_hot.astype(F32) * gl, R.mi[...].astype(F32), 0, 0, TOP)
-    all_tok = norm_parts(R.tok[...].astype(F32))[0]
-    own_tok, own_inv = norm_parts(route.own(R.tok[...]))
+    all_tok = norm_parts(route.sort(R.tok[...]).astype(F32))[0]
+    own_tok, own_inv = norm_parts(S.own_tokens)
     for cp in S.pending[: zs - 1]:
         cp.wait_recv()
     R.out[...] = route.unsort(R.sorted_out[...])
@@ -747,30 +793,43 @@
     for n in range(1, fs * 4):
         total = total + R.stat_all[n]
     R.stat_out[...] = total
-    for cp in gathers:
-        cp.wait_recv()
-    gb = route.unsort(R.sorted_gb[...])
-    gct = jnp.transpose(nn(gb, R.wo[...])).astype(BF)
-    dq = attend_back(gct, R.qt, R.kv, R.pt, R.near, R.away)
-    swap = remote(R.away, R.away_in, R.k_s.at[0], R.k_r.at[0], sibling)
-    swap.start()
-    og = tn(gb, R.ctx[...])
-    swap.wait_recv()
-    R.far_out[...] = (R.near[1] + R.away_in[1]).astype(BF)
-    cross = remote(R.far_out, R.far_in, R.k_s.at[1], R.k_r.at[1], across)
-    cross.start()
+    n = R.tok.shape[0]
+    swaps = [remote(R.away.at[j], R.away_in.at[j], R.k_s.at[j], R.k_r.at[j], sibling) for j in range(2)]
+    cross = remote(R.far_out, R.far_in, R.k_s.at[2], R.k_r.at[2], across)
+
+    def nothing(j):
+        pass
+
+    def made(j):
+        if j == 3:
+            swaps[1].start()
+        if j == 1:
+            swaps[1].wait_recv()
+            R.far_out[...] = (R.near[1] + R.away_in[1]).astype(BF)
+            cross.start()
+        if j == 2:
+            swaps[0].start()
+
+    dqs = {}
+    for half, steps in ((1, (0,)), (0, range(1, zs - 1))):
+        for s in steps:
+            gathers[s].wait_recv()
+        gct = jnp.transpose(nn(R.sorted_gb[pl.ds(half * (n // 2), n // 2), :], R.wo[...])).astype(BF)
+        dqs[half] = S.attention.back(half, gct, half == 1, nothing if half == 1 else made)
+    dq = jnp.transpose(jnp.concatenate([dqs[0], dqs[1]], axis=1)).astype(BF)
     normed = R.normed[...]
-    mg = [tn(normed, dq), None, None]
     gq = nt(dq, R.w3[0])
+    mg = [tn(normed, route.unsort(dq)), None, None]
+    og = tn(R.sorted_gb[...], R.ctx[...])
+    swaps[0].wait_recv()
+    near = R.near[0] + R.away_in[0]
     cross.wait_recv()
-    kvg = (R.near[0] + R.away_in[0] + R.far_in[...].astype(F32)).astype(BF)
-    partial_normed = gq + nt(kvg[:, :k], R.w3[1]) + nt(kvg[:, k:], R.w3[2])
-    R.gn[...] = route.sort(partial_normed.astype(BF))
-    scat = []
-    for s, peer in enumerate(z_peers(zs)):
-        cp = remote(R.gn.at[span(lax.rem(z + s + 1, zs), m)], R.gn_in.at[s], R.bs_s.at[s], R.bs_r.at[s], peer)
-        cp.start()
-        scat.append(cp)
+    kvg = (near + R.far_in[...].astype(F32)).astype(BF)
+    kvs = route.sort(kvg)
+    partial_normed = gq + nt(kvs[:, :k], R.w3[1]) + nt(kvs[:, k:], R.w3[2])
+    R.gn[...] = partial_normed.astype(BF)
+    scat = Scatter(zs, R.gn, R.gn_in, R.bs_s, R.bs_r)
+    scat.start(0, zs)
     mg[1] = tn(normed, kvg[:, :k])
     mg[2] = tn(normed, kvg[:, k:])
     g1 = jnp.sum(partial_normed * all_tok, axis=0, keepdims=True)
@@ -784,7 +843,7 @@
             dense[at[0], at[1], at[2], 0:rows, j * k : (j + 1) * k] = mg[j][lo : lo + rows, :]
         dense[at[0], at[1], at[2], 0:rows, 3 * k : 4 * k] = og[lo : lo + rows, :]
         dense[at[0], at[1], at[2], last : last + TAB, 0:rows] = small[:, lo : lo + rows]
-    pair = remote(dense.at[:, :, 1 - c], R.dense_in, R.k_s.at[2], R.k_r.at[2], sibling)
+    pair = remote(dense.at[:, :, 1 - c], R.dense_in, R.k_s.at[3], R.k_r.at[3], sibling)
     pair.start()
     pair.wait_recv()
     shares = []
@@ -793,12 +852,9 @@
         cp = remote(R.give.at[s], R.taken.at[s], R.bg_s.at[s], R.bg_r.at[s], peer)
         cp.start()
         shares.append(cp)
-    total = R.gn[span(z, m), :].astype(F32)
-    for s, cp in enumerate(scat):
-        cp.wait_recv()
-        total = total + R.gn_in[s].astype(F32)
+    total = scat.finish()
     tg = grad + norm_back(total, own_tok, own_inv, R.table[EXP : EXP + 1, :].astype(F32))
-    R.sorted_tg[span(z, m), :] = tg.astype(BF)
+    R.sorted_tg[pl.ds((zs - 1) * m, m), :] = tg.astype(BF)
     ends = gather_z(zs, R.sorted_tg, m, R.bt_s, R.bt_r)
     kept = dense[f, y, c] + R.dense_in[f, y]
     for s, cp in enumerate(shares):
@@ -824,7 +880,7 @@
         cp.wait_recv()
         total = total + R.sm_in[s]
     R.sm_out[...] = total
-    for cp in S.waits + gathers + [swap, cross, pair] + scat + shares + ends + smalls:
+    for cp in S.waits + gathers + swaps + [cross, pair] + [v[1] for v in scat.copies] + shares + ends + smalls:
         cp.wait_send()
 
     @pl.loop(0, R.wu.shape[0])
@@ -924,7 +980,7 @@
     for name, shape in (("hz", (zs - 1,)), ("wx", (2,)), ("kv", (3,)), ("d", (sources - 1,)), ("g", (sources - 1,)),
                         ("b", (sources - 1,)), ("c", (sources - 1,)), ("u", (sources - 1,)), ("o", (zs - 1,)),
                         ("t", (zs - 1,)), ("e", (4,)), ("ba", (zs - 1,)), ("bs", (zs - 1,)), ("bt", (zs - 1,)),
-                        ("v", (zs - 1,)), ("k", (3,)), ("bg", (others,)),
+                        ("v", (zs - 1,)), ("k", (4,)), ("bg", (others,)),
                         ("one_a", (half, zs - 1)), ("one_x", (half,)), ("one_r", (half, zs - 1)),
                         ("two_a", (half, zs - 1)), ("two_x", (half,)), ("two_r", (half, zs - 1))):
         scratch += [(name + "_s", shape, dma), (name + "_r", shape, dma)]

time: 195 us -> 192 us (0.985)
  Pallas kernels: 193 us -> 190 us
    pallas_call x1, Pallas kernels: 182 us -> 179 us  [per_device(): pl.pallas_call(partial(layer_body, names, fs, zs, gather, rows), out_shap...]
where the time goes in v6:
time: 192 us
  Pallas kernels  190 us (99%)
    pallas_call x1, Pallas kernels, per_device(): pl.pallas_call(partial(layer_body, names, fs, zs, gather, rows), out_shap...  179 us
    pallas_call x1, Pallas kernels, finish(): pl.pallas_call(partial(finish_body, float(tokens)), grid_spec=pltpu.Prefe...  11.6 us

profile of v6, /device:TPU:0, one launch (start us, length us, event | category | flops | bytes accessed | tf_op | source)
XLA Modules:
  0.0 191.6 jit_solution(14992820000844189444)
XLA Ops:
  1.3 178.6 %layer.1 = (bf16[8,192,128]{2,1,0:T(8,128)(2,1)}, bf16[8,192,128]{2,1,0:T(8,128)(2,1)}, bf16[8,128,768]{2,1,0:T(8,128)(2,1)}, bf16[8,128,768]{2,1,0:T(8,128)(2,1...) custom-call(s32[1]{0:T(128)S(6)} %copy.24.refs_0_, ...), custom_call_target="tpu_custom_call" | custom-call | tf_op jit(solution)/shard_map/layer/pallas_call | solution.py:989
  179.9 11.6 %finish.1 = (f32[2,8,192,768]{3,2,1,0:T(8,128)}, f32[2,8,192,768]{3,2,1,0:T(8,128)}, bf16[256,768]{1,0:T(8,128)(2,1)}, bf16[256,768]{1,0:T(8,128)(2,1)}, f32[3,9...) custom-call(s32[1]{0:T(128)} %bitcast.c_ref, ...), custom_call_target="tpu_custom_call" | custom-call | tf_op jit(solution)/shard_map/finish/pallas_call | solution.py:345

commit v7 on v6

--- a/solution.py
+++ b/solution.py
@@ -498,6 +498,15 @@
     for cp in loads:
         cp.start()
     xhat, _ = norm_parts(R.tok[...].astype(F32))
+    others = []
+
+    def over_z(rows_, pair):
+        n_ = len(others) // (zs - 1)
+        for s, peer in enumerate(z_peers(zs)):
+            cp = remote(R.wo.at[rows_, :], R.wo_all.at[z, pair, c], R.wz_s.at[s, n_], R.wz_r.at[s, n_], peer)
+            cp.start()
+            others.append(cp)
+
     if gather:
 
         def places(at):
@@ -505,11 +514,12 @@
             return [R.w3.at[1:3, rows_, :], R.small_all.at[at], R.w3.at[0:1, rows_, :], R.wo.at[rows_, :]]
 
         sends = {}
-        for m, ref in enumerate(places(me)):
+        for m, ref in sorted(enumerate(places(me)), key=lambda v: (0, 1, 3, 2)[v[0]]):
             for n_, (_, _, peer, _) in enumerate(same):
                 cp = remote(ref, ref, R.p_s.at[n_, m], R.p_r.at[n_, m], peer)
                 cp.start()
                 sends[n_, m] = cp
+        over_z(span(me, rows), f * 2 + y)
         relays = {}
 
         def relay(n_, m, at):
@@ -527,6 +537,9 @@
         for m in range(4):
             relay(0, m, me)
         pass_on((0, 1))
+        pass_on((3,))
+        for _, _, _, at in same:
+            over_z(span(at, rows), lax.div(at, 2))
         for n_ in range(len(same) + 1):
             for m in (0, 1):
                 relays[n_, m].wait_recv()
@@ -542,11 +555,13 @@
     far.start()
     sib.start()
     if gather:
-        pass_on((2, 3))
+        pass_on((2,))
         for n_ in range(len(same) + 1):
             for m in (2, 3):
                 relays[n_, m].wait_recv()
         waits += list(sends.values()) + list(relays.values())
+    else:
+        over_z(span(c, d // 2), 0)
     route = Route(R.chosen[...], zs, z, d)
     R.qt[...] = jnp.transpose(route.sort(nn(normed, R.w3[0]).astype(BF)).astype(F32)).astype(BF)
     teacher, cotangent = route.own(R.tea[...]), route.own(R.cot[...])
@@ -567,16 +582,34 @@
     attention.scores(0, 1)
     attention.scores(1, 1)
     last.wait_recv()
-    sums = Scatter(zs, R.branch, R.parts, R.hz_s, R.hz_r)
     n = R.tok.shape[0]
+    m = n // zs
+    peers = z_peers(zs)
+    sums, passed = [], []
     for half_ in range(2):
         attention.scores(half_, 3)
-        rows_ = pl.ds(half_ * (n // 2), n // 2)
-        ctx = attention.context(half_)
-        R.ctx[rows_, :] = ctx
-        R.branch[rows_, :] = nt(ctx, R.wo[...]).astype(BF)
-        sums.start(half_ * (zs // 2), (half_ + 1) * (zs // 2))
-    residual = own_tokens + sums.finish()
+        R.ctx[pl.ds(half_ * (n // 2), n // 2), :] = attention.context(half_)
+        for k_, step in list(enumerate(owners(zs)))[half_ * (zs // 2) : (half_ + 1) * (zs // 2)]:
+            if step:
+                cp = remote(
+                    R.ctx.at[pl.ds(k_ * m, m)], R.ctx_in.at[step - 1],
+                    R.hz_s.at[step - 1], R.hz_r.at[step - 1], peers[step - 1],
+                )
+                cp.start()
+                sums.append(cp)
+        if half_ == 1:
+            for cp in others:
+                cp.wait_recv()
+            for s in range(zs - 1):
+                ref = R.wo_all.at[lax.rem(z - s - 1 + zs, zs), :, c]
+                cp = remote(ref, ref, R.wy_s.at[s], R.wy_r.at[s], sibling)
+                cp.start()
+                passed.append(cp)
+    residual = own_tokens + nt(R.ctx[pl.ds((zs - 1) * m, m), :], R.wo[...])
+    for cp in sums + passed:
+        cp.wait_recv()
+    for step in range(1, zs):
+        residual = residual + nt(R.ctx_in[step - 1], R.wo_all[lax.rem(z - step + zs, zs)].reshape(R.wo.shape))
     R.res[...] = residual
     xhat, _ = norm_parts(residual)
     mixed_in = (xhat * R.table[EXP + 1 : EXP + 2, :].astype(F32)).astype(BF)
@@ -590,7 +623,7 @@
     slope = jnp.broadcast_to(gate * gate * weight, (known.shape[0], 128))
     route.fill(jnp.concatenate([known, slope], axis=1).astype(BF), R.slots_g)
     sends_g = dispatch(fs, R.slots_g, R.rg, R.g_s, R.g_r, R.wsem.at[3])
-    waits += swaps + [v[1] for v in sums.copies] + [far, sib, last]
+    waits += swaps + sums + others + passed + [far, sib, last]
     return SimpleNamespace(route=route, attention=attention, own_tokens=own_tokens, sends=sends, sends_g=sends_g, gate=gate, teacher=teacher, cotangent=cotangent, valid=own_valid, scale=scale,
                            loads=loads, swaps=swaps, waits=waits)
 
@@ -779,6 +812,16 @@
     xhat, inv = norm_parts(R.res[...])
     grad = R.gm[...] + norm_back(grad_in, xhat, inv, R.table[EXP + 1 : EXP + 2, :].astype(F32))
     R.sorted_gb[pl.ds((zs - 1) * m, m), :] = grad.astype(BF)
+    gb = grad.astype(BF)
+    order = owners(zs)
+    pieces = []
+    for s, peer in enumerate(z_peers(zs)):
+        R.gct_out[s] = nn(gb, R.wo_all[lax.rem(z + s + 1, zs)].reshape(R.wo.shape)).astype(BF)
+        to = R.gct.at[pl.ds(order.index(zs - s - 1) * m, m)]
+        cp = remote(R.gct_out.at[s], to, R.gc_s.at[s], R.gc_r.at[s], peer)
+        cp.start()
+        pieces.append(cp)
+    R.gct[pl.ds((zs - 1) * m, m), :] = nn(gb, R.wo[...]).astype(BF)
     gathers = gather_z(zs, R.sorted_gb, m, R.ba_s, R.ba_r)
     g2 = jnp.sum(grad_in * xhat, axis=0, keepdims=True)
     cg = _dot(route.own_hot.astype(F32) * gl, R.mi[...].astype(F32), 0, 0, TOP)
@@ -813,14 +856,13 @@
     dqs = {}
     for half, steps in ((1, (0,)), (0, range(1, zs - 1))):
         for s in steps:
-            gathers[s].wait_recv()
-        gct = jnp.transpose(nn(R.sorted_gb[pl.ds(half * (n // 2), n // 2), :], R.wo[...])).astype(BF)
+            pieces[s].wait_recv()
+        gct = jnp.transpose(R.gct[pl.ds(half * (n // 2), n // 2), :])
         dqs[half] = S.attention.back(half, gct, half == 1, nothing if half == 1 else made)
     dq = jnp.transpose(jnp.concatenate([dqs[0], dqs[1]], axis=1)).astype(BF)
     normed = R.normed[...]
     gq = nt(dq, R.w3[0])
     mg = [tn(normed, route.unsort(dq)), None, None]
-    og = tn(R.sorted_gb[...], R.ctx[...])
     swaps[0].wait_recv()
     near = R.near[0] + R.away_in[0]
     cross.wait_recv()
@@ -833,6 +875,9 @@
     mg[1] = tn(normed, kvg[:, :k])
     mg[2] = tn(normed, kvg[:, k:])
     g1 = jnp.sum(partial_normed * all_tok, axis=0, keepdims=True)
+    for cp in gathers:
+        cp.wait_recv()
+    og = tn(R.sorted_gb[...], R.ctx[...])
     dense = R.dense
     last = dense.shape[3] - TAB
     small = jnp.concatenate([cg, g1, g2, jnp.zeros((TAB - EXP - 2, d), F32)], axis=0)
@@ -880,7 +925,7 @@
         cp.wait_recv()
         total = total + R.sm_in[s]
     R.sm_out[...] = total
-    for cp in S.waits + gathers + swaps + [cross, pair] + [v[1] for v in scat.copies] + shares + ends + smalls:
+    for cp in S.waits + pieces + gathers + swaps + [cross, pair] + [v[1] for v in scat.copies] + shares + ends + smalls:
         cp.wait_send()
 
     @pl.loop(0, R.wu.shape[0])
@@ -924,6 +969,7 @@
     scratch = []
     weights = [("w3", (3, d, k), BF), ("wo", (d, k), BF), ("table", (TAB, d), BF), ("valid", (sources, n), F32)]
     gather = rows % 16 == 0
+    pairs = 2 * fs if gather else 1
     if gather:
         ins += [("mix", mixing, vspec()), ("ow", output_weight, vspec()), ("cent", centroids, vspec()),
                 ("gain1", first_gain.reshape(1, rows), vspec()), ("gain2", second_gain.reshape(1, rows), vspec()),
@@ -958,7 +1004,8 @@
     slots = (fs, 2, 2, r)
     scratch += [
         ("normed", (n, d), BF), ("qt", (k, n), BF), ("kv", (4, n, 2 * k), BF), ("pt", (heads, 4, n, n), BF),
-        ("scores", (heads, 4, n, n), F32), ("ctx", (n, k), BF), ("branch", (n, d), BF), ("parts", (zs - 1, m, d), BF),
+        ("scores", (heads, 4, n, n), F32), ("ctx", (n, k), BF), ("ctx_in", (zs - 1, m, k), BF), ("wo_all", (zs, pairs, 2, d // (2 * pairs), k), BF),
+        ("gct", (n, k), BF), ("gct_out", (zs - 1, m, k), BF),
         ("res", (m, d), F32), ("mi", (m, d), BF), ("slots", slots + (dh,), BF), ("slots_g", slots + (dh + 128,), BF),
         ("wu", (half, dh, units), BF), ("wd", (half, dh, units), BF), ("gp", hidden, BF),
         ("act", hidden, BF), ("gh", hidden, BF), ("x", received, BF), ("gx", received, BF),
@@ -980,7 +1027,7 @@
     for name, shape in (("hz", (zs - 1,)), ("wx", (2,)), ("kv", (3,)), ("d", (sources - 1,)), ("g", (sources - 1,)),
                         ("b", (sources - 1,)), ("c", (sources - 1,)), ("u", (sources - 1,)), ("o", (zs - 1,)),
                         ("t", (zs - 1,)), ("e", (4,)), ("ba", (zs - 1,)), ("bs", (zs - 1,)), ("bt", (zs - 1,)),
-                        ("v", (zs - 1,)), ("k", (4,)), ("bg", (others,)),
+                        ("v", (zs - 1,)), ("k", (4,)), ("wz", (zs - 1, pairs)), ("wy", (zs - 1,)), ("gc", (zs - 1,)), ("bg", (others,)),
                         ("one_a", (half, zs - 1)), ("one_x", (half,)), ("one_r", (half, zs - 1)),
                         ("two_a", (half, zs - 1)), ("two_x", (half,)), ("two_r", (half, zs - 1))):
         scratch += [(name + "_s", shape, dma), (name + "_r", shape, dma)]

time: 192 us -> 188 us (0.979)
  Pallas kernels: 190 us -> 186 us
    pallas_call x1, Pallas kernels: 179 us -> 174 us  [per_device(): pl.pallas_call(partial(layer_body, names, fs, zs, gather, rows), out_shap...]
where the time goes in v7:
time: 188 us; the launch traced here: 187 us
  Pallas kernels  186 us (99%)
    pallas_call x1, Pallas kernels, per_device(): pl.pallas_call(partial(layer_body, names, fs, zs, gather, rows), out_shap...  174 us
    pallas_call x1, Pallas kernels, finish(): pl.pallas_call(partial(finish_body, float(tokens)), grid_spec=pltpu.Prefe...  11.6 us

profile of v7, /device:TPU:0, one launch (start us, length us, event | category | flops | bytes accessed | tf_op | source)
XLA Modules:
  0.0 187.4 jit_solution(16590441425578512133)
XLA Ops:
  1.3 174.3 %layer.1 = (bf16[8,192,128]{2,1,0:T(8,128)(2,1)}, bf16[8,192,128]{2,1,0:T(8,128)(2,1)}, bf16[8,128,768]{2,1,0:T(8,128)(2,1)}, bf16[8,128,768]{2,1,0:T(8,128)(2,1...) custom-call(s32[1]{0:T(128)S(6)} %copy.24.refs_0_, ...), custom_call_target="tpu_custom_call" | custom-call | tf_op jit(solution)/shard_map/layer/pallas_call | solution.py:1036
  175.6 11.6 %finish.1 = (f32[2,8,192,768]{3,2,1,0:T(8,128)}, f32[2,8,192,768]{3,2,1,0:T(8,128)}, bf16[256,768]{1,0:T(8,128)(2,1)}, bf16[256,768]{1,0:T(8,128)(2,1)}, f32[3,9...) custom-call(s32[1]{0:T(128)} %bitcast.c_ref, ...), custom_call_target="tpu_custom_call" | custom-call | tf_op jit(solution)/shard_map/finish/pallas_call | solution.py:345

commit v8 on v7

--- a/solution.py
+++ b/solution.py
@@ -19,6 +19,7 @@
 ANY = pl.ANY
 CAP = 16
 EXP = 32
+STEP = 4
 TAB = 48
 
 
@@ -309,53 +310,67 @@
         return jnp.concatenate(dqs, axis=0) * scale
 
 
-def finish_body(scalars, c_ref, *refs):
+def finish_body(tokens, step, *refs):
+    ins = refs[:8]
     tg_in, act_in, mix_in, og_in, sm_in, stat_in = refs[8:14]
-    up_ref, down_ref, tg_ref, act_ref, mix_ref, og_ref, cen_ref, g1_ref, g2_ref, bal_ref, dis_ref = refs[14:]
-    c = c_ref[0]
-    for out_ref, at in ((up_ref, 0), (down_ref, 4)):
-        for core, (left_ref, right_ref) in ((c, refs[at : at + 2]), (1 - c, refs[at + 2 : at + 4])):
-            for e in range(left_ref.shape[0]):
-                out_ref[core, e] = nn(left_ref[e], right_ref[e])
-
-    @pl.when(pl.program_id(0) == 0)
-    def _():
-        tg_ref[...] = tg_in[...]
-        act_ref[...] = act_in[...]
-        mix_ref[...] = mix_in[...]
-        og_ref[...] = og_in[...]
-        rows = cen_ref.shape[1]
-        cen_ref[...] = sm_in[0:EXP, :rows]
-        g1_ref[...] = sm_in[EXP : EXP + 1, :rows]
-        g2_ref[...] = sm_in[EXP + 1 : EXP + 2, :rows]
-        share = stat_in[0:1, :EXP] / scalars - 1.0 / EXP
-        bal_ref[0, 0] = EXP * EXP * jnp.sum(share * stat_in[1:2, :EXP] / scalars)
-        dis_ref[0, 0] = jnp.sum(stat_in[2:3, 0:1])
-
-
-def finish(c, tokens, pairs, small, shapes):
+    up_out, down_out, tg_ref, act_ref, mix_ref, og_ref, cen_ref, g1_ref, g2_ref, bal_ref, dis_ref = refs[14:25]
+    held, (up, down, in_sem, out_sem) = refs[25:33], refs[33:]
+    c = lax.rem(lax.axis_index("ctx"), 2)
+    half = up.shape[1]
+    loads = {}
+    for n in range(half // step):
+        at = pl.ds(n * step, step)
+        for k in range(8):
+            cp = pltpu.make_async_copy(ins[k].at[at], held[k].at[at], in_sem.at[k, n])
+            cp.start()
+            loads[k, n] = cp
+    tg_ref[...] = tg_in[...]
+    act_ref[...] = act_in[...]
+    mix_ref[...] = mix_in[...]
+    og_ref[...] = og_in[...]
+    rows = cen_ref.shape[1]
+    cen_ref[...] = sm_in[0:EXP, :rows]
+    g1_ref[...] = sm_in[EXP : EXP + 1, :rows]
+    g2_ref[...] = sm_in[EXP + 1 : EXP + 2, :rows]
+    share = stat_in[0:1, :EXP] / tokens - 1.0 / EXP
+    bal_ref[0, 0] = EXP * EXP * jnp.sum(share * stat_in[1:2, :EXP] / tokens)
+    dis_ref[0, 0] = jnp.sum(stat_in[2:3, 0:1])
+    stores = []
+    for n in range(half // step):
+        for m, (made, out) in enumerate(((up, up_out), (down, down_out))):
+            for k, core in enumerate((c, 1 - c)):
+                left, right = 4 * m + 2 * k, 4 * m + 2 * k + 1
+                loads[left, n].wait()
+                loads[right, n].wait()
+                for e in range(n * step, (n + 1) * step):
+                    made[k, e] = nn(held[left][e], held[right][e])
+                at = pl.ds(n * step, step)
+                cp = pltpu.make_async_copy(made.at[k, at], out.at[core, at], out_sem.at[m, k, n])
+                cp.start()
+                stores.append(cp)
+    for cp in stores:
+        cp.wait()
+
+
+def finish(tokens, pairs, small, shapes):
     half, q, n = pairs[0].shape
     units = pairs[1].shape[2]
-    step = 2 if half % 2 == 0 else 1
-    block = lambda e, c_ref: (e, 0, 0)
+    step = STEP if half % STEP == 0 else 1
     out = sds((2, half, q, units), F32)
-    whole = lambda v: pl.BlockSpec(v.shape, lambda e, c_ref: (0,) * len(v.shape))
     smem = pl.BlockSpec(memory_space=pltpu.SMEM)
-    scalar = sds((1, 1), F32)
+    anyspec = pl.BlockSpec(memory_space=ANY)
+    dma = pltpu.SemaphoreType.DMA
     return pl.pallas_call(
-        partial(finish_body, float(tokens)),
-        grid_spec=pltpu.PrefetchScalarGridSpec(
-            num_scalar_prefetch=1,
-            grid=(half // step,),
-            in_specs=[pl.BlockSpec((step, q, n), block), pl.BlockSpec((step, n, units), block)] * 4
-            + [whole(v) for v in small],
-            out_specs=[pl.BlockSpec((2, step, q, units), lambda e, c_ref: (0, e, 0, 0))] * 2
-            + [whole(v) for v in shapes] + [smem] * 2,
-        ),
-        out_shape=[out, out] + shapes + [scalar] * 2,
+        partial(finish_body, float(tokens), step),
+        in_specs=[anyspec] * 8 + [vspec()] * len(small),
+        out_specs=[anyspec] * 2 + [vspec()] * len(shapes) + [smem] * 2,
+        out_shape=[out, out] + shapes + [sds((1, 1), F32)] * 2,
+        scratch_shapes=[VMEM(v.shape, BF) for v in pairs]
+        + [VMEM(out.shape, F32)] * 2
+        + [dma((8, half // step)), dma((2, 2, half // step))],
         compiler_params=params(),
         name="finish",
-    )(c.reshape(1), *pairs, *small)
+    )(*pairs, *small)
 
 
 def whereabouts():
@@ -702,9 +717,9 @@
         scale = R.grads[e, :, dh:].astype(F32)[:, :1]
         two.spread(e, (R.grads[e, :, :dh].astype(F32) + scale * result.astype(F32)).astype(BF))
 
-    lag, lag2 = 2, 4
+    lag, lag2 = 3, 6
     start = max(half, lag2 + 1)
-    ahead = 3
+    ahead = 2
 
     def step(t, fixed=True):
         if not fixed or t < half:
@@ -777,13 +792,13 @@
             begun += 1
         if 0 <= t - 1 - start < half:
             R.xg[t - 1 - start] = two.total(t - 1 - start)
-        if t == max(start + half - 4, start + 1) or (half == 1 and t == start):
+        if t == half - 1 + lag2:
 
             @pl.loop(0, half)
             def _(e):
                 R.gxt[e] = jnp.transpose(R.gx[e])
 
-        if t == start + half - 2 or (half == 1 and t == start):
+        if t == start + half - 2:
             arrived(given)
             report()
         if t == start + half - 1:
@@ -943,7 +958,6 @@
 def per_device(tokens, mixing_weight, output_weight, first_gain, second_gain, centroids, expert_up,
                expert_down, prefix_length, assignment, validity, teacher, cotangent):
     fs, zs = lax.axis_size("fsdp"), lax.axis_size("tp")
-    c = lax.rem(lax.axis_index("ctx"), 2)
     n, d = tokens.shape[1], tokens.shape[2]
     rows, k = mixing_weight.shape[0], mixing_weight.shape[2]
     local_experts, width, units = expert_up.shape
@@ -1046,7 +1060,7 @@
     shapes = [sds((n, d), BF), sds((n, d), BF), sds((3, rows, k), F32), sds((k, rows), F32),
               sds((experts, rows), F32), sds((1, rows), F32), sds((1, rows), F32)]
     up, down, tokens_gradient, activations, mix_part, out_part, cen_part, g1, g2, balance, distill = finish(
-        c, n * sources, (xt, gh, xt_x, gh_x, gxt, act, gxt_x, act_x), results[8:], shapes
+        n * sources, (xt, gh, xt_x, gh_x, gxt, act, gxt_x, act_x), results[8:], shapes
     )
     return (
         activations[None],

time: 188 us -> 184 us (0.979)
  Pallas kernels: 186 us -> 182 us
    pallas_call x1, Pallas kernels: 174 us -> 172 us  [per_device(): pl.pallas_call(partial(layer_body, names, fs, zs, gather, rows), out_shap...]
where the time goes in v8:
time: 184 us
  Pallas kernels  182 us (99%)
    pallas_call x1, Pallas kernels, per_device(): pl.pallas_call(partial(layer_body, names, fs, zs, gather, rows), out_shap...  172 us
    pallas_call x1, Pallas kernels, finish(): pl.pallas_call(partial(finish_body, float(tokens), step), in_specs=[anysp...  10.9 us

profile of v8, /device:TPU:0, one launch (start us, length us, event | category | flops | bytes accessed | tf_op | source)
XLA Modules:
  0.0 183.9 jit_solution(4463952853132944634)
XLA Ops:
  1.3 171.6 %layer.1 = (bf16[8,192,128]{2,1,0:T(8,128)(2,1)}, bf16[8,192,128]{2,1,0:T(8,128)(2,1)}, bf16[8,128,768]{2,1,0:T(8,128)(2,1)}, bf16[8,128,768]{2,1,0:T(8,128)(2,1...) custom-call(s32[1]{0:T(128)S(6)} %copy.24.refs_0_, ...), custom_call_target="tpu_custom_call" | custom-call | tf_op jit(solution)/shard_map/layer/pallas_call | solution.py:1050
  172.9 10.9 %finish.1 = (f32[2,8,192,768]{3,2,1,0:T(8,128)}, f32[2,8,192,768]{3,2,1,0:T(8,128)}, bf16[256,768]{1,0:T(8,128)(2,1)}, bf16[256,768]{1,0:T(8,128)(2,1)}, f32[3,9...) custom-call(bf16[8,192,128]{2,1,0:T(8,128)(2,1)} %get-tuple-element., ...), custom_call_target="tpu_custom_call" | custom-call | tf_op jit(solution)/shard_map/finish/pallas_call | solution.py:363
